TPU v7x, 512 devices: a whole 4x8x8 slice. The times are simulated.
512 devices in a mesh: tm: 32 (over z, x), row: 4 (over y_lo, core), col: 4 (over y_hi).
Axes of the slice: x: 4, y: 8 (y_hi: 4, y_lo: 2; y = y_hi * 2 + y_lo), z: 8, core: 2. Of those that a mesh axis runs over, the one named last changes fastest.
Arguments:
- query_tokens: bfloat16 [64, 32, 64, 1152], P('tm', 'row', 'col'), may hold values from -0.119628906 to 0.119628906
- key_tokens: bfloat16 [64, 32, 64, 1152], P('tm', 'row', 'col'), may hold values from -6 to 6
- value_tokens: bfloat16 [64, 32, 64, 1152], P('tm', 'row', 'col'), may hold values from -6 to 6
- grad_output: bfloat16 [64, 32, 64, 1152], P('tm', 'row', 'col'), may hold values from -6 to 6
- frame_decay: float32 [64, 36], P('tm'), may hold values from 0 to 1
- conv_weight: float32 [9, 1152], replicated, may hold values from -1.5 to 1.5
Outputs:
- query_grad: bfloat16 [64, 32, 64, 1152], P('tm', 'row', 'col')
- lookup_vector_gradient: bfloat16 [64, 32, 64, 1152], P('tm', 'row', 'col')
- value_grad: bfloat16 [64, 32, 64, 1152], P('tm', 'row', 'col')
All inputs are finite; a program needn't handle non-finite values.
Results may differ from a plain program's by a relative error of at most 0.015.
Values may be sent and summed in bfloat16 or wider, within the bound.
No kernel may reach another device: no remote copies, remote signals or barrier semaphores. Data moves between devices by JAX's collectives and lax.ppermute only.
A program may use at most 64 MiB of HBM per device.

v0:
```python
import jax
import jax.numpy as jnp
from jax import lax
from jax.sharding import PartitionSpec as P

MIXING_CHANNELS = 36
HEAD_DIM = 32


def padded_2(cells, sides, width):
    for axis, dim in sides:
        count = lax.axis_size(axis)
        ends = count - 1
        head = lax.slice_in_dim(cells, 0, width, axis=dim)
        tail = lax.slice_in_dim(cells, cells.shape[dim] - width, cells.shape[dim], axis=dim)
        cells = jnp.concatenate(
            [
                lax.ppermute(tail, axis, [(i, (i + 1) % count) for i in range(ends)]),
                cells,
                lax.ppermute(head, axis, [((i + 1) % count, i) for i in range(ends)]),
            ],
            axis=dim,
        )
    return cells


def entering(value, axis, join, neutral, backward):
    count, mine = (lax.axis_size(axis), lax.axis_index(axis))
    pieces = jax.tree.map(lambda part: lax.all_gather(part, axis), value)
    if backward:
        pieces = jax.tree.map(lambda part: part[::-1], pieces)
        mine = count - 1 - mine
    subtotal = jax.tree.map(
        lambda part, zero: jnp.full_like(part, 0) + jnp.asarray(zero, part.dtype), value, neutral
    )

    def lap(position, subtotal):
        longer = join(subtotal, jax.tree.map(lambda part: part[position], pieces))
        return jax.tree.map(lambda new, old: jnp.where(position < mine, new, old), longer, subtotal)

    return lax.fori_loop(0, count - 1, lap, subtotal)


def combine_blocks(earlier, later):
    decay_e, state_e, normal_e = earlier
    decay_l, state_l, normal_l = later
    state = decay_l[:, None] * state_e + state_l
    normal = jnp.repeat(decay_l, HEAD_DIM) * normal_e + normal_l
    return (decay_e * decay_l, state, normal)


def per_device(query_tokens, key_tokens, value_tokens, grad_output, frame_decay, conv_weight):
    fr_count, row_count, col_count, width = query_tokens.shape
    count = row_count * col_count
    block_decay = jnp.prod(frame_decay, axis=0)
    zero_state = jnp.zeros((MIXING_CHANNELS, HEAD_DIM * HEAD_DIM), jnp.float32)
    zero_normal = jnp.zeros((MIXING_CHANNELS * HEAD_DIM,), jnp.float32)
    identity = (jnp.ones((MIXING_CHANNELS,), jnp.float32), zero_state, zero_normal)
    padded = padded_2(grad_output, (("row", 1), ("col", 2)), 1)
    grad_attn = grad_output.astype(jnp.float32)
    for row_off in (-1, 0, 1):
        for col_off in (-1, 0, 1):
            tap_index = (row_off + 1) * 3 + col_off + 1
            window = padded[
                :, 1 - row_off : 1 - row_off + row_count, 1 - col_off : 1 - col_off + col_count
            ]
            grad_attn = grad_attn + conv_weight[tap_index] * window.astype(jnp.float32)
    grad_attn = grad_attn.reshape(fr_count, count, MIXING_CHANNELS, HEAD_DIM)
    keys_all = key_tokens.reshape(fr_count, count, MIXING_CHANNELS, HEAD_DIM)
    values_all = value_tokens.reshape(fr_count, count, MIXING_CHANNELS, HEAD_DIM)
    queries = query_tokens.reshape(fr_count, count, MIXING_CHANNELS, HEAD_DIM)
    pos_keys = jnp.maximum(keys_all, 0)
    pos_q = jnp.maximum(queries, 0)
    state_updates = jnp.einsum(
        "fphd,fphe->fhde", pos_keys, values_all, preferred_element_type=jnp.float32
    )
    state_updates = state_updates.reshape(fr_count, MIXING_CHANNELS, HEAD_DIM * HEAD_DIM)
    normalizer_summands = jnp.sum(pos_keys.astype(jnp.float32), axis=1).reshape(
        fr_count, MIXING_CHANNELS * HEAD_DIM
    )
    state_updates, normalizer_summands = lax.psum(
        (state_updates, normalizer_summands), ("row", "col")
    )
    state = zero_state
    normal = zero_normal
    for forward_frame in range(fr_count):
        state = frame_decay[forward_frame][:, None] * state + state_updates[forward_frame]
        normal = (
            jnp.repeat(frame_decay[forward_frame], HEAD_DIM) * normal
            + normalizer_summands[forward_frame]
        )
    block_state = state
    block_normal = normal
    _, prev_state, prev_normal = entering(
        (block_decay, block_state, block_normal), "tm", combine_blocks, identity, False
    )
    prev_state, prev_normal = (prev_state, prev_normal)
    state_list = []
    normal_list = []
    state, normal = (prev_state, prev_normal)
    for frame in range(fr_count):
        state = frame_decay[frame][:, None] * state + state_updates[frame]
        normal = jnp.repeat(frame_decay[frame], HEAD_DIM) * normal + normalizer_summands[frame]
        state_list.append(state.reshape(MIXING_CHANNELS, HEAD_DIM, HEAD_DIM))
        normal_list.append(normal.reshape(MIXING_CHANNELS, HEAD_DIM))
    states = jnp.stack(state_list)
    normals = jnp.stack(normal_list)
    pos_qf = pos_q.astype(jnp.float32)
    numer = jnp.einsum("fphd,fhde->fphe", pos_qf, states)
    denom = jnp.einsum("fphd,fhd->fph", pos_qf, normals) + 1.0
    attn = numer / denom[..., None]
    grad_num = grad_attn / denom[..., None]
    grad_den = -jnp.sum(grad_attn * attn, axis=-1) / denom
    grad_posq = (
        jnp.einsum("fphe,fhde->fphd", grad_num, states) + grad_den[..., None] * normals[:, None]
    )
    query_grad = jnp.where(queries > 0, grad_posq, 0.0).astype(jnp.bfloat16)
    locals_all = jnp.einsum("fphd,fphe->fhde", pos_qf, grad_num).reshape(
        fr_count, MIXING_CHANNELS, HEAD_DIM * HEAD_DIM
    )
    localz_all = jnp.einsum("fph,fphd->fhd", grad_den, pos_qf).reshape(
        fr_count, MIXING_CHANNELS * HEAD_DIM
    )
    locals_all, localz_all = lax.psum((locals_all, localz_all), ("row", "col"))
    state = zero_state
    normal = zero_normal
    for reverse_frame in reversed(range(fr_count)):
        state = frame_decay[reverse_frame][:, None] * (locals_all[reverse_frame] + state)
        normal = jnp.repeat(frame_decay[reverse_frame], HEAD_DIM) * (
            localz_all[reverse_frame] + normal
        )
    _, next_state, next_normal = entering(
        (block_decay, state, normal), "tm", combine_blocks, identity, True
    )
    next_state, next_normal = (next_state, next_normal)
    carried_list = [None] * fr_count
    carriedz_list = [None] * fr_count
    carry_state, carry_normal = (next_state, next_normal)
    for frame in reversed(range(fr_count)):
        total = locals_all[frame] + carry_state
        totalz = localz_all[frame] + carry_normal
        carried_list[frame] = total.reshape(MIXING_CHANNELS, HEAD_DIM, HEAD_DIM)
        carriedz_list[frame] = totalz.reshape(MIXING_CHANNELS, HEAD_DIM)
        carry_state = frame_decay[frame][:, None] * total
        carry_normal = jnp.repeat(frame_decay[frame], HEAD_DIM) * totalz
    carried = jnp.stack(carried_list)
    carriedz = jnp.stack(carriedz_list)
    grad_posk = (
        jnp.einsum("fphe,fhde->fphd", values_all.astype(jnp.float32), carried) + carriedz[:, None]
    )
    lookup_vector_gradient = jnp.where(keys_all > 0, grad_posk, 0.0).astype(jnp.bfloat16)
    value_grad = jnp.einsum("fphd,fhde->fphe", pos_keys.astype(jnp.float32), carried).astype(
        jnp.bfloat16
    )
    shape = (fr_count, row_count, col_count, width)
    return (
        query_grad.reshape(shape),
        lookup_vector_gradient.reshape(shape),
        value_grad.reshape(shape),
    )


def solution(mesh):
    return jax.shard_map(
        per_device,
        mesh=mesh,
        in_specs=(
            P("tm", "row", "col", None),
            P("tm", "row", "col", None),
            P("tm", "row", "col", None),
            P("tm", "row", "col", None),
            P("tm", None),
            P(),
        ),
        out_specs=(
            P("tm", "row", "col", None),
            P("tm", "row", "col", None),
            P("tm", "row", "col", None),
        ),
        check_vma=False,
    )
```

profile of v0, /device:TPU:1, one launch (start us, length us, event | category | flops | bytes accessed | tf_op | source)
XLA Modules:
  0.0 722.6 jit_solution(12127165388218187701)
XLA Ops:
  10.5 4.5 reshape.124
  15.0 3.5 fusion.6
  21.3 116.3 %all-reduce.4.cloned.1.call-done = f32[2,36,1024]{2,0,1:T(2,128)} async-done(((f32[2,36,1024]{2,0,1:T(2,128)}), f32[2,36,1024]{2,0,1:T(2,128)}) %all-reduce.4.cloned.1.call-update) | async-done | bytes 294928 | tf_op jit(solution)/shard_map/psum | solution.py:81
  148.0 31.2 %psum.29 = f32[2,1152]{1,0:T(2,128)S(1)} all-reduce(f32[2,1152]{1,0:T(2,128)S(1)} %convert_reduce_fusion), channel_id=1, replica_groups=mesh['tm'=32,'row'=4,'col'=4] {'row','col'}, use_global_device_ids=true, to_apply=%region_3.0 | all-reduce | flops 2304 | bytes 18432 | tf_op jit(solution)/shard_map/psum | solution.py:81
  185.1 5.5 collective-permute-start.3
  197.2 63.4 %all-reduce = f32[1152]{0:T(1024)S(1)} all-reduce(f32[1152]{0:T(1024)} %dynamic-update-slice), channel_id=2, replica_groups=mesh['tm'=32,'row'=4,'col'=4] {'tm'}, use_global_device_ids=true, to_apply=%add | all-reduce | flops 1152 | bytes 9216
  261.4 31.9 %all-gather.1 = f32[32,1,1152]{2,1,0:T(1,128)S(1)} all-gather(f32[1,1,1152]{2,1,0:T(1,128)} %get-tuple-element.364), channel_id=1, replica_groups=mesh['tm'=32,'row'=4,'col'=4] {'tm'}, dimensions={0}, use_global_device_ids=true | all-gather | bytes 152064 | tf_op jit(solution)/shard_map/all_gather | solution.py:29
  294.0 4.5 max.16
  298.4 4.6 copy.50
  303.0 5.9 fusion.44
  308.9 4.8 reshape.128
  313.7 5.2 copy.48
  318.8 62.3 %while.32 = (s32[]{:T(128)}, f32[36,1024]{1,0:T(8,128)S(1)}, f32[1152]{0:T(1024)S(1)}, s32[]{:T(128)}, f32[32,36]{1,0:T(8,128)S(1)}, /*index=5*/f32[32,36,1024]{...) while((s32[]{:T(128)}, f32[36,1024]{1,0:T(8,128)S(1)}, f32[1152]{0:T(1024)S(1)}, s32[]{:T(128)}, ...), condition=%wide.region_5.6_spmd.clone, body=%wide.region_4.5_spmd.clone.sunk | while | flops 152068 | bytes 484551 | solution.py:41
  383.9 3.9 fusion.4
  392.5 135.8 %all-reduce.6.cloned.1.call-done = f32[2,36,1024]{2,1,0:T(8,128)} async-done(((f32[2,36,1024]{2,1,0:T(8,128)}), f32[2,36,1024]{2,1,0:T(8,128)}) %all-reduce.6.cloned.1.call-update) | async-done | bytes 294928 | tf_op jit(solution)/shard_map/psum | solution.py:124
  531.5 4.2 gt.15
  535.7 3.4 copy.58
  542.7 3.4 copy.52
  549.5 31.8 %psum.31 = f32[2,1152]{1,0:T(2,128)S(1)} all-reduce(f32[2,1152]{1,0:T(2,128)S(1)} %reshape.133), channel_id=1, replica_groups=mesh['tm'=32,'row'=4,'col'=4] {'row','col'}, use_global_device_ids=true, to_apply=%region_8.9 | all-reduce | flops 2304 | bytes 18432 | tf_op jit(solution)/shard_map/psum | solution.py:124
  582.0 41.7 %all-gather.2 = f32[32,1,1152]{2,1,0:T(1,128)S(1)} all-gather(f32[1,1,1152]{2,1,0:T(1,128)S(1)} %get-tuple-element.363), channel_id=1, replica_groups=mesh['tm'=32,'row'=4,'col'=4] {'tm'}, dimensions={0}, use_global_device_ids=true | all-gather | bytes 152064 | tf_op jit(solution)/shard_map/all_gather | solution.py:29
  625.8 3.4 copy.53
  629.2 4.2 reshape.131
  633.4 5.7 rev.10
  639.1 59.2 %while.33 = (s32[]{:T(128)}, f32[36,1024]{1,0:T(8,128)S(1)}, f32[1152]{0:T(1024)S(1)}, s32[]{:T(128)}, f32[32,36]{1,0:T(8,128)}, /*index=5*/f32[32,36,1024]{2,1,...) while((s32[]{:T(128)}, f32[36,1024]{1,0:T(8,128)S(1)}, f32[1152]{0:T(1024)S(1)}, s32[]{:T(128)}, ...), condition=%wide.region_10.11_spmd.clone, body=%wide.region_9.10_spmd.clone.sunk | while | flops 152068 | bytes 484551 | solution.py:41
  (538 shorter events, 186.9 us)
Async XLA Ops:
  7.2 130.4 %all-reduce.4.cloned.1.call-start = ((), (), s32[]{:S(2)}) async-start(), calls=%async_computation | async-start | bytes 589824 | tf_op jit(solution)/shard_map/psum | solution.py:81
  21.1 126.7 %copy-start = (bf16[2,8,16,1152]{3,2,1,0:T(8,128)(2,1)S(1)}, bf16[2,8,16,1152]{3,2,1,0:T(8,128)(2,1)}, u32[]{:S(2)}) copy-start(bf16[2,8,16,1152]{3,2,1,0:T(8,128)(2,1)} %param.11) | copy-start | bytes 1769476
  21.2 297.6 %all-gather.6.cloned.1.call-start = ((), (), s32[]{:S(2)}) async-start(), calls=%async_computation.1 | async-start | bytes 5406720 | tf_op jit(solution)/shard_map/all_gather | solution.py:29
  21.2 126.3 %copy-start.33 = (f32[36]{0:T(128)}, f32[36]{0:T(128)S(1)}, u32[]{:S(2)}) copy-start(f32[36]{0:T(128)S(1)} %get-tuple-element.365) | copy-start | bytes 436
  21.2 126.5 %copy-start.28 = (f32[36]{0:T(128)}, f32[36]{0:T(128)S(1)}, u32[]{:S(2)}) copy-start(f32[36]{0:T(128)S(1)} %get-tuple-element.366) | copy-start | bytes 436
  140.3 387.9 %all-reduce.6.cloned.1.call-start = ((), (), s32[]{:S(2)}) async-start(), calls=%async_computation.2 | async-start | bytes 655360 | tf_op jit(solution)/shard_map/psum | solution.py:124
  142.0 40.1 %collective-permute-start.1 = (bf16[2,1,16,1152]{3,2,1,0:T(8,128)(2,1)S(1)}, bf16[2,1,16,1152]{3,2,1,0:T(8,128)(2,1)S(1)}, u32[]{:S(2)}, u32[]{:S(2)}) collective-permute-start(bf16[2,1,16,1152]{3,2,1,0:T(8,128)(2,1)S(1)} %get-tuple-element.359), channel_id=1, source_target_pairs={{4,0},{8,4},{12,8},{5,1},{9,5},{13,9},{6,2},{10,6},{14,10},{7,3},{... | collective-permute-start | bytes 221192 | tf_op jit(solution)/shard_map/ppermute | solution.py:20
  144.2 37.8 %collective-permute-start = (bf16[2,1,16,1152]{3,2,1,0:T(8,128)(2,1)}, bf16[2,1,16,1152]{3,2,1,0:T(8,128)(2,1)S(1)}, u32[]{:S(2)}, u32[]{:S(2)}) collective-permute-start(bf16[2,1,16,1152]{3,2,1,0:T(8,128)(2,1)} %get-tuple-element.360), channel_id=1, source_target_pairs={{0,4},{4,8},{8,12},{1,5},{5,9},{9,13},{2,6},{6,10},{10,14},{3,7},{... | collective-permute-start | bytes 221192 | tf_op jit(solution)/shard_map/ppermute | solution.py:18
  147.7 42.9 %copy-start.15 = (f32[1,1152]{1,0:T(1,128)}, f32[1,1152]{1,0:T(1,128)S(1)}, u32[]{:S(2)}) copy-start(f32[1,1152]{1,0:T(1,128)S(1)} %reshape.127) | copy-start | bytes 13828
  147.9 42.7 %copy-start.17 = (f32[1,1152]{1,0:T(1,128)}, f32[1,1152]{1,0:T(1,128)S(1)}, u32[]{:S(2)}) copy-start(f32[1,1152]{1,0:T(1,128)S(1)} %reshape.126) | copy-start | bytes 13828
  183.8 119.2 %collective-permute-start.2 = (bf16[2,10,1,1152]{3,2,1,0:T(2,128)(2,1)}, bf16[2,10,1,1152]{3,2,1,0:T(2,128)(2,1)}, u32[]{:S(2)}, u32[]{:S(2)}) collective-permute-start(bf16[2,10,1,1152]{3,2,1,0:T(2,128)(2,1)} %get-tuple-element.357), channel_id=1, source_target_pairs={{1,0},{2,1},{3,2},{5,4},{6,5},{7,6},{9,8},{10,9},{11,10},{13,12},{... | collective-permute-start | bytes 138248 | tf_op jit(solution)/shard_map/ppermute | solution.py:20
  185.1 117.9 %collective-permute-start.3 = (bf16[2,10,1,1152]{3,2,1,0:T(2,128)(2,1)}, bf16[2,10,1,1152]{3,2,1,0:T(2,128)(2,1)}, u32[]{:S(2)}, u32[]{:S(2)}) collective-permute-start(bf16[2,10,1,1152]{3,2,1,0:T(2,128)(2,1)} %get-tuple-element.358), channel_id=1, source_target_pairs={{0,1},{1,2},{2,3},{4,5},{5,6},{6,7},{8,9},{9,10},{10,11},{12,13},{... | collective-permute-start | bytes 138248 | tf_op jit(solution)/shard_map/ppermute | solution.py:18
  318.8 62.3 %copy-start.23 = (f32[1152]{0:T(1024)S(1)}, f32[1152]{0:T(1024)}, u32[]{:S(2)}) copy-start(f32[1152]{0:T(1024)} %get-tuple-element.319) | copy-start | bytes 13828
  318.8 62.3 %copy-start.24 = (f32[1152]{0:T(1024)S(1)}, f32[1152]{0:T(1024)}, u32[]{:S(2)}) copy-start(f32[1152]{0:T(1024)} %get-tuple-element.320) | copy-start | bytes 13828
  318.8 62.3 %copy-start.25 = (f32[1152]{0:T(1024)S(1)}, f32[1152]{0:T(1024)}, u32[]{:S(2)}) copy-start(f32[1152]{0:T(1024)} %reshape.129) | copy-start | bytes 13828
  387.8 140.4 %copy-start.29 = (f32[36]{0:T(128)S(1)}, f32[36]{0:T(128)}, u32[]{:S(2)}) copy-start(f32[36]{0:T(128)} %copy-done.28) | copy-start | bytes 436
  387.8 140.4 %copy-start.34 = (f32[36]{0:T(128)S(1)}, f32[36]{0:T(128)}, u32[]{:S(2)}) copy-start(f32[36]{0:T(128)} %copy-done.33) | copy-start | bytes 436
  392.2 241.2 %all-gather.8.cloned.1.call-start = ((), (), s32[]{:S(2)}) async-start(), calls=%async_computation.3 | async-start | bytes 5406720 | tf_op jit(solution)/shard_map/all_gather | solution.py:29
  546.8 34.5 %copy-start.16 = (f32[1,1152]{1,0:T(1,128)S(1)}, f32[1,1152]{1,0:T(1,128)}, u32[]{:S(2)}) copy-start(f32[1,1152]{1,0:T(1,128)} %copy-done.15) | copy-start | bytes 13828
  546.8 34.5 %copy-start.18 = (f32[1,1152]{1,0:T(1,128)S(1)}, f32[1,1152]{1,0:T(1,128)}, u32[]{:S(2)}) copy-start(f32[1,1152]{1,0:T(1,128)} %copy-done.17) | copy-start | bytes 13828
  549.0 33.0 %copy-start.21 = (f32[2,128,36]{1,2,0:T(8,128)}, f32[2,128,36]{1,2,0:T(8,128)S(1)}, u32[]{:S(2)}) copy-start(f32[2,128,36]{1,2,0:T(8,128)S(1)} %negate_divide_fusion) | copy-start | bytes 110596
  639.1 59.2 %copy-start.26 = (f32[1152]{0:T(1024)S(1)}, f32[1152]{0:T(1024)}, u32[]{:S(2)}) copy-start(f32[1152]{0:T(1024)} %get-tuple-element.318) | copy-start | bytes 13828
  639.1 59.4 %copy-start.8 = (f32[2,36,1024]{2,1,0:T(8,128)S(1)}, f32[2,36,1024]{2,1,0:T(8,128)}, u32[]{:S(2)}) copy-start(f32[2,36,1024]{2,1,0:T(8,128)} %all-reduce.6.cloned.1.call-done) | copy-start | bytes 884740
  639.1 59.4 %copy-start.31 = (f32[36]{0:T(128)S(1)}, f32[36]{0:T(128)}, u32[]{:S(2)}) copy-start(f32[36]{0:T(128)} %copy-done.28) | copy-start | bytes 436
  (21 other events, 50.8 us)
Sparse Core Ops, SparseCore 0:
  21.3 116.2 all-reduce.3
  141.8 89.6 all-gather.5
  392.3 135.8 all-reduce.5
  531.3 88.6 all-gather.7
where the time goes:
time: 736 us; the launch traced here: 723 us
  waiting for transfers between devices  252 us (34%)
  blocking collectives  200 us (27%)
  local copies, waits for them, and re-layouts  143 us (19%)
  other arithmetic  78.8 us (11%)
  matrix products  18.8 us (3%)
  between operations  15 us (2%)
  starting transfers between devices  12.7 us (2%)
    psum x1, waiting for transfers between devices, per_device(): locals_all, localz_all = lax.psum((locals_all, localz_all), ('row', 'col'))  136 us
    psum x1, waiting for transfers between devices, per_device(): lax.psum((state_updates, normalizer_summands), ('row', 'col'))  116 us
    all_gather x2, blocking collectives, entering(): pieces = jax.tree.map(lambda part: lax.all_gather(part, axis), value)  73.6 us
    unnamed x1, blocking collectives  63.4 us
    select_n x124, other arithmetic, lap(): jnp.where(position < mine, new, old)  63.3 us
    psum x1, blocking collectives, per_device(): locals_all, localz_all = lax.psum((locals_all, localz_all), ('row', 'col'))  31.8 us
    psum x1, blocking collectives, per_device(): lax.psum((state_updates, normalizer_summands), ('row', 'col'))  31.2 us
    dynamic_slice x62, local copies, waits for them, and re-layouts, lap(): longer = join(subtotal, jax.tree.map(lambda part: part[position], pieces))  25.4 us
  transfers between devices with their start and end apart: 8, of which 2 were waited for; matrix products, arithmetic and copies ran while one was open for 9% of the time, Pallas kernels for 0%

commit v1 on v0

v1 whole, which is shorter than its diff:
```python
import jax
import jax.numpy as jnp
from jax import lax
from jax.experimental import pallas as pl
from jax.experimental.pallas import tpu as pltpu
from jax.sharding import PartitionSpec as P

HEADS = 36
DIM = 32
LANES = 128
GROUPS = HEADS * DIM // LANES
PER_GROUP = LANES // DIM
FRAMES = 2
ROWS = 8
COLS = 16
TOKENS = ROWS * COLS
CH = HEADS * DIM
OWNERS = 16
HALF = DIM // 2
NORMAL = 2 * GROUPS
EXTRA = NORMAL + 1
SLOTS = 20
OWNED = FRAMES * SLOTS
SPACE = ("row", "col")
VMEM_BYTES = 24 * 1024 * 1024
F32 = jnp.float32
BF16 = jnp.bfloat16


def call(body, outs, *args, scratch=(), flops=1_000_000, name=None):
    out_shape = tuple(jax.ShapeDtypeStruct(shape, dtype) for shape, dtype in outs)
    moved = sum(a.size * a.dtype.itemsize for a in args) + sum(o.size * o.dtype.itemsize for o in out_shape)
    return pl.pallas_call(
        body,
        out_shape=out_shape,
        in_specs=[pl.BlockSpec(memory_space=pltpu.VMEM)] * len(args),
        out_specs=tuple(pl.BlockSpec(memory_space=pltpu.VMEM) for _ in outs),
        scratch_shapes=list(scratch),
        compiler_params=pltpu.CompilerParams(vmem_limit_bytes=VMEM_BYTES),
        cost_estimate=pl.CostEstimate(flops=flops, bytes_accessed=moved, transcendentals=0),
        name=name,
    )(*args)


def dot(a, b, contract=((1,), (0,)), precision=None):
    return lax.dot_general(a, b, (contract, ((), ())), preferred_element_type=F32, precision=precision)


def iota(shape, dim):
    return lax.broadcasted_iota(jnp.int32, shape, dim)


def lane_head(shape):
    return iota(shape, 1) // DIM


def compact(square):
    head = lane_head((DIM, LANES))
    out = square[(PER_GROUP - 1) * DIM :]
    for i in reversed(range(PER_GROUP - 1)):
        out = jnp.where(head == i, square[i * DIM : (i + 1) * DIM], out)
    return out


def spread(rows):
    head = lane_head((DIM, LANES))
    return jnp.concatenate([jnp.where(head == i, rows, 0.0) for i in range(PER_GROUP)], axis=0).astype(BF16)


def head_ones():
    return (iota((LANES, LANES), 0) // DIM == lane_head((LANES, LANES))).astype(BF16)


def clear_unused(held):
    for owner in range(OWNERS):
        for f in range(FRAMES):
            first = owner * OWNED + f * SLOTS + (EXTRA if owner < GROUPS else NORMAL)
            last = owner * OWNED + (f + 1) * SLOTS
            held[first:last, :] = jnp.zeros((last - first, LANES), F32)


def put_rows(held, f, g, rows, normal):
    for half in range(2):
        held[pl.ds(f * SLOTS + half * GROUPS + g, OWNERS, stride=OWNED), :] = rows[half * HALF : (half + 1) * HALF]
    at = g * OWNED + f * SLOTS + NORMAL
    held[at : at + 1, :] = normal


def take_rows(held, f, g):
    rows = jnp.concatenate(
        [held[pl.ds(f * SLOTS + half * GROUPS + g, OWNERS, stride=OWNED), :] for half in range(2)], axis=0
    )
    at = g * OWNED + f * SLOTS + NORMAL
    return rows, held[at : at + 1, :]


def part(ref, f, g):
    return ref[f * TOKENS : (f + 1) * TOKENS, g * LANES : (g + 1) * LANES]


def update_kernel(k_ref, v_ref, out_ref, held):
    clear_unused(held)
    for f in range(FRAMES):
        for g in range(GROUPS):
            pos_k = jnp.maximum(part(k_ref, f, g), 0)
            rows = compact(dot(pos_k, part(v_ref, f, g), ((0,), (0,))))
            put_rows(held, f, g, rows, jnp.sum(pos_k.astype(F32), axis=0, keepdims=True))
    out_ref[...] = held[...].astype(BF16)


def decay_kernel(decay_ref, lanes_ref, row_ref):
    mine = lax.axis_index("row") * lax.axis_size("col") + lax.axis_index("col")
    decay = decay_ref[...]
    slot = iota((SLOTS, HEADS), 0)
    group = jnp.where(slot < GROUPS, slot, jnp.where(slot < NORMAL, slot - GROUPS, mine))
    own = iota((SLOTS, HEADS), 1) // PER_GROUP == group
    onto = (iota((HEADS, LANES), 0) % PER_GROUP == lane_head((HEADS, LANES))).astype(F32)
    for f in range(FRAMES):
        picked = jnp.where(own, decay[f : f + 1], 0.0)
        lanes_ref[f * SLOTS : (f + 1) * SLOTS, :] = dot(picked, onto, precision=lax.Precision.HIGHEST)
    rest = jnp.broadcast_to(decay[0:1] * decay[1:2], (8, HEADS))
    row = jnp.zeros((8, LANES), F32)
    for third in range(3):
        piece = rest.astype(BF16)
        rest = rest - piece.astype(F32)
        row = row + dot(piece, (iota((HEADS, LANES), 1) == iota((HEADS, LANES), 0) + third * HEADS).astype(BF16))
    row_ref[...] = row


def frame_sums(x_ref):
    return jnp.sum(x_ref[...].astype(F32).reshape(OWNERS, OWNED, LANES), axis=0)


def copies(block, out_ref):
    count = out_ref.shape[0] // block.shape[0]
    out_ref[...] = jnp.broadcast_to(block[None], (count,) + block.shape).reshape(out_ref.shape).astype(BF16)


def block_forward_kernel(x_ref, lanes_ref, row_ref, sums_ref, out_ref):
    sums = frame_sums(x_ref)
    sums_ref[...] = sums
    total = lanes_ref[SLOTS:, :] * sums[:SLOTS] + sums[SLOTS:]
    total = jnp.where(iota((SLOTS, LANES), 0) == EXTRA, row_ref[0:1, :], total)
    copies(jnp.concatenate([total, total], axis=0), out_ref)


def block_reverse_kernel(x_ref, lanes_ref, sums_ref, out_ref):
    sums = frame_sums(x_ref)
    sums_ref[...] = sums
    total = lanes_ref[:SLOTS, :] * (sums[:SLOTS] + lanes_ref[SLOTS:, :] * sums[SLOTS:])
    copies(jnp.concatenate([total, total], axis=0), out_ref)


def shifted(x, by, count):
    row = iota(x.shape, 0)
    if by > 0:
        return jnp.where(row < by, 1.0, pltpu.roll(x, by, 0))
    return jnp.where(row >= count + by, 1.0, pltpu.roll(x, count + by, 0))


def block_weights(held, index, count, backward):
    mine = lax.axis_index("tm")
    decays = held[pl.ds(EXTRA, count, stride=SLOTS), :].astype(BF16)
    source = iota((LANES, LANES), 0)
    onto = (source < 3 * HEADS) & (source % HEADS == index * PER_GROUP + lane_head((LANES, LANES)))
    block = dot(decays, onto.astype(BF16))
    at = iota((count, LANES), 0)
    between = at > mine if backward else at < mine
    product = shifted(jnp.where(between, block, 1.0), 1 if backward else -1, count)
    step = 1
    while step < count:
        product = product * shifted(product, step if backward else -step, count)
        step *= 2
    return jnp.where(between, product, 0.0)


def weights_kernel(y_ref, out_ref, held):
    count = y_ref.shape[0] // SLOTS
    held[...] = y_ref[...].astype(F32)
    mine = lax.axis_index("row") * lax.axis_size("col") + lax.axis_index("col")
    for i in range(GROUPS + 1):
        out_ref[i] = block_weights(held, i if i < GROUPS else mine, count, True)


def entering(held, carry, weights, count):
    carry[...] = jnp.zeros(carry.shape, F32)
    for slot in range(NORMAL + 1):
        weight = weights[GROUPS if slot == NORMAL else slot % GROUPS]
        rows = held[pl.ds(slot, count, stride=SLOTS), :]
        carry[slot : slot + 1, :] = jnp.sum(weight * rows, axis=0, keepdims=True)
    return carry[:SLOTS, :]


def states_kernel(y_ref, sums_ref, lanes_ref, out_ref, held, carry):
    count = y_ref.shape[0] // SLOTS
    held[...] = y_ref[...].astype(F32)
    mine = lax.axis_index("row") * lax.axis_size("col") + lax.axis_index("col")
    weights = [block_weights(held, i if i < GROUPS else mine, count, False) for i in range(GROUPS + 1)]
    before = entering(held, carry, weights, count)
    first = lanes_ref[:SLOTS, :] * before + sums_ref[:SLOTS, :]
    second = lanes_ref[SLOTS:, :] * first + sums_ref[SLOTS:, :]
    copies(jnp.concatenate([first, second], axis=0), out_ref)


def carried_kernel(y_ref, sums_ref, lanes_ref, weights_ref, out_ref, held, carry):
    count = y_ref.shape[0] // SLOTS
    held[...] = y_ref[...].astype(F32)
    after = entering(held, carry, [weights_ref[i] for i in range(GROUPS + 1)], count)
    second = sums_ref[SLOTS:, :] + after
    first = sums_ref[:SLOTS, :] + lanes_ref[SLOTS:, :] * second
    copies(jnp.concatenate([first, second], axis=0), out_ref)


def conv_kernel(g_ref, above_ref, below_ref, left_ref, right_ref, weight_ref, out_ref):
    at = iota((COLS, LANES), 0)
    for f in range(FRAMES):
        left = left_ref[f].astype(F32)
        right = right_ref[f].astype(F32)
        for g in range(GROUPS):
            lanes = slice(g * LANES, (g + 1) * LANES)
            taps = [weight_ref[t : t + 1, lanes] for t in range(9)]
            total = [None] * ROWS
            for source in range(-1, ROWS + 1):
                if source < 0:
                    x = above_ref[f, :, lanes]
                elif source == ROWS:
                    x = below_ref[f, :, lanes]
                else:
                    first = (f * ROWS + source) * COLS
                    x = g_ref[first : first + COLS, lanes]
                x = x.astype(F32)
                from_left = jnp.where(at == 0, left[source + 1 : source + 2, lanes], pltpu.roll(x, 1, 0))
                from_right = jnp.where(
                    at == COLS - 1, right[source + 1 : source + 2, lanes], pltpu.roll(x, COLS - 1, 0)
                )
                for row_off in (-1, 0, 1):
                    row = source + row_off
                    if 0 <= row < ROWS:
                        tap = (row_off + 1) * 3
                        add = taps[tap] * from_right + taps[tap + 1] * x + taps[tap + 2] * from_left
                        if row_off == 0:
                            add = add + x
                        total[row] = add if total[row] is None else total[row] + add
            for row in range(ROWS):
                first = (f * ROWS + row) * COLS
                out_ref[first : first + COLS, lanes] = total[row]


def query_kernel(q_ref, ga_ref, z_ref, grad_ref, out_ref, held, sent):
    held[...] = z_ref[...].astype(F32)
    clear_unused(sent)
    ones = head_ones()
    for f in range(FRAMES):
        for g in range(GROUPS):
            rows, normal = take_rows(held, f, g)
            state = spread(rows)
            query = part(q_ref, f, g)
            pos_q = jnp.maximum(query, 0)
            pos_qf = pos_q.astype(F32)
            grad_attn = part(ga_ref, f, g)
            inverse = 1.0 / (dot((pos_qf * normal).astype(BF16), ones) + 1.0)
            attn = dot(pos_q, state) * inverse
            grad_num = grad_attn * inverse
            grad_den = -dot((grad_attn * attn).astype(BF16), ones) * inverse
            grad_num = grad_num.astype(BF16)
            grad_posq = dot(grad_num, state, ((1,), (1,))) + grad_den * normal
            grad_ref[f * TOKENS : (f + 1) * TOKENS, g * LANES : (g + 1) * LANES] = jnp.where(
                pos_qf > 0, grad_posq, 0.0
            ).astype(BF16)
            local = compact(dot(pos_q, grad_num, ((0,), (0,))))
            put_rows(sent, f, g, local, jnp.sum(grad_den * pos_qf, axis=0, keepdims=True))
    out_ref[...] = sent[...].astype(BF16)


def key_kernel(k_ref, v_ref, z_ref, key_grad_ref, value_grad_ref, held):
    held[...] = z_ref[...].astype(F32)
    for f in range(FRAMES):
        for g in range(GROUPS):
            rows, normal = take_rows(held, f, g)
            carried = spread(rows)
            keys = part(k_ref, f, g)
            here = (slice(f * TOKENS, (f + 1) * TOKENS), slice(g * LANES, (g + 1) * LANES))
            grad = dot(part(v_ref, f, g), carried, ((1,), (1,))) + normal
            key_grad_ref[here] = jnp.where(keys.astype(F32) > 0, grad, 0.0).astype(BF16)
            value_grad_ref[here] = dot(jnp.maximum(keys, 0), carried).astype(BF16)


def exchange(block, axes, count):
    rows = block.shape[0] // count
    block = block.reshape(count, rows // 2, 2, LANES)
    return lax.all_to_all(block, axes, 0, 0, tiled=True).reshape(count * rows, LANES)


def neighbours(cells, axis, dim):
    count, size = lax.axis_size(axis), cells.shape[dim]
    tail = lax.slice_in_dim(cells, size - 1, size, axis=dim)
    head = lax.slice_in_dim(cells, 0, 1, axis=dim)
    up = lax.ppermute(tail, axis, [(i, i + 1) for i in range(count - 1)])
    down = lax.ppermute(head, axis, [(i + 1, i) for i in range(count - 1)])
    return up, down


def per_device(query_tokens, key_tokens, value_tokens, grad_output, frame_decay, conv_weight):
    shape = query_tokens.shape
    flat = (FRAMES * TOKENS, CH)
    blocks = lax.axis_size("tm")
    q, k, v, g = (x.reshape(flat) for x in (query_tokens, key_tokens, value_tokens, grad_output))
    space = ((OWNERS * OWNED, LANES), BF16)
    time = ((blocks * SLOTS, LANES), BF16)
    owned = ((OWNED, LANES), F32)
    held_space = pltpu.VMEM(space[0], F32)
    held_time = pltpu.VMEM(time[0], F32)
    carry = pltpu.VMEM((24, LANES), F32)
    work = 2 * FRAMES * GROUPS * TOKENS * LANES * LANES

    above, below = neighbours(grad_output, "row", 1)
    (sent,) = call(update_kernel, [space], k, v, scratch=[held_space], flops=work, name="update")
    lanes, decay_row = call(decay_kernel, [owned, ((8, LANES), F32)], frame_decay, name="decay")
    tall = jnp.concatenate([above, grad_output, below], axis=1)
    left, right = neighbours(tall, "col", 2)

    x = exchange(sent, SPACE, OWNERS)
    sums, sent = call(block_forward_kernel, [owned, time], x, lanes, decay_row, name="block_forward")
    y = exchange(sent, "tm", blocks)
    (sent,) = call(states_kernel, [space], y, sums, lanes, scratch=[held_time, carry], name="states")
    (weights,) = call(
        weights_kernel, [((GROUPS + 1, blocks, LANES), F32)], y, scratch=[held_time], name="reverse_weights"
    )
    z = exchange(sent, SPACE, OWNERS)
    (grad_attn,) = call(
        conv_kernel,
        [(flat, F32)],
        g,
        above.reshape(FRAMES, COLS, CH),
        below.reshape(FRAMES, COLS, CH),
        left.reshape(FRAMES, ROWS + 2, CH),
        right.reshape(FRAMES, ROWS + 2, CH),
        conv_weight,
        flops=20 * flat[0] * flat[1],
        name="conv",
    )
    query_grad, sent = call(
        query_kernel, [(flat, BF16), space], q, grad_attn, z, scratch=[held_space, held_space], flops=5 * work, name="query"
    )
    x = exchange(sent, SPACE, OWNERS)
    sums, sent = call(block_reverse_kernel, [owned, time], x, lanes, name="block_reverse")
    y = exchange(sent, "tm", blocks)
    (sent,) = call(carried_kernel, [space], y, sums, lanes, weights, scratch=[held_time, carry], name="carried")
    z = exchange(sent, SPACE, OWNERS)
    key_grad, value_grad = call(
        key_kernel, [(flat, BF16), (flat, BF16)], k, v, z, scratch=[held_space], flops=2 * work, name="key"
    )
    return query_grad.reshape(shape), key_grad.reshape(shape), value_grad.reshape(shape)


def solution(mesh):
    tokens = P("tm", "row", "col", None)
    return jax.shard_map(
        per_device,
        mesh=mesh,
        in_specs=(tokens, tokens, tokens, tokens, P("tm", None), P()),
        out_specs=(tokens, tokens, tokens),
        check_vma=False,
    )
```

time: 736 us -> 117 us (0.16); the launches traced: 723 us -> 116 us
  waiting for transfers between devices: 252 us -> 29.2 us
  blocking collectives: 200 us -> 31.5 us
  local copies, waits for them, and re-layouts: 143 us -> 2.53 us
  other arithmetic: 78.8 us -> 0.07 us
  starting transfers between devices: 12.7 us -> 41.2 us
  matrix products: 18.8 us -> 0 us
  between operations: 15 us -> 0.82 us
  Pallas kernels: 0 us -> 10.8 us
    psum x2 -> x0, waiting for transfers between devices: 252 us -> none  [the longest x1 136 us: per_device(): locals_all, localz_all = lax.psum((locals_all, localz_all), ('row', 'col'))]
    all_gather x2 -> x0, blocking collectives: 73.6 us -> none  [entering(): pieces = jax.tree.map(lambda part: lax.all_gather(part, axis), value)]
    unnamed x1 -> x0, blocking collectives: 63.4 us -> none
    select_n x124 -> x0, other arithmetic: 63.3 us -> none  [lap(): jnp.where(position < mine, new, old)]
    psum x2 -> x0, blocking collectives: 62.9 us -> none  [the longest x1 31.8 us: per_device(): locals_all, localz_all = lax.psum((locals_all, localz_all), ('row', 'col'))]
    reshape x76 -> x0, local copies, waits for them, and re-layouts: 35.3 us -> none  [the longest x2 9.91 us: per_device(): grad_attn = grad_attn.reshape(fr_count, count, MIXING_CHANNELS, HEAD_DIM)]
    all_to_all x0 -> x2, blocking collectives: none -> 31.5 us  [exchange(): lax.all_to_all(block, axes, 0, 0, tiled=True).reshape(count * rows, LANES)]
    all_to_all x0 -> x4, starting transfers between devices: none -> 29.3 us  [exchange(): lax.all_to_all(block, axes, 0, 0, tiled=True).reshape(count * rows, LANES)]
  transfers between devices with their start and end apart: 8 -> 8, of which waited for: 2 -> 4; matrix products, arithmetic and copies ran while one was open for 9% -> 0% of each run, Pallas kernels for 0% -> 2%
where the time goes in v1:
time: 117 us; the launch traced here: 116 us
  starting transfers between devices  41.2 us (35%)
  blocking collectives  31.5 us (27%)
  waiting for transfers between devices  29.2 us (25%)
  Pallas kernels  10.8 us (9%)
  local copies, waits for them, and re-layouts  2.53 us (2%)
    all_to_all x2, blocking collectives, exchange(): lax.all_to_all(block, axes, 0, 0, tiled=True).reshape(count * rows, LANES)  31.5 us
    all_to_all x4, starting transfers between devices, exchange(): lax.all_to_all(block, axes, 0, 0, tiled=True).reshape(count * rows, LANES)  29.3 us
    all_to_all x4, waiting for transfers between devices, exchange(): lax.all_to_all(block, axes, 0, 0, tiled=True).reshape(count * rows, LANES)  25.3 us
    pallas_call x10, Pallas kernels, call(): pl.pallas_call(body, out_shape=out_shape, in_specs=[pl.BlockSpec(memory_s...  10.8 us
    ppermute x2, starting transfers between devices, neighbours(): up = lax.ppermute(tail, axis, [(i, i + 1) for i in range(count - 1)])  8.53 us
    ppermute x2, waiting for transfers between devices, neighbours(): down = lax.ppermute(head, axis, [(i + 1, i) for i in range(count - 1)])  3.86 us
    ppermute x2, starting transfers between devices, neighbours(): down = lax.ppermute(head, axis, [(i + 1, i) for i in range(count - 1)])  3.34 us
  transfers between devices with their start and end apart: 8, of which 4 were waited for; matrix products, arithmetic and copies ran while one was open for 0% of the time, Pallas kernels for 2%

profile of v1, /device:TPU:1, one launch (start us, length us, event | category | flops | bytes accessed | tf_op | source)
XLA Modules:
  0.0 116.0 jit_solution(1383402554117971357)
XLA Ops:
  0.7 1.1 copy-done.1
  1.8 1.1 copy-done.3
  2.8 1.0 update.1
  3.9 10.2 %all-to-all-start = ((bf16[16,20,2,128]{3,2,1,0:T(2,128)(2,1)}), bf16[16,20,2,128]{3,2,1,0:T(2,128)(2,1)S(1)}, u32[]{:S(2)}, u32[]{:S(2)}) async-start(bf16[16,20,2,128]{3,2,1,0:T(2,128)(2,1)} %bitcast.8), calls=%async_computation | async-start | bytes 327680 | tf_op jit(solution)/shard_map/all_to_all | solution.py:291
  14.4 9.2 %all-to-all-done = bf16[16,20,2,128]{3,2,1,0:T(2,128)(2,1)S(1)} async-done(((bf16[16,20,2,128]{3,2,1,0:T(2,128)(2,1)}), bf16[16,20,2,128]{3,2,1,0:T(2,128)(2,1)S(1)}, u32[]{:S(2)}, u32[]{:S(2)}) %all-to-all-start) | async-done | bytes 163872 | tf_op jit(solution)/shard_map/all_to_all | solution.py:291
  23.6 0.7 block_forward.1
  24.3 11.4 %all-to-all-start.1 = ((bf16[32,10,2,128]{3,2,1,0:T(2,128)(2,1)}), bf16[32,10,2,128]{3,2,1,0:T(2,128)(2,1)S(1)}, u32[]{:S(2)}, u32[]{:S(2)}) async-start(bf16[32,10,2,128]{3,2,1,0:T(2,128)(2,1)} %bitcast.10), calls=%async_computation.1 | async-start | bytes 327680 | tf_op jit(solution)/shard_map/all_to_all | solution.py:291
  35.9 2.1 %collective-permute-start.1 = (bf16[2,1,16,1152]{3,1,0,2:T(2,128)(2,1)S(1)}, bf16[2,1,16,1152]{3,1,0,2:T(2,128)(2,1)S(1)}, u32[]{:S(2)}, u32[]{:S(2)}) collective-permute-start(bf16[2,1,16,1152]{3,1,0,2:T(2,128)(2,1)S(1)} %get-tuple-element.25), channel_id=1, source_target_pairs={{4,0},{8,4},{12,8},{5,1},{9,5},{13,9},{6,2},{10,6},{14,10},{7,3},{... | collective-permute-start | bytes 221192 | tf_op jit(solution)/shard_map/ppermute | solution.py:299
  38.0 3.6 %collective-permute-start = (bf16[2,1,16,1152]{3,1,0,2:T(2,128)(2,1)S(1)}, bf16[2,1,16,1152]{3,1,0,2:T(2,128)(2,1)S(1)}, u32[]{:S(2)}, u32[]{:S(2)}) collective-permute-start(bf16[2,1,16,1152]{3,1,0,2:T(2,128)(2,1)S(1)} %get-tuple-element.26), channel_id=1, source_target_pairs={{0,4},{4,8},{8,12},{1,5},{5,9},{9,13},{2,6},{6,10},{10,14},{3,7},{... | collective-permute-start | bytes 221192 | tf_op jit(solution)/shard_map/ppermute | solution.py:298
  41.6 5.2 %all-to-all-done.1 = bf16[32,10,2,128]{3,2,1,0:T(2,128)(2,1)S(1)} async-done(((bf16[32,10,2,128]{3,2,1,0:T(2,128)(2,1)}), bf16[32,10,2,128]{3,2,1,0:T(2,128)(2,1)S(1)}, u32[]{:S(2)}, u32[]{:S(2)}) %all-to-all-start.1) | async-done | bytes 163872 | tf_op jit(solution)/shard_map/all_to_all | solution.py:291
  46.8 1.0 states.1
  47.8 3.9 %all-to-all-start.2 = ((bf16[16,20,2,128]{3,2,1,0:T(2,128)(2,1)}), bf16[16,20,2,128]{3,2,1,0:T(2,128)(2,1)S(1)}, u32[]{:S(2)}, u32[]{:S(2)}) async-start(bf16[16,20,2,128]{3,2,1,0:T(2,128)(2,1)} %bitcast.12), calls=%async_computation.2 | async-start | bytes 327680 | tf_op jit(solution)/shard_map/all_to_all | solution.py:291
  51.7 1.3 %collective-permute-start.3 = (bf16[2,10,1,1152]{3,1,0,2:T(8,128)(2,1)S(1)}, bf16[2,10,1,1152]{3,1,0,2:T(8,128)(2,1)S(1)}, u32[]{:S(2)}, u32[]{:S(2)}) collective-permute-start(bf16[2,10,1,1152]{3,1,0,2:T(8,128)(2,1)S(1)} %get-tuple-element.23), channel_id=1, source_target_pairs={{1,0},{2,1},{3,2},{5,4},{6,5},{7,6},{9,8},{10,9},{11,10},{13,12},{... | collective-permute-start | bytes 138248 | tf_op jit(solution)/shard_map/ppermute | solution.py:299
  53.0 4.9 %collective-permute-start.2 = (bf16[2,10,1,1152]{3,1,0,2:T(8,128)(2,1)S(1)}, bf16[2,10,1,1152]{3,1,0,2:T(8,128)(2,1)S(1)}, u32[]{:S(2)}, u32[]{:S(2)}) collective-permute-start(bf16[2,10,1,1152]{3,1,0,2:T(8,128)(2,1)S(1)} %get-tuple-element.24), channel_id=1, source_target_pairs={{0,1},{1,2},{2,3},{4,5},{5,6},{6,7},{8,9},{9,10},{10,11},{12,13},{... | collective-permute-start | bytes 138248 | tf_op jit(solution)/shard_map/ppermute | solution.py:298
  58.0 3.9 %collective-permute-done.3 = bf16[2,10,1,1152]{3,1,0,2:T(8,128)(2,1)S(1)} collective-permute-done((bf16[2,10,1,1152]{3,1,0,2:T(8,128)(2,1)S(1)}, bf16[2,10,1,1152]{3,1,0,2:T(8,128)(2,1)S(1)}, u32[]{:S(2)}, u32[]{:S(2)}) %collective-permute-start.3) | collective-permute-done | bytes 46112 | tf_op jit(solution)/shard_map/ppermute | solution.py:299
  61.8 1.0 conv.1.ga_ref
  62.9 4.2 %query.1 = (bf16[256,1152]{1,0:T(8,128)(2,1)}, bf16[640,128]{1,0:T(8,128)(2,1)S(1)}) custom-call(bf16[256,1152]{1,0:T(8,128)(2,1)S(1)} %bitcast.40, f32[256,1152]{1,0:T(8,128)S(1)} %conv.1.ga_ref, bf16[640,128]{1,0:T(8,128)(2,1)S(1)} %bitcast.38), custom_call_target="tpu_custom_call" | custom-call | flops 377487360 | bytes 2686976 | tf_op jit(solution)/shard_map/query/pallas_call | solution.py:33
  67.1 18.7 %all_to_all.30 = bf16[16,20,2,128]{3,2,1,0:T(2,128)(2,1)S(1)} all-to-all(bf16[16,20,2,128]{3,2,1,0:T(2,128)(2,1)S(1)} %bitcast.43), channel_id=1, replica_groups=mesh['tm'=32,'row'=4,'col'=4] {'row','col'}, dimensions={0} | all-to-all | bytes 327680 | tf_op jit(solution)/shard_map/all_to_all | solution.py:291
  85.8 0.7 block_reverse.1
  86.5 3.9 %all-to-all-start.4 = ((bf16[32,10,2,128]{3,2,1,0:T(2,128)(2,1)}), bf16[32,10,2,128]{3,2,1,0:T(2,128)(2,1)S(1)}, u32[]{:S(2)}, u32[]{:S(2)}) async-start(bf16[32,10,2,128]{3,2,1,0:T(2,128)(2,1)} %bitcast.17), calls=%async_computation.4 | async-start | bytes 327680 | tf_op jit(solution)/shard_map/all_to_all | solution.py:291
  90.4 0.2 reverse_weights.1.weights_ref
  90.6 10.9 %all-to-all-done.4 = bf16[32,10,2,128]{3,2,1,0:T(2,128)(2,1)S(1)} async-done(((bf16[32,10,2,128]{3,2,1,0:T(2,128)(2,1)}), bf16[32,10,2,128]{3,2,1,0:T(2,128)(2,1)S(1)}, u32[]{:S(2)}, u32[]{:S(2)}) %all-to-all-start.4) | async-done | bytes 163872 | tf_op jit(solution)/shard_map/all_to_all | solution.py:291
  101.6 12.7 %all_to_all.31 = bf16[16,20,2,128]{3,2,1,0:T(2,128)(2,1)S(1)} all-to-all(bf16[16,20,2,128]{3,2,1,0:T(2,128)(2,1)S(1)} %bitcast.36), channel_id=1, replica_groups=mesh['tm'=32,'row'=4,'col'=4] {'row','col'}, dimensions={0} | all-to-all | bytes 327680 | tf_op jit(solution)/shard_map/all_to_all | solution.py:291
  114.4 1.7 %key.1 = (bf16[256,1152]{1,0:T(8,128)(2,1)}, bf16[256,1152]{1,0:T(8,128)(2,1)}) custom-call(bf16[256,1152]{1,0:T(8,128)(2,1)S(1)} %bitcast.29, bf16[256,1152]{1,0:T(8,128)(2,1)S(1)} %bitcast.31, bf16[640,128]{1,0:T(8,128)(2,1)S(1)} %bitcast.39), custom_call_target="tpu_custom_call" | custom-call | flops 150994944 | bytes 2523136 | tf_op jit(solution)/shard_map/key/pallas_call | solution.py:33
  (25 shorter events, 0.7 us)
Async XLA Ops:
  0.6 13.5 %copy-start = (bf16[2,8,16,1152]{3,2,1,0:T(8,128)(2,1)S(1)}, bf16[2,8,16,1152]{3,2,1,0:T(8,128)(2,1)}, u32[]{:S(2)}) copy-start(bf16[2,8,16,1152]{3,2,1,0:T(8,128)(2,1)} %param.9) | copy-start | bytes 1769476
  0.6 1.1 copy-start.1
  1.8 1.1 copy-start.3
  2.8 11.4 %copy-start.7 = (f32[2,36]{1,0:T(2,128)S(1)}, f32[2,36]{1,0:T(2,128)}, u32[]{:S(2)}) copy-start(f32[2,36]{1,0:T(2,128)} %decay_ref.1) | copy-start | bytes 868
  3.9 19.7 %all-to-all-start = ((bf16[16,20,2,128]{3,2,1,0:T(2,128)(2,1)}), bf16[16,20,2,128]{3,2,1,0:T(2,128)(2,1)S(1)}, u32[]{:S(2)}, u32[]{:S(2)}) async-start(bf16[16,20,2,128]{3,2,1,0:T(2,128)(2,1)} %bitcast.8), calls=%async_computation | async-start | bytes 327680 | tf_op jit(solution)/shard_map/all_to_all | solution.py:291
  24.3 22.5 %all-to-all-start.1 = ((bf16[32,10,2,128]{3,2,1,0:T(2,128)(2,1)}), bf16[32,10,2,128]{3,2,1,0:T(2,128)(2,1)S(1)}, u32[]{:S(2)}, u32[]{:S(2)}) async-start(bf16[32,10,2,128]{3,2,1,0:T(2,128)(2,1)} %bitcast.10), calls=%async_computation.1 | async-start | bytes 327680 | tf_op jit(solution)/shard_map/all_to_all | solution.py:291
  35.9 25.9 %copy-start.6 = (f32[9,1152]{1,0:T(8,128)S(1)}, f32[9,1152]{1,0:T(8,128)}, u32[]{:S(2)}) copy-start(f32[9,1152]{1,0:T(8,128)} %weight_ref.1) | copy-start | bytes 124420
  35.9 15.7 %collective-permute-start.1 = (bf16[2,1,16,1152]{3,1,0,2:T(2,128)(2,1)S(1)}, bf16[2,1,16,1152]{3,1,0,2:T(2,128)(2,1)S(1)}, u32[]{:S(2)}, u32[]{:S(2)}) collective-permute-start(bf16[2,1,16,1152]{3,1,0,2:T(2,128)(2,1)S(1)} %get-tuple-element.25), channel_id=1, source_target_pairs={{4,0},{8,4},{12,8},{5,1},{9,5},{13,9},{6,2},{10,6},{14,10},{7,3},{... | collective-permute-start | bytes 221192 | tf_op jit(solution)/shard_map/ppermute | solution.py:299
  38.0 13.7 %collective-permute-start = (bf16[2,1,16,1152]{3,1,0,2:T(2,128)(2,1)S(1)}, bf16[2,1,16,1152]{3,1,0,2:T(2,128)(2,1)S(1)}, u32[]{:S(2)}, u32[]{:S(2)}) collective-permute-start(bf16[2,1,16,1152]{3,1,0,2:T(2,128)(2,1)S(1)} %get-tuple-element.26), channel_id=1, source_target_pairs={{0,4},{4,8},{8,12},{1,5},{5,9},{9,13},{2,6},{6,10},{10,14},{3,7},{... | collective-permute-start | bytes 221192 | tf_op jit(solution)/shard_map/ppermute | solution.py:298
  47.8 15.1 %all-to-all-start.2 = ((bf16[16,20,2,128]{3,2,1,0:T(2,128)(2,1)}), bf16[16,20,2,128]{3,2,1,0:T(2,128)(2,1)S(1)}, u32[]{:S(2)}, u32[]{:S(2)}) async-start(bf16[16,20,2,128]{3,2,1,0:T(2,128)(2,1)} %bitcast.12), calls=%async_computation.2 | async-start | bytes 327680 | tf_op jit(solution)/shard_map/all_to_all | solution.py:291
  51.7 10.1 %collective-permute-start.3 = (bf16[2,10,1,1152]{3,1,0,2:T(8,128)(2,1)S(1)}, bf16[2,10,1,1152]{3,1,0,2:T(8,128)(2,1)S(1)}, u32[]{:S(2)}, u32[]{:S(2)}) collective-permute-start(bf16[2,10,1,1152]{3,1,0,2:T(8,128)(2,1)S(1)} %get-tuple-element.23), channel_id=1, source_target_pairs={{1,0},{2,1},{3,2},{5,4},{6,5},{7,6},{9,8},{10,9},{11,10},{13,12},{... | collective-permute-start | bytes 138248 | tf_op jit(solution)/shard_map/ppermute | solution.py:299
  53.0 8.8 %collective-permute-start.2 = (bf16[2,10,1,1152]{3,1,0,2:T(8,128)(2,1)S(1)}, bf16[2,10,1,1152]{3,1,0,2:T(8,128)(2,1)S(1)}, u32[]{:S(2)}, u32[]{:S(2)}) collective-permute-start(bf16[2,10,1,1152]{3,1,0,2:T(8,128)(2,1)S(1)} %get-tuple-element.24), channel_id=1, source_target_pairs={{0,1},{1,2},{2,3},{4,5},{5,6},{6,7},{8,9},{9,10},{10,11},{12,13},{... | collective-permute-start | bytes 138248 | tf_op jit(solution)/shard_map/ppermute | solution.py:298
  58.0 4.9 %copy-start.5 = (bf16[2,8,16,1152]{3,2,1,0:T(8,128)(2,1)S(1)}, bf16[2,8,16,1152]{3,2,1,0:T(8,128)(2,1)}, u32[]{:S(2)}) copy-start(bf16[2,8,16,1152]{3,2,1,0:T(8,128)(2,1)} %param.6) | copy-start | bytes 1769476
  67.1 47.3 %copy-start.2 = (bf16[2,8,16,1152]{3,2,1,0:T(8,128)(2,1)S(1)}, bf16[2,8,16,1152]{3,2,1,0:T(8,128)(2,1)}, u32[]{:S(2)}) copy-start(bf16[2,8,16,1152]{3,2,1,0:T(8,128)(2,1)} %param.7) | copy-start | bytes 1769476
  67.1 47.3 %copy-start.4 = (bf16[2,8,16,1152]{3,2,1,0:T(8,128)(2,1)S(1)}, bf16[2,8,16,1152]{3,2,1,0:T(8,128)(2,1)}, u32[]{:S(2)}) copy-start(bf16[2,8,16,1152]{3,2,1,0:T(8,128)(2,1)} %param.8) | copy-start | bytes 1769476
  86.5 15.0 %all-to-all-start.4 = ((bf16[32,10,2,128]{3,2,1,0:T(2,128)(2,1)}), bf16[32,10,2,128]{3,2,1,0:T(2,128)(2,1)S(1)}, u32[]{:S(2)}, u32[]{:S(2)}) async-start(bf16[32,10,2,128]{3,2,1,0:T(2,128)(2,1)} %bitcast.17), calls=%async_computation.4 | async-start | bytes 327680 | tf_op jit(solution)/shard_map/all_to_all | solution.py:291

commit v2 on v1

v2 whole, which is shorter than its diff:
```python
import jax
import jax.numpy as jnp
from jax import lax
from jax.experimental import pallas as pl
from jax.experimental.pallas import tpu as pltpu
from jax.sharding import PartitionSpec as P

HEADS = 36
DIM = 32
LANES = 128
GROUPS = HEADS * DIM // LANES
PER_GROUP = LANES // DIM
FRAMES = 2
ROWS = 8
COLS = 16
TOKENS = ROWS * COLS
CH = HEADS * DIM
OWNERS = 16
HALF = DIM // 2
STATES = 2 * GROUPS
EXTRA = STATES + GROUPS
SLOTS = EXTRA + 1
OWNED = FRAMES * SLOTS
BOTH = 2 * FRAMES * STATES
SPACE = ("row", "col")
VMEM_BYTES = 16 * 1024 * 1024
F32 = jnp.float32
BF16 = jnp.bfloat16


def call(body, outs, *args, scratch=(), flops=1_000_000, unread=0, name=None):
    out_shape = tuple(jax.ShapeDtypeStruct(shape, dtype) for shape, dtype in outs)
    moved = sum(a.size * a.dtype.itemsize for a in args) + sum(o.size * o.dtype.itemsize for o in out_shape)
    return pl.pallas_call(
        body,
        out_shape=out_shape,
        in_specs=[pl.BlockSpec(memory_space=pltpu.VMEM)] * (len(args) - unread)
        + [pl.BlockSpec(memory_space=pl.ANY)] * unread,
        out_specs=tuple(pl.BlockSpec(memory_space=pltpu.VMEM) for _ in outs),
        scratch_shapes=list(scratch),
        compiler_params=pltpu.CompilerParams(vmem_limit_bytes=VMEM_BYTES),
        cost_estimate=pl.CostEstimate(flops=flops, bytes_accessed=moved, transcendentals=0),
        name=name,
    )(*args)


def dot(a, b, contract=((1,), (0,)), precision=None):
    return lax.dot_general(a, b, (contract, ((), ())), preferred_element_type=F32, precision=precision)


def iota(shape, dim):
    return lax.broadcasted_iota(jnp.int32, shape, dim)


def lane_head(shape):
    return iota(shape, 1) // DIM


def compact(square):
    head = lane_head((DIM, LANES))
    out = square[(PER_GROUP - 1) * DIM :]
    for i in reversed(range(PER_GROUP - 1)):
        out = jnp.where(head == i, square[i * DIM : (i + 1) * DIM], out)
    return out


def spread(rows):
    head = lane_head((DIM, LANES))
    return jnp.concatenate([jnp.where(head == i, rows, 0.0) for i in range(PER_GROUP)], axis=0).astype(BF16)


def head_ones():
    return (iota((LANES, LANES), 0) // DIM == lane_head((LANES, LANES))).astype(BF16)


def put_rows(held, size, start, rows):
    for half in range(2):
        held[pl.ds(start + half * GROUPS, OWNERS, stride=size), :] = rows[half * HALF : (half + 1) * HALF]


def take_rows(held, size, start):
    return jnp.concatenate([held[pl.ds(start + half * GROUPS, OWNERS, stride=size), :] for half in range(2)], axis=0)


def part(ref, f, g):
    return ref[f * TOKENS : (f + 1) * TOKENS, g * LANES : (g + 1) * LANES]


def update_kernel(k_ref, v_ref, out_ref, held):
    for f in range(FRAMES):
        held[pl.ds(f * SLOTS + EXTRA, OWNERS, stride=OWNED), :] = jnp.zeros((OWNERS, LANES), F32)
        for g in range(GROUPS):
            pos_k = jnp.maximum(part(k_ref, f, g), 0)
            put_rows(held, OWNED, f * SLOTS + g, compact(dot(pos_k, part(v_ref, f, g), ((0,), (0,)))))
            normal = jnp.sum(pos_k.astype(F32), axis=0, keepdims=True)
            held[pl.ds(f * SLOTS + STATES + g, OWNERS, stride=OWNED), :] = jnp.broadcast_to(normal, (OWNERS, LANES))
    out_ref[...] = held[...].astype(BF16)


def decay_kernel(decay_ref, lanes_ref, row_ref):
    decay = decay_ref[...]
    own = iota((SLOTS, HEADS), 1) // PER_GROUP == iota((SLOTS, HEADS), 0) % GROUPS
    onto = (iota((HEADS, LANES), 0) % PER_GROUP == lane_head((HEADS, LANES))).astype(F32)
    for f in range(FRAMES):
        picked = jnp.where(own, decay[f : f + 1], 0.0)
        lanes_ref[f * SLOTS : (f + 1) * SLOTS, :] = dot(picked, onto, precision=lax.Precision.HIGHEST)
    rest = jnp.broadcast_to(decay[0:1] * decay[1:2], (8, HEADS))
    row = jnp.zeros((8, LANES), F32)
    for third in range(3):
        piece = rest.astype(BF16)
        rest = rest - piece.astype(F32)
        row = row + dot(piece, (iota((HEADS, LANES), 1) == iota((HEADS, LANES), 0) + third * HEADS).astype(BF16))
    row_ref[...] = row


def frame_sums(x_ref):
    return jnp.sum(x_ref[...].astype(F32).reshape(OWNERS, OWNED, LANES), axis=0)


def copies(block, out_ref):
    count = out_ref.shape[0] // block.shape[0]
    out_ref[...] = jnp.broadcast_to(block[None], (count,) + block.shape).reshape(out_ref.shape).astype(BF16)


def block_forward_kernel(x_ref, lanes_ref, row_ref, above_ref, below_ref, sums_ref, out_ref):
    del above_ref, below_ref
    sums = frame_sums(x_ref)
    sums_ref[...] = sums
    total = lanes_ref[SLOTS:, :] * sums[:SLOTS] + sums[SLOTS:]
    total = jnp.where(iota((SLOTS, LANES), 0) == EXTRA, row_ref[0:1, :], total)
    copies(jnp.concatenate([total, total], axis=0), out_ref)


def shifted(x, by, count):
    row = iota(x.shape, 0)
    if by > 0:
        return jnp.where(row < by, 1.0, pltpu.roll(x, by, 0))
    return jnp.where(row >= count + by, 1.0, pltpu.roll(x, count + by, 0))


def block_weights(held, index, count, backward):
    mine = lax.axis_index("tm")
    decays = held[pl.ds(EXTRA, count, stride=SLOTS), :].astype(BF16)
    source = iota((LANES, LANES), 0)
    onto = (source < 3 * HEADS) & (source % HEADS == index * PER_GROUP + lane_head((LANES, LANES)))
    block = dot(decays, onto.astype(BF16))
    at = iota((count, LANES), 0)
    between = at > mine if backward else at < mine
    product = shifted(jnp.where(between, block, 1.0), 1 if backward else -1, count)
    step = 1
    while step < count:
        product = product * shifted(product, step if backward else -step, count)
        step *= 2
    return jnp.where(between, product, 0.0)


def entering(held, carry, weights, count):
    carry[EXTRA:SLOTS, :] = jnp.zeros((1, LANES), F32)
    for slot in range(EXTRA):
        rows = held[pl.ds(slot, count, stride=SLOTS), :]
        carry[slot : slot + 1, :] = jnp.sum(weights[slot % GROUPS] * rows, axis=0, keepdims=True)
    return carry[:SLOTS, :]


def states_kernel(y_ref, sums_ref, lanes_ref, q_ref, ga_ref, own_ref, inverse_ref, num_ref, out_ref, after_ref, held, carry, sent):
    count = y_ref.shape[0] // SLOTS
    held[...] = y_ref[...].astype(F32)
    weights = [block_weights(held, g, count, False) for g in range(GROUPS)]
    before = entering(held, carry, weights, count)
    for g in range(GROUPS):
        after_ref[g] = block_weights(held, g, count, True)
    first = lanes_ref[:SLOTS, :] * before + sums_ref[:SLOTS, :]
    second = lanes_ref[SLOTS:, :] * first + sums_ref[SLOTS:, :]
    own_ref[:SLOTS, :] = first
    own_ref[SLOTS:, :] = second
    for owner in range(OWNERS):
        sent[owner * BOTH : owner * BOTH + STATES, :] = first[:STATES]
        sent[owner * BOTH + STATES : owner * BOTH + 2 * STATES, :] = second[:STATES]
    ones = head_ones()
    for f in range(FRAMES):
        for g in range(GROUPS):
            normal = (first, second)[f][STATES + g : STATES + g + 1]
            pos_q = jnp.maximum(part(q_ref, f, g), 0)
            inverse = 1.0 / (dot((pos_q.astype(F32) * normal).astype(BF16), ones) + 1.0)
            grad_num = (part(ga_ref, f, g) * inverse).astype(BF16)
            here = (slice(f * TOKENS, (f + 1) * TOKENS), slice(g * LANES, (g + 1) * LANES))
            inverse_ref[here] = inverse
            num_ref[here] = grad_num
            put_rows(sent, BOTH, (FRAMES + f) * STATES + g, compact(dot(pos_q, grad_num, ((0,), (0,)))))
    out_ref[...] = sent[...].astype(BF16)


def locals_kernel(z_ref, q_ref, num_ref, inverse_ref, lanes_ref, sums_ref, den_ref, out_ref, held):
    held[...] = z_ref[...].astype(F32)
    sums = jnp.sum(z_ref[...].astype(F32).reshape(OWNERS, BOTH, LANES), axis=0)
    ones = head_ones()
    lane = iota((TOKENS, LANES), 1) % DIM
    for f in range(FRAMES):
        sums_ref[f * SLOTS : f * SLOTS + STATES, :] = sums[(FRAMES + f) * STATES : (FRAMES + f + 1) * STATES]
        sums_ref[f * SLOTS + EXTRA : (f + 1) * SLOTS, :] = jnp.zeros((1, LANES), F32)
        packed = jnp.zeros((TOKENS, LANES), F32)
        for g in range(GROUPS):
            state = spread(take_rows(held, BOTH, f * STATES + g))
            pos_q = jnp.maximum(part(q_ref, f, g), 0)
            product = part(num_ref, f, g).astype(F32) * dot(pos_q, state)
            grad_den = -dot(product.astype(BF16), ones) * part(inverse_ref, f, g)
            packed = packed + jnp.where(lane == g, grad_den, 0.0)
            at = f * SLOTS + STATES + g
            sums_ref[at : at + 1, :] = jnp.sum(grad_den * pos_q.astype(F32), axis=0, keepdims=True)
        den_ref[f * TOKENS : (f + 1) * TOKENS, :] = packed.astype(BF16)
    total = lanes_ref[:SLOTS, :] * (sums_ref[:SLOTS, :] + lanes_ref[SLOTS:, :] * sums_ref[SLOTS:, :])
    copies(jnp.concatenate([total, total], axis=0), out_ref)


def query_kernel(z_ref, q_ref, num_ref, den_ref, own_ref, grad_ref, held):
    held[...] = z_ref[...].astype(F32)
    source = iota((LANES, LANES), 0)
    same = source // DIM == lane_head((LANES, LANES))
    for f in range(FRAMES):
        den = den_ref[f * TOKENS : (f + 1) * TOKENS, :]
        for g in range(GROUPS):
            state = spread(take_rows(held, BOTH, f * STATES + g))
            at = f * SLOTS + STATES + g
            here = (slice(f * TOKENS, (f + 1) * TOKENS), slice(g * LANES, (g + 1) * LANES))
            grad_den = dot(den, (same & (source % DIM == g)).astype(BF16))
            grad = dot(num_ref[here], state, ((1,), (1,))) + grad_den * own_ref[at : at + 1, :]
            grad_ref[here] = jnp.where(q_ref[here].astype(F32) > 0, grad, 0.0).astype(BF16)


def carried_kernel(y_ref, sums_ref, lanes_ref, weights_ref, query_ref, out_ref, held, carry):
    del query_ref
    count = y_ref.shape[0] // SLOTS
    held[...] = y_ref[...].astype(F32)
    after = entering(held, carry, [weights_ref[g] for g in range(GROUPS)], count)
    second = sums_ref[SLOTS:, :] + after
    first = sums_ref[:SLOTS, :] + lanes_ref[SLOTS:, :] * second
    copies(jnp.concatenate([first, second], axis=0), out_ref)


def conv_kernel(g_ref, above_ref, below_ref, left_ref, right_ref, weight_ref, out_ref):
    at = iota((COLS, LANES), 0)
    for f in range(FRAMES):
        left = left_ref[f].astype(F32)
        right = right_ref[f].astype(F32)
        for g in range(GROUPS):
            lanes = slice(g * LANES, (g + 1) * LANES)
            taps = [weight_ref[t : t + 1, lanes] for t in range(9)]
            total = [None] * ROWS
            for source in range(-1, ROWS + 1):
                if source < 0:
                    x = above_ref[f, :, lanes]
                elif source == ROWS:
                    x = below_ref[f, :, lanes]
                else:
                    first = (f * ROWS + source) * COLS
                    x = g_ref[first : first + COLS, lanes]
                x = x.astype(F32)
                from_left = jnp.where(at == 0, left[source + 1 : source + 2, lanes], pltpu.roll(x, 1, 0))
                from_right = jnp.where(
                    at == COLS - 1, right[source + 1 : source + 2, lanes], pltpu.roll(x, COLS - 1, 0)
                )
                for row_off in (-1, 0, 1):
                    row = source + row_off
                    if 0 <= row < ROWS:
                        tap = (row_off + 1) * 3
                        add = taps[tap] * from_right + taps[tap + 1] * x + taps[tap + 2] * from_left
                        if row_off == 0:
                            add = add + x
                        total[row] = add if total[row] is None else total[row] + add
            for row in range(ROWS):
                first = (f * ROWS + row) * COLS
                out_ref[first : first + COLS, lanes] = total[row]


def key_kernel(k_ref, v_ref, z_ref, key_grad_ref, value_grad_ref, held):
    held[...] = z_ref[...].astype(F32)
    sums = frame_sums(z_ref)
    for f in range(FRAMES):
        for g in range(GROUPS):
            carried = spread(take_rows(held, OWNED, f * SLOTS + g))
            at = f * SLOTS + STATES + g
            keys = part(k_ref, f, g)
            here = (slice(f * TOKENS, (f + 1) * TOKENS), slice(g * LANES, (g + 1) * LANES))
            grad = dot(part(v_ref, f, g), carried, ((1,), (1,))) + sums[at : at + 1]
            key_grad_ref[here] = jnp.where(keys.astype(F32) > 0, grad, 0.0).astype(BF16)
            value_grad_ref[here] = dot(jnp.maximum(keys, 0), carried).astype(BF16)


def exchange(block, axes, count):
    rows = block.shape[0] // count
    block = block.reshape(count, rows // 2, 2, LANES)
    return lax.all_to_all(block, axes, 0, 0, tiled=True).reshape(count * rows, LANES)


def neighbours(cells, axis, dim):
    count, size = lax.axis_size(axis), cells.shape[dim]
    tail = lax.slice_in_dim(cells, size - 1, size, axis=dim)
    head = lax.slice_in_dim(cells, 0, 1, axis=dim)
    up = lax.ppermute(tail, axis, [(i, i + 1) for i in range(count - 1)])
    down = lax.ppermute(head, axis, [(i + 1, i) for i in range(count - 1)])
    return up, down


def per_device(query_tokens, key_tokens, value_tokens, grad_output, frame_decay, conv_weight):
    shape = query_tokens.shape
    flat = (FRAMES * TOKENS, CH)
    blocks = lax.axis_size("tm")
    q, k, v, g = (x.reshape(flat) for x in (query_tokens, key_tokens, value_tokens, grad_output))
    space = ((OWNERS * OWNED, LANES), BF16)
    both = ((OWNERS * BOTH, LANES), BF16)
    time = ((blocks * SLOTS, LANES), BF16)
    owned = ((OWNED, LANES), F32)
    held_space, held_both, held_time = (pltpu.VMEM(kind[0], F32) for kind in (space, both, time))
    carry = pltpu.VMEM((32, LANES), F32)
    work = 2 * FRAMES * GROUPS * TOKENS * LANES * LANES

    above, below = neighbours(grad_output, "row", 1)
    (sent,) = call(update_kernel, [space], k, v, scratch=[held_space], flops=work, name="update")
    lanes, decay_row = call(decay_kernel, [owned, ((8, LANES), F32)], frame_decay, name="decay")
    x = exchange(sent, SPACE, OWNERS)
    tall = jnp.concatenate([above, grad_output, below], axis=1)
    left, right = neighbours(tall, "col", 2)
    above, below = (edge.reshape(FRAMES, COLS, CH) for edge in (above, below))
    left, right = (edge.reshape(FRAMES, ROWS + 2, CH) for edge in (left, right))
    sums, sent = call(
        block_forward_kernel, [owned, time], x, lanes, decay_row, above, below, unread=2, name="block_forward"
    )
    y = exchange(sent, "tm", blocks)
    (grad_attn,) = call(
        conv_kernel, [(flat, F32)], g, above, below, left, right, conv_weight, flops=20 * flat[0] * flat[1], name="conv"
    )
    own, inverse, grad_num, sent, weights = call(
        states_kernel,
        [owned, (flat, F32), (flat, BF16), both, ((GROUPS, blocks, LANES), F32)],
        y,
        sums,
        lanes,
        q,
        grad_attn,
        scratch=[held_time, carry, held_both],
        flops=2 * work,
        name="states",
    )
    z = exchange(sent, SPACE, OWNERS)
    sums, grad_den, sent = call(
        locals_kernel,
        [owned, ((FRAMES * TOKENS, LANES), BF16), time],
        z,
        q,
        grad_num,
        inverse,
        lanes,
        scratch=[held_both],
        flops=2 * work,
        name="locals",
    )
    y = exchange(sent, "tm", blocks)
    (query_grad,) = call(
        query_kernel, [(flat, BF16)], z, q, grad_num, grad_den, own, scratch=[held_both], flops=work, name="query"
    )
    (sent,) = call(
        carried_kernel, [space], y, sums, lanes, weights, query_grad, unread=1, scratch=[held_time, carry], name="carried"
    )
    z = exchange(sent, SPACE, OWNERS)
    key_grad, value_grad = call(
        key_kernel, [(flat, BF16), (flat, BF16)], k, v, z, scratch=[held_space], flops=2 * work, name="key"
    )
    return query_grad.reshape(shape), key_grad.reshape(shape), value_grad.reshape(shape)


def solution(mesh):
    tokens = P("tm", "row", "col", None)
    return jax.shard_map(
        per_device,
        mesh=mesh,
        in_specs=(tokens, tokens, tokens, tokens, P("tm", None), P()),
        out_specs=(tokens, tokens, tokens),
        check_vma=False,
    )
```

time: 117 us -> 110 us (0.940)
  waiting for transfers between devices: 29.2 us -> 19.4 us
  blocking collectives: 31.5 us -> 33.9 us
  Pallas kernels: 10.8 us -> 8.81 us
  starting transfers between devices: 41.2 us -> 42.7 us
    all_to_all x4 -> x3, waiting for transfers between devices: 25.3 us -> 14.4 us  [exchange(): lax.all_to_all(block, axes, 0, 0, tiled=True).reshape(count * rows, LANES)]
    all_to_all x2, blocking collectives: 31.5 us -> 33.9 us  [exchange(): lax.all_to_all(block, axes, 0, 0, tiled=True).reshape(count * rows, LANES)]
    pallas_call x10 -> x9, Pallas kernels: 10.8 us -> 8.81 us  [call(): pl.pallas_call(body, out_shape=out_shape, in_specs=[pl.BlockSpec(memory_s...]
    all_to_all x4 -> x3, starting transfers between devices: 29.3 us -> 30.8 us  [exchange(): lax.all_to_all(block, axes, 0, 0, tiled=True).reshape(count * rows, LANES)]
    ppermute x2, waiting for transfers between devices: 3.86 us -> 5.06 us  [neighbours(): down = lax.ppermute(head, axis, [(i + 1, i) for i in range(count - 1)])]
    unnamed x17 -> x19, local copies, waits for them, and re-layouts: 2.31 us -> 3.38 us
  transfers between devices with their start and end apart: 8 -> 7, of which waited for: 4 -> 5; matrix products, arithmetic and copies ran while one was open for 0% -> 0% of each run, Pallas kernels for 2% -> 3%
where the time goes in v2:
time: 110 us; the launch traced here: 109 us
  starting transfers between devices  42.7 us (39%)
  blocking collectives  33.9 us (31%)
  waiting for transfers between devices  19.4 us (18%)
  Pallas kernels  8.81 us (8%)
  local copies, waits for them, and re-layouts  3.6 us (3%)
    all_to_all x2, blocking collectives, exchange(): lax.all_to_all(block, axes, 0, 0, tiled=True).reshape(count * rows, LANES)  33.9 us
    all_to_all x3, starting transfers between devices, exchange(): lax.all_to_all(block, axes, 0, 0, tiled=True).reshape(count * rows, LANES)  30.8 us
    all_to_all x3, waiting for transfers between devices, exchange(): lax.all_to_all(block, axes, 0, 0, tiled=True).reshape(count * rows, LANES)  14.4 us
    pallas_call x9, Pallas kernels, call(): pl.pallas_call(body, out_shape=out_shape, in_specs=[pl.BlockSpec(memory_s...  8.81 us
    ppermute x2, starting transfers between devices, neighbours(): up = lax.ppermute(tail, axis, [(i, i + 1) for i in range(count - 1)])  8.34 us
    ppermute x2, waiting for transfers between devices, neighbours(): down = lax.ppermute(head, axis, [(i + 1, i) for i in range(count - 1)])  5.06 us
    ppermute x2, starting transfers between devices, neighbours(): down = lax.ppermute(head, axis, [(i + 1, i) for i in range(count - 1)])  3.54 us
    unnamed x19, local copies, waits for them, and re-layouts  3.38 us
  transfers between devices with their start and end apart: 7, of which 5 were waited for; matrix products, arithmetic and copies ran while one was open for 0% of the time, Pallas kernels for 3%

profile of v2, /device:TPU:1, one launch (start us, length us, event | category | flops | bytes accessed | tf_op | source)
XLA Modules:
  0.0 109.4 jit_solution(7382300155953921182)
XLA Ops:
  0.7 1.1 %copy-done.3 = bf16[2,8,16,1152]{3,2,1,0:T(8,128)(2,1)S(1)} copy-done((bf16[2,8,16,1152]{3,2,1,0:T(8,128)(2,1)S(1)}, bf16[2,8,16,1152]{3,2,1,0:T(8,128)(2,1)}, u32[]{:S(2)}) %copy-start.3) | copy-done | bytes 589848
  1.8 1.1 copy-done.5
  2.8 1.1 update.1
  3.9 10.3 %all-to-all-start = ((bf16[16,28,2,128]{3,2,1,0:T(2,128)(2,1)}), bf16[16,28,2,128]{3,2,1,0:T(2,128)(2,1)S(1)}, u32[]{:S(2)}, u32[]{:S(2)}) async-start(bf16[16,28,2,128]{3,2,1,0:T(2,128)(2,1)} %bitcast.2), calls=%async_computation | async-start | bytes 458752 | tf_op jit(solution)/shard_map/all_to_all | solution.py:292
  14.6 2.1 %collective-permute-start.1 = (bf16[2,1,16,1152]{3,1,0,2:T(2,128)(2,1)S(1)}, bf16[2,1,16,1152]{3,1,0,2:T(2,128)(2,1)S(1)}, u32[]{:S(2)}, u32[]{:S(2)}) collective-permute-start(bf16[2,1,16,1152]{3,1,0,2:T(2,128)(2,1)S(1)} %get-tuple-element.33), channel_id=1, source_target_pairs={{4,0},{8,4},{12,8},{5,1},{9,5},{13,9},{6,2},{10,6},{14,10},{7,3},{... | collective-permute-start | bytes 221192 | tf_op jit(solution)/shard_map/ppermute | solution.py:300
  16.7 3.5 %collective-permute-start = (bf16[2,1,16,1152]{3,1,0,2:T(2,128)(2,1)S(1)}, bf16[2,1,16,1152]{3,1,0,2:T(2,128)(2,1)S(1)}, u32[]{:S(2)}, u32[]{:S(2)}) collective-permute-start(bf16[2,1,16,1152]{3,1,0,2:T(2,128)(2,1)S(1)} %get-tuple-element.34), channel_id=1, source_target_pairs={{0,4},{4,8},{8,12},{1,5},{5,9},{9,13},{2,6},{6,10},{10,14},{3,7},{... | collective-permute-start | bytes 221192 | tf_op jit(solution)/shard_map/ppermute | solution.py:299
  20.3 3.1 %collective-permute-done.1 = bf16[2,1,16,1152]{3,1,0,2:T(2,128)(2,1)S(1)} collective-permute-done((bf16[2,1,16,1152]{3,1,0,2:T(2,128)(2,1)S(1)}, bf16[2,1,16,1152]{3,1,0,2:T(2,128)(2,1)S(1)}, u32[]{:S(2)}, u32[]{:S(2)}) %collective-permute-start.1) | collective-permute-done | bytes 73760 | tf_op jit(solution)/shard_map/ppermute | solution.py:300
  23.5 1.8 %all-to-all-done = bf16[16,28,2,128]{3,2,1,0:T(2,128)(2,1)S(1)} async-done(((bf16[16,28,2,128]{3,2,1,0:T(2,128)(2,1)}), bf16[16,28,2,128]{3,2,1,0:T(2,128)(2,1)S(1)}, u32[]{:S(2)}, u32[]{:S(2)}) %all-to-all-start) | async-done | bytes 229408 | tf_op jit(solution)/shard_map/all_to_all | solution.py:292
  25.3 0.7 block_forward.1
  26.0 11.2 %all-to-all-start.1 = ((bf16[32,14,2,128]{3,2,1,0:T(2,128)(2,1)}), bf16[32,14,2,128]{3,2,1,0:T(2,128)(2,1)S(1)}, u32[]{:S(2)}, u32[]{:S(2)}) async-start(bf16[32,14,2,128]{3,2,1,0:T(2,128)(2,1)} %bitcast.6), calls=%async_computation.1 | async-start | bytes 458752 | tf_op jit(solution)/shard_map/all_to_all | solution.py:292
  37.3 1.4 %collective-permute-start.3 = (bf16[2,10,1,1152]{3,1,0,2:T(8,128)(2,1)S(1)}, bf16[2,10,1,1152]{3,1,0,2:T(8,128)(2,1)S(1)}, u32[]{:S(2)}, u32[]{:S(2)}) collective-permute-start(bf16[2,10,1,1152]{3,1,0,2:T(8,128)(2,1)S(1)} %get-tuple-element.31), channel_id=1, source_target_pairs={{1,0},{2,1},{3,2},{5,4},{6,5},{7,6},{9,8},{10,9},{11,10},{13,12},{... | collective-permute-start | bytes 138248 | tf_op jit(solution)/shard_map/ppermute | solution.py:300
  38.8 4.9 %collective-permute-start.2 = (bf16[2,10,1,1152]{3,1,0,2:T(8,128)(2,1)S(1)}, bf16[2,10,1,1152]{3,1,0,2:T(8,128)(2,1)S(1)}, u32[]{:S(2)}, u32[]{:S(2)}) collective-permute-start(bf16[2,10,1,1152]{3,1,0,2:T(8,128)(2,1)S(1)} %get-tuple-element.32), channel_id=1, source_target_pairs={{0,1},{1,2},{2,3},{4,5},{5,6},{6,7},{8,9},{9,10},{10,11},{12,13},{... | collective-permute-start | bytes 138248 | tf_op jit(solution)/shard_map/ppermute | solution.py:299
  43.7 2.0 %collective-permute-done.3 = bf16[2,10,1,1152]{3,1,0,2:T(8,128)(2,1)S(1)} collective-permute-done((bf16[2,10,1,1152]{3,1,0,2:T(8,128)(2,1)S(1)}, bf16[2,10,1,1152]{3,1,0,2:T(8,128)(2,1)S(1)}, u32[]{:S(2)}, u32[]{:S(2)}) %collective-permute-start.3) | collective-permute-done | bytes 46112 | tf_op jit(solution)/shard_map/ppermute | solution.py:300
  45.6 1.0 conv.1.ga_ref
  46.7 2.7 %all-to-all-done.1 = bf16[32,14,2,128]{3,2,1,0:T(2,128)(2,1)S(1)} async-done(((bf16[32,14,2,128]{3,2,1,0:T(2,128)(2,1)}), bf16[32,14,2,128]{3,2,1,0:T(2,128)(2,1)S(1)}, u32[]{:S(2)}, u32[]{:S(2)}) %all-to-all-start.1) | async-done | bytes 229408 | tf_op jit(solution)/shard_map/all_to_all | solution.py:292
  49.4 1.0 states.1
  50.4 19.0 %all_to_all.25 = bf16[16,36,2,128]{3,2,1,0:T(2,128)(2,1)S(1)} all-to-all(bf16[16,36,2,128]{3,2,1,0:T(2,128)(2,1)S(1)} %bitcast.45), channel_id=1, replica_groups=mesh['tm'=32,'row'=4,'col'=4] {'row','col'}, dimensions={0} | all-to-all | bytes 589824 | tf_op jit(solution)/shard_map/all_to_all | solution.py:292
  69.5 1.4 %locals.1 = (f32[56,128]{1,0:T(8,128)S(1)}, bf16[256,128]{1,0:T(8,128)(2,1)S(1)}, bf16[896,128]{1,0:T(8,128)(2,1)}) custom-call(bf16[1152,128]{1,0:T(8,128)(2,1)S(1)} %bitcast.28, bf16[256,1152]{1,0:T(8,128)(2,1)S(1)} %bitcast.26, bf16[256,1152]{1,0:T(8,128)(2,1)S(1)} %get-tuple-element.22.num_ref, f32[256,1152]{1,0:T(8,128)S(1)} %get-tuple-element.23.inverse_ref, ...), custom_call_target="tpu_custom_call" | custom-call | flops 150994944 | bytes 3006464 | tf_op jit(solution)/shard_map/locals/pallas_call | solution.py:34
  70.9 9.3 %all-to-all-start.3 = ((bf16[32,14,2,128]{3,2,1,0:T(2,128)(2,1)}), bf16[32,14,2,128]{3,2,1,0:T(2,128)(2,1)S(1)}, u32[]{:S(2)}, u32[]{:S(2)}) async-start(bf16[32,14,2,128]{3,2,1,0:T(2,128)(2,1)} %bitcast.15), calls=%async_computation.3 | async-start | bytes 458752 | tf_op jit(solution)/shard_map/all_to_all | solution.py:292
  80.2 1.6 %query.1.query_ref = bf16[256,1152]{1,0:T(8,128)(2,1)} custom-call(bf16[1152,128]{1,0:T(8,128)(2,1)S(1)} %bitcast.29, bf16[256,1152]{1,0:T(8,128)(2,1)S(1)} %bitcast.27, bf16[256,1152]{1,0:T(8,128)(2,1)S(1)} %get-tuple-element.22.num_ref, bf16[256,128]{1,0:T(8,128)(2,1)S(1)} %get-tuple-element.24.den_ref, f32[56,128]{1,0:T(8,128)S(1)} %get-tuple-element.25.own_ref), custom_call_target="tpu_custom_call" | custom-call | flops 75497472 | bytes 2158592 | tf_op jit(solution)/shard_map/query/pallas_call | solution.py:34
  81.8 9.8 %all-to-all-done.3 = bf16[32,14,2,128]{3,2,1,0:T(2,128)(2,1)S(1)} async-done(((bf16[32,14,2,128]{3,2,1,0:T(2,128)(2,1)}), bf16[32,14,2,128]{3,2,1,0:T(2,128)(2,1)S(1)}, u32[]{:S(2)}, u32[]{:S(2)}) %all-to-all-start.3) | async-done | bytes 229408 | tf_op jit(solution)/shard_map/all_to_all | solution.py:292
  91.7 1.1 copy-done.1
  92.9 14.9 %all_to_all.26 = bf16[16,28,2,128]{3,2,1,0:T(2,128)(2,1)S(1)} all-to-all(bf16[16,28,2,128]{3,2,1,0:T(2,128)(2,1)S(1)} %bitcast.37), channel_id=1, replica_groups=mesh['tm'=32,'row'=4,'col'=4] {'row','col'}, dimensions={0} | all-to-all | bytes 458752 | tf_op jit(solution)/shard_map/all_to_all | solution.py:292
  107.7 1.6 %key.1 = (bf16[256,1152]{1,0:T(8,128)(2,1)}, bf16[256,1152]{1,0:T(8,128)(2,1)}) custom-call(bf16[256,1152]{1,0:T(8,128)(2,1)S(1)} %bitcast.33, bf16[256,1152]{1,0:T(8,128)(2,1)S(1)} %bitcast.35, bf16[896,128]{1,0:T(8,128)(2,1)S(1)} %bitcast.40), custom_call_target="tpu_custom_call" | custom-call | flops 150994944 | bytes 2588672 | tf_op jit(solution)/shard_map/key/pallas_call | solution.py:34
  (24 shorter events, 0.7 us)
Async XLA Ops:
  0.6 13.6 %copy-start.2 = (bf16[2,8,16,1152]{3,2,1,0:T(8,128)(2,1)S(1)}, bf16[2,8,16,1152]{3,2,1,0:T(8,128)(2,1)}, u32[]{:S(2)}) copy-start(bf16[2,8,16,1152]{3,2,1,0:T(8,128)(2,1)} %param.9) | copy-start | bytes 1769476
  0.6 1.1 %copy-start.3 = (bf16[2,8,16,1152]{3,2,1,0:T(8,128)(2,1)S(1)}, bf16[2,8,16,1152]{3,2,1,0:T(8,128)(2,1)}, u32[]{:S(2)}) copy-start(bf16[2,8,16,1152]{3,2,1,0:T(8,128)(2,1)} %param.7) | copy-start | bytes 1769476
  1.8 1.1 copy-start.5
  3.9 16.2 %copy-start.8 = (f32[2,36]{1,0:T(2,128)S(1)}, f32[2,36]{1,0:T(2,128)}, u32[]{:S(2)}) copy-start(f32[2,36]{1,0:T(2,128)} %decay_ref.1) | copy-start | bytes 868
  3.9 21.4 %all-to-all-start = ((bf16[16,28,2,128]{3,2,1,0:T(2,128)(2,1)}), bf16[16,28,2,128]{3,2,1,0:T(2,128)(2,1)S(1)}, u32[]{:S(2)}, u32[]{:S(2)}) async-start(bf16[16,28,2,128]{3,2,1,0:T(2,128)(2,1)} %bitcast.2), calls=%async_computation | async-start | bytes 458752 | tf_op jit(solution)/shard_map/all_to_all | solution.py:292
  14.6 8.9 %collective-permute-start.1 = (bf16[2,1,16,1152]{3,1,0,2:T(2,128)(2,1)S(1)}, bf16[2,1,16,1152]{3,1,0,2:T(2,128)(2,1)S(1)}, u32[]{:S(2)}, u32[]{:S(2)}) collective-permute-start(bf16[2,1,16,1152]{3,1,0,2:T(2,128)(2,1)S(1)} %get-tuple-element.33), channel_id=1, source_target_pairs={{4,0},{8,4},{12,8},{5,1},{9,5},{13,9},{6,2},{10,6},{14,10},{7,3},{... | collective-permute-start | bytes 221192 | tf_op jit(solution)/shard_map/ppermute | solution.py:300
  16.7 6.8 %collective-permute-start = (bf16[2,1,16,1152]{3,1,0,2:T(2,128)(2,1)S(1)}, bf16[2,1,16,1152]{3,1,0,2:T(2,128)(2,1)S(1)}, u32[]{:S(2)}, u32[]{:S(2)}) collective-permute-start(bf16[2,1,16,1152]{3,1,0,2:T(2,128)(2,1)S(1)} %get-tuple-element.34), channel_id=1, source_target_pairs={{0,4},{4,8},{8,12},{1,5},{5,9},{9,13},{2,6},{6,10},{10,14},{3,7},{... | collective-permute-start | bytes 221192 | tf_op jit(solution)/shard_map/ppermute | solution.py:299
  20.3 25.3 %copy-start.7 = (f32[9,1152]{1,0:T(8,128)S(1)}, f32[9,1152]{1,0:T(8,128)}, u32[]{:S(2)}) copy-start(f32[9,1152]{1,0:T(8,128)} %weight_ref.1) | copy-start | bytes 124420
  26.0 23.4 %all-to-all-start.1 = ((bf16[32,14,2,128]{3,2,1,0:T(2,128)(2,1)}), bf16[32,14,2,128]{3,2,1,0:T(2,128)(2,1)S(1)}, u32[]{:S(2)}, u32[]{:S(2)}) async-start(bf16[32,14,2,128]{3,2,1,0:T(2,128)(2,1)} %bitcast.6), calls=%async_computation.1 | async-start | bytes 458752 | tf_op jit(solution)/shard_map/all_to_all | solution.py:292
  37.3 12.1 %copy-start = (bf16[2,8,16,1152]{3,2,1,0:T(8,128)(2,1)S(1)}, bf16[2,8,16,1152]{3,2,1,0:T(8,128)(2,1)}, u32[]{:S(2)}) copy-start(bf16[2,8,16,1152]{3,2,1,0:T(8,128)(2,1)} %param.6) | copy-start | bytes 1769476
  37.3 8.3 %collective-permute-start.3 = (bf16[2,10,1,1152]{3,1,0,2:T(8,128)(2,1)S(1)}, bf16[2,10,1,1152]{3,1,0,2:T(8,128)(2,1)S(1)}, u32[]{:S(2)}, u32[]{:S(2)}) collective-permute-start(bf16[2,10,1,1152]{3,1,0,2:T(8,128)(2,1)S(1)} %get-tuple-element.31), channel_id=1, source_target_pairs={{1,0},{2,1},{3,2},{5,4},{6,5},{7,6},{9,8},{10,9},{11,10},{13,12},{... | collective-permute-start | bytes 138248 | tf_op jit(solution)/shard_map/ppermute | solution.py:300
  38.8 6.9 %collective-permute-start.2 = (bf16[2,10,1,1152]{3,1,0,2:T(8,128)(2,1)S(1)}, bf16[2,10,1,1152]{3,1,0,2:T(8,128)(2,1)S(1)}, u32[]{:S(2)}, u32[]{:S(2)}) collective-permute-start(bf16[2,10,1,1152]{3,1,0,2:T(8,128)(2,1)S(1)} %get-tuple-element.32), channel_id=1, source_target_pairs={{0,1},{1,2},{2,3},{4,5},{5,6},{6,7},{8,9},{9,10},{10,11},{12,13},{... | collective-permute-start | bytes 138248 | tf_op jit(solution)/shard_map/ppermute | solution.py:299
  70.9 20.8 %all-to-all-start.3 = ((bf16[32,14,2,128]{3,2,1,0:T(2,128)(2,1)}), bf16[32,14,2,128]{3,2,1,0:T(2,128)(2,1)S(1)}, u32[]{:S(2)}, u32[]{:S(2)}) async-start(bf16[32,14,2,128]{3,2,1,0:T(2,128)(2,1)} %bitcast.15), calls=%async_computation.3 | async-start | bytes 458752 | tf_op jit(solution)/shard_map/all_to_all | solution.py:292
  80.2 27.5 %copy-start.4 = (bf16[2,8,16,1152]{3,2,1,0:T(8,128)(2,1)S(1)}, bf16[2,8,16,1152]{3,2,1,0:T(8,128)(2,1)}, u32[]{:S(2)}) copy-start(bf16[2,8,16,1152]{3,2,1,0:T(8,128)(2,1)} %param.7) | copy-start | bytes 1769476
  80.2 27.5 %copy-start.6 = (bf16[2,8,16,1152]{3,2,1,0:T(8,128)(2,1)S(1)}, bf16[2,8,16,1152]{3,2,1,0:T(8,128)(2,1)}, u32[]{:S(2)}) copy-start(bf16[2,8,16,1152]{3,2,1,0:T(8,128)(2,1)} %param.8) | copy-start | bytes 1769476
  91.7 1.1 copy-start.1

commit v3 on v2

--- a/solution.py
+++ b/solution.py
@@ -22,23 +22,26 @@
 SLOTS = EXTRA + 1
 OWNED = FRAMES * SLOTS
 BOTH = 2 * FRAMES * STATES
+PIECE = 64
+PIECES = FRAMES * TOKENS // PIECE
 SPACE = ("row", "col")
 VMEM_BYTES = 16 * 1024 * 1024
+WIDE_BYTES = 60 * 1024 * 1024
 F32 = jnp.float32
 BF16 = jnp.bfloat16
 
 
-def call(body, outs, *args, scratch=(), flops=1_000_000, unread=0, name=None):
+def call(body, outs, *args, far=0, unread=0, far_outs=0, scratch=(), flops=1_000_000, vmem=VMEM_BYTES, name=None):
     out_shape = tuple(jax.ShapeDtypeStruct(shape, dtype) for shape, dtype in outs)
     moved = sum(a.size * a.dtype.itemsize for a in args) + sum(o.size * o.dtype.itemsize for o in out_shape)
+    near, away = pl.BlockSpec(memory_space=pltpu.VMEM), pl.BlockSpec(memory_space=pltpu.HBM)
     return pl.pallas_call(
         body,
         out_shape=out_shape,
-        in_specs=[pl.BlockSpec(memory_space=pltpu.VMEM)] * (len(args) - unread)
-        + [pl.BlockSpec(memory_space=pl.ANY)] * unread,
-        out_specs=tuple(pl.BlockSpec(memory_space=pltpu.VMEM) for _ in outs),
+        in_specs=[near] * (len(args) - far - unread) + [away] * far + [pl.BlockSpec(memory_space=pl.ANY)] * unread,
+        out_specs=tuple([near] * (len(outs) - far_outs) + [away] * far_outs),
         scratch_shapes=list(scratch),
-        compiler_params=pltpu.CompilerParams(vmem_limit_bytes=VMEM_BYTES),
+        compiler_params=pltpu.CompilerParams(vmem_limit_bytes=vmem),
         cost_estimate=pl.CostEstimate(flops=flops, bytes_accessed=moved, transcendentals=0),
         name=name,
     )(*args)
@@ -84,17 +87,6 @@
 
 def part(ref, f, g):
     return ref[f * TOKENS : (f + 1) * TOKENS, g * LANES : (g + 1) * LANES]
-
-
-def update_kernel(k_ref, v_ref, out_ref, held):
-    for f in range(FRAMES):
-        held[pl.ds(f * SLOTS + EXTRA, OWNERS, stride=OWNED), :] = jnp.zeros((OWNERS, LANES), F32)
-        for g in range(GROUPS):
-            pos_k = jnp.maximum(part(k_ref, f, g), 0)
-            put_rows(held, OWNED, f * SLOTS + g, compact(dot(pos_k, part(v_ref, f, g), ((0,), (0,)))))
-            normal = jnp.sum(pos_k.astype(F32), axis=0, keepdims=True)
-            held[pl.ds(f * SLOTS + STATES + g, OWNERS, stride=OWNED), :] = jnp.broadcast_to(normal, (OWNERS, LANES))
-    out_ref[...] = held[...].astype(BF16)
 
 
 def decay_kernel(decay_ref, lanes_ref, row_ref):
@@ -113,6 +105,31 @@
     row_ref[...] = row
 
 
+def update_kernel(k_ref, v_ref, out_ref, held, keys, values, sems):
+    pieces = [
+        [
+            pltpu.make_async_copy(source.at[piece], target.at[piece], sems.at[i, j])
+            for i, (source, target) in enumerate(((k_ref, keys), (v_ref, values)))
+        ]
+        for j, piece in enumerate(pl.ds(j * PIECE, PIECE) for j in range(PIECES))
+    ]
+    for piece in pieces:
+        for move in piece:
+            move.start()
+    for f in range(FRAMES):
+        held[pl.ds(f * SLOTS + EXTRA, OWNERS, stride=OWNED), :] = jnp.zeros((OWNERS, LANES), F32)
+    for f in range(FRAMES):
+        for piece in pieces[f * PIECES // FRAMES : (f + 1) * PIECES // FRAMES]:
+            for move in piece:
+                move.wait()
+        for g in range(GROUPS):
+            pos_k = jnp.maximum(part(keys, f, g), 0)
+            put_rows(held, OWNED, f * SLOTS + g, compact(dot(pos_k, part(values, f, g), ((0,), (0,)))))
+            normal = jnp.sum(pos_k.astype(F32), axis=0, keepdims=True)
+            held[pl.ds(f * SLOTS + STATES + g, OWNERS, stride=OWNED), :] = jnp.broadcast_to(normal, (OWNERS, LANES))
+    out_ref[...] = held[...].astype(BF16)
+
+
 def frame_sums(x_ref):
     return jnp.sum(x_ref[...].astype(F32).reshape(OWNERS, OWNED, LANES), axis=0)
 
@@ -122,8 +139,7 @@
     out_ref[...] = jnp.broadcast_to(block[None], (count,) + block.shape).reshape(out_ref.shape).astype(BF16)
 
 
-def block_forward_kernel(x_ref, lanes_ref, row_ref, above_ref, below_ref, sums_ref, out_ref):
-    del above_ref, below_ref
+def block_forward_kernel(x_ref, lanes_ref, row_ref, sums_ref, out_ref):
     sums = frame_sums(x_ref)
     sums_ref[...] = sums
     total = lanes_ref[SLOTS:, :] * sums[:SLOTS] + sums[SLOTS:]
@@ -162,7 +178,42 @@
     return carry[:SLOTS, :]
 
 
-def states_kernel(y_ref, sums_ref, lanes_ref, q_ref, ga_ref, own_ref, inverse_ref, num_ref, out_ref, after_ref, held, carry, sent):
+def around(x, before, after):
+    at = iota(x.shape, 0)
+    from_left = jnp.where(at == 0, before, pltpu.roll(x, 1, 0))
+    from_right = jnp.where(at == COLS - 1, after, pltpu.roll(x, COLS - 1, 0))
+    return from_right, x, from_left
+
+
+def weighted(taps, row_off, cells):
+    tap = (row_off + 1) * 3
+    return taps[tap] * cells[0] + taps[tap + 1] * cells[1] + taps[tap + 2] * cells[2]
+
+
+def from_row(ref, taps, row_off, f, lanes):
+    corners = ref[FRAMES * COLS :, lanes].astype(F32)
+    x = ref[f * COLS : (f + 1) * COLS, lanes].astype(F32)
+    return weighted(taps, row_off, around(x, corners[2 * f : 2 * f + 1], corners[2 * f + 1 : 2 * f + 2]))
+
+
+def states_kernel(
+    y_ref,
+    sums_ref,
+    lanes_ref,
+    q_ref,
+    ga_ref,
+    above_ref,
+    below_ref,
+    weight_ref,
+    own_ref,
+    inverse_ref,
+    num_ref,
+    out_ref,
+    after_ref,
+    held,
+    carry,
+    sent,
+):
     count = y_ref.shape[0] // SLOTS
     held[...] = y_ref[...].astype(F32)
     weights = [block_weights(held, g, count, False) for g in range(GROUPS)]
@@ -182,7 +233,13 @@
             normal = (first, second)[f][STATES + g : STATES + g + 1]
             pos_q = jnp.maximum(part(q_ref, f, g), 0)
             inverse = 1.0 / (dot((pos_q.astype(F32) * normal).astype(BF16), ones) + 1.0)
-            grad_num = (part(ga_ref, f, g) * inverse).astype(BF16)
+            lanes = slice(g * LANES, (g + 1) * LANES)
+            taps = [weight_ref[t : t + 1, lanes] for t in range(9)]
+            inner = part(ga_ref, f, g)
+            top = inner[:COLS] + from_row(above_ref, taps, 1, f, lanes)
+            bottom = inner[-COLS:] + from_row(below_ref, taps, -1, f, lanes)
+            grad_attn = jnp.concatenate([top, inner[COLS:-COLS], bottom], axis=0)
+            grad_num = (grad_attn * inverse).astype(BF16)
             here = (slice(f * TOKENS, (f + 1) * TOKENS), slice(g * LANES, (g + 1) * LANES))
             inverse_ref[here] = inverse
             num_ref[here] = grad_num
@@ -227,8 +284,7 @@
             grad_ref[here] = jnp.where(q_ref[here].astype(F32) > 0, grad, 0.0).astype(BF16)
 
 
-def carried_kernel(y_ref, sums_ref, lanes_ref, weights_ref, query_ref, out_ref, held, carry):
-    del query_ref
+def carried_kernel(y_ref, sums_ref, lanes_ref, weights_ref, out_ref, held, carry):
     count = y_ref.shape[0] // SLOTS
     held[...] = y_ref[...].astype(F32)
     after = entering(held, carry, [weights_ref[g] for g in range(GROUPS)], count)
@@ -237,33 +293,44 @@
     copies(jnp.concatenate([first, second], axis=0), out_ref)
 
 
-def conv_kernel(g_ref, above_ref, below_ref, left_ref, right_ref, weight_ref, out_ref):
-    at = iota((COLS, LANES), 0)
-    for f in range(FRAMES):
-        left = left_ref[f].astype(F32)
-        right = right_ref[f].astype(F32)
+def edge_cols_kernel(g_ref, first_ref, last_ref, first, last):
+    for at in range(FRAMES * ROWS):
+        x = g_ref[at * COLS : (at + 1) * COLS, :].astype(F32)
+        first[at : at + 1, :] = x[:1]
+        last[at : at + 1, :] = x[COLS - 1 :]
+    first_ref[...] = first[...].astype(BF16)
+    last_ref[...] = last[...].astype(BF16)
+
+
+def edge_rows_kernel(g_ref, left_ref, right_ref, first_ref, last_ref, corners):
+    left = left_ref[...].astype(F32)
+    right = right_ref[...].astype(F32)
+    for out_ref, row in ((first_ref, 0), (last_ref, ROWS - 1)):
+        corners[...] = jnp.zeros(corners.shape, F32)
+        for f in range(FRAMES):
+            at = f * ROWS + row
+            out_ref[f * COLS : (f + 1) * COLS, :] = g_ref[at * COLS : (at + 1) * COLS, :]
+            corners[2 * f : 2 * f + 1, :] = left[at : at + 1]
+            corners[2 * f + 1 : 2 * f + 2, :] = right[at : at + 1]
+        out_ref[FRAMES * COLS :, :] = corners[...].astype(BF16)
+
+
+def conv_kernel(g_ref, left_ref, right_ref, weight_ref, out_ref):
+    left = left_ref[...].astype(F32)
+    right = right_ref[...].astype(F32)
+    for f in range(FRAMES):
         for g in range(GROUPS):
             lanes = slice(g * LANES, (g + 1) * LANES)
             taps = [weight_ref[t : t + 1, lanes] for t in range(9)]
             total = [None] * ROWS
-            for source in range(-1, ROWS + 1):
-                if source < 0:
-                    x = above_ref[f, :, lanes]
-                elif source == ROWS:
-                    x = below_ref[f, :, lanes]
-                else:
-                    first = (f * ROWS + source) * COLS
-                    x = g_ref[first : first + COLS, lanes]
-                x = x.astype(F32)
-                from_left = jnp.where(at == 0, left[source + 1 : source + 2, lanes], pltpu.roll(x, 1, 0))
-                from_right = jnp.where(
-                    at == COLS - 1, right[source + 1 : source + 2, lanes], pltpu.roll(x, COLS - 1, 0)
-                )
+            for source in range(ROWS):
+                first = f * ROWS + source
+                x = g_ref[first * COLS : (first + 1) * COLS, lanes].astype(F32)
+                cells = around(x, left[first : first + 1, lanes], right[first : first + 1, lanes])
                 for row_off in (-1, 0, 1):
                     row = source + row_off
                     if 0 <= row < ROWS:
-                        tap = (row_off + 1) * 3
-                        add = taps[tap] * from_right + taps[tap + 1] * x + taps[tap + 2] * from_left
+                        add = weighted(taps, row_off, cells)
                         if row_off == 0:
                             add = add + x
                         total[row] = add if total[row] is None else total[row] + add
@@ -272,9 +339,10 @@
                 out_ref[first : first + COLS, lanes] = total[row]
 
 
-def key_kernel(k_ref, v_ref, z_ref, key_grad_ref, value_grad_ref, held):
+def key_kernel(k_ref, v_ref, z_ref, key_grad_ref, value_grad_ref, held, key_grad, value_grad, sems):
     held[...] = z_ref[...].astype(F32)
     sums = frame_sums(z_ref)
+    moves = []
     for f in range(FRAMES):
         for g in range(GROUPS):
             carried = spread(take_rows(held, OWNED, f * SLOTS + g))
@@ -282,8 +350,16 @@
             keys = part(k_ref, f, g)
             here = (slice(f * TOKENS, (f + 1) * TOKENS), slice(g * LANES, (g + 1) * LANES))
             grad = dot(part(v_ref, f, g), carried, ((1,), (1,))) + sums[at : at + 1]
-            key_grad_ref[here] = jnp.where(keys.astype(F32) > 0, grad, 0.0).astype(BF16)
-            value_grad_ref[here] = dot(jnp.maximum(keys, 0), carried).astype(BF16)
+            key_grad[here] = jnp.where(keys.astype(F32) > 0, grad, 0.0).astype(BF16)
+            value_grad[here] = dot(jnp.maximum(keys, 0), carried).astype(BF16)
+        for j in range(f * PIECES // FRAMES, (f + 1) * PIECES // FRAMES):
+            piece = pl.ds(j * PIECE, PIECE)
+            for i, (source, target) in enumerate(((key_grad, key_grad_ref), (value_grad, value_grad_ref))):
+                move = pltpu.make_async_copy(source.at[piece], target.at[piece], sems.at[i, j])
+                move.start()
+                moves.append(move)
+    for move in moves:
+        move.wait()
 
 
 def exchange(block, axes, count):
@@ -292,13 +368,11 @@
     return lax.all_to_all(block, axes, 0, 0, tiled=True).reshape(count * rows, LANES)
 
 
-def neighbours(cells, axis, dim):
-    count, size = lax.axis_size(axis), cells.shape[dim]
-    tail = lax.slice_in_dim(cells, size - 1, size, axis=dim)
-    head = lax.slice_in_dim(cells, 0, 1, axis=dim)
-    up = lax.ppermute(tail, axis, [(i, i + 1) for i in range(count - 1)])
-    down = lax.ppermute(head, axis, [(i + 1, i) for i in range(count - 1)])
-    return up, down
+def neighbours(first, last, axis):
+    count = lax.axis_size(axis)
+    before = lax.ppermute(last, axis, [(i, i + 1) for i in range(count - 1)])
+    after = lax.ppermute(first, axis, [(i + 1, i) for i in range(count - 1)])
+    return before, after
 
 
 def per_device(query_tokens, key_tokens, value_tokens, grad_output, frame_decay, conv_weight):
@@ -314,20 +388,32 @@
     carry = pltpu.VMEM((32, LANES), F32)
     work = 2 * FRAMES * GROUPS * TOKENS * LANES * LANES
 
-    above, below = neighbours(grad_output, "row", 1)
-    (sent,) = call(update_kernel, [space], k, v, scratch=[held_space], flops=work, name="update")
+    buffer = pltpu.VMEM(flat, BF16)
+    copies_done = pltpu.SemaphoreType.DMA((2, PIECES))
+    (sent,) = call(
+        update_kernel,
+        [space],
+        k,
+        v,
+        far=2,
+        scratch=[held_space, buffer, buffer, copies_done],
+        flops=work,
+        vmem=WIDE_BYTES,
+        name="update",
+    )
     lanes, decay_row = call(decay_kernel, [owned, ((8, LANES), F32)], frame_decay, name="decay")
     x = exchange(sent, SPACE, OWNERS)
-    tall = jnp.concatenate([above, grad_output, below], axis=1)
-    left, right = neighbours(tall, "col", 2)
-    above, below = (edge.reshape(FRAMES, COLS, CH) for edge in (above, below))
-    left, right = (edge.reshape(FRAMES, ROWS + 2, CH) for edge in (left, right))
-    sums, sent = call(
-        block_forward_kernel, [owned, time], x, lanes, decay_row, above, below, unread=2, name="block_forward"
-    )
+    side = ((FRAMES * ROWS, CH), BF16)
+    edge = ((FRAMES * COLS + 16, CH), BF16)
+    held_side = pltpu.VMEM(side[0], F32)
+    first, last = call(edge_cols_kernel, [side, side], g, scratch=[held_side, held_side], name="edge_cols")
+    left, right = neighbours(first, last, "col")
+    first, last = call(edge_rows_kernel, [edge, edge], g, left, right, scratch=[held_side], flops=20_000_000_000, name="edge_rows")
+    above, below = neighbours(first, last, "row")
+    sums, sent = call(block_forward_kernel, [owned, time], x, lanes, decay_row, name="block_forward")
     y = exchange(sent, "tm", blocks)
     (grad_attn,) = call(
-        conv_kernel, [(flat, F32)], g, above, below, left, right, conv_weight, flops=20 * flat[0] * flat[1], name="conv"
+        conv_kernel, [(flat, F32)], g, left, right, conv_weight, flops=20 * flat[0] * flat[1], name="conv"
     )
     own, inverse, grad_num, sent, weights = call(
         states_kernel,
@@ -337,6 +423,9 @@
         lanes,
         q,
         grad_attn,
+        above,
+        below,
+        conv_weight,
         scratch=[held_time, carry, held_both],
         flops=2 * work,
         name="states",
@@ -358,12 +447,18 @@
     (query_grad,) = call(
         query_kernel, [(flat, BF16)], z, q, grad_num, grad_den, own, scratch=[held_both], flops=work, name="query"
     )
-    (sent,) = call(
-        carried_kernel, [space], y, sums, lanes, weights, query_grad, unread=1, scratch=[held_time, carry], name="carried"
-    )
+    (sent,) = call(carried_kernel, [space], y, sums, lanes, weights, scratch=[held_time, carry], name="carried")
     z = exchange(sent, SPACE, OWNERS)
     key_grad, value_grad = call(
-        key_kernel, [(flat, BF16), (flat, BF16)], k, v, z, scratch=[held_space], flops=2 * work, name="key"
+        key_kernel,
+        [(flat, BF16), (flat, BF16)],
+        k,
+        v,
+        z,
+        far_outs=2,
+        scratch=[held_space, buffer, buffer, copies_done],
+        flops=2 * work,
+        name="key",
     )
     return query_grad.reshape(shape), key_grad.reshape(shape), value_grad.reshape(shape)
 

time: 110 us -> 103 us (0.936)
  starting transfers between devices: 42.7 us -> 35.7 us
  local copies, waits for them, and re-layouts: 3.6 us -> 0.03 us
  Pallas kernels: 8.81 us -> 10.4 us
  waiting for transfers between devices: 19.4 us -> 20.9 us
    all_to_all x3, starting transfers between devices: 30.8 us -> 25.7 us  [exchange(): lax.all_to_all(block, axes, 0, 0, tiled=True).reshape(count * rows, LANES)]
    all_to_all x3, waiting for transfers between devices: 14.4 us -> 17.9 us  [exchange(): lax.all_to_all(block, axes, 0, 0, tiled=True).reshape(count * rows, LANES)]
    unnamed x19 -> x12, local copies, waits for them, and re-layouts: 3.38 us -> 0.03 us
    ppermute x4, waiting for transfers between devices: 5.06 us -> 3.02 us  [the longest x2 3.02 us: neighbours(): after = lax.ppermute(first, axis, [(i + 1, i) for i in range(count - 1)])]
    ppermute x4, starting transfers between devices: 11.9 us -> 9.93 us  [the longest x2 6.23 us: neighbours(): before = lax.ppermute(last, axis, [(i, i + 1) for i in range(count - 1)])]
    pallas_call x9 -> x11, Pallas kernels: 8.81 us -> 10.4 us  [call(): pl.pallas_call(body, out_shape=out_shape, in_specs=[near] * (len(args) -...]
  transfers between devices with their start and end apart: 7 -> 7, of which waited for: 5 -> 4; matrix products, arithmetic and copies ran while one was open for 0% -> 0% of each run, Pallas kernels for 3% -> 4%
where the time goes in v3:
time: 103 us; the launch traced here: 102 us
  starting transfers between devices  35.7 us (35%)
  blocking collectives  34.1 us (33%)
  waiting for transfers between devices  20.9 us (20%)
  Pallas kernels  10.4 us (10%)
    all_to_all x2, blocking collectives, exchange(): lax.all_to_all(block, axes, 0, 0, tiled=True).reshape(count * rows, LANES)  34.1 us
    all_to_all x3, starting transfers between devices, exchange(): lax.all_to_all(block, axes, 0, 0, tiled=True).reshape(count * rows, LANES)  25.7 us
    all_to_all x3, waiting for transfers between devices, exchange(): lax.all_to_all(block, axes, 0, 0, tiled=True).reshape(count * rows, LANES)  17.9 us
    pallas_call x11, Pallas kernels, call(): pl.pallas_call(body, out_shape=out_shape, in_specs=[near] * (len(args) -...  10.4 us
    ppermute x2, starting transfers between devices, neighbours(): before = lax.ppermute(last, axis, [(i, i + 1) for i in range(count - 1)])  6.23 us
    ppermute x2, starting transfers between devices, neighbours(): after = lax.ppermute(first, axis, [(i + 1, i) for i in range(count - 1)])  3.7 us
    ppermute x2, waiting for transfers between devices, neighbours(): after = lax.ppermute(first, axis, [(i + 1, i) for i in range(count - 1)])  3.02 us
  transfers between devices with their start and end apart: 7, of which 4 were waited for; matrix products, arithmetic and copies ran while one was open for 0% of the time, Pallas kernels for 4%

profile of v3, /device:TPU:1, one launch (start us, length us, event | category | flops | bytes accessed | tf_op | source)
XLA Modules:
  0.0 101.9 jit_solution(5380226003104941112)
XLA Ops:
  0.7 2.5 %update.1 = bf16[896,128]{1,0:T(8,128)(2,1)} custom-call(bf16[256,1152]{1,0:T(8,128)(2,1)} %bitcast.25, bf16[256,1152]{1,0:T(8,128)(2,1)} %bitcast.27), custom_call_target="tpu_custom_call" | custom-call | flops 75497472 | bytes 1409024 | tf_op jit(solution)/shard_map/update/pallas_call | solution.py:38
  3.2 10.2 %all-to-all-start = ((bf16[16,28,2,128]{3,2,1,0:T(2,128)(2,1)}), bf16[16,28,2,128]{3,2,1,0:T(2,128)(2,1)S(1)}, u32[]{:S(2)}, u32[]{:S(2)}) async-start(bf16[16,28,2,128]{3,2,1,0:T(2,128)(2,1)} %bitcast.35), calls=%async_computation | async-start | bytes 458752 | tf_op jit(solution)/shard_map/all_to_all | solution.py:368
  13.4 0.1 edge_cols.1
  13.5 4.2 %collective-permute-start = (bf16[16,1152]{1,0:T(8,128)(2,1)S(1)}, bf16[16,1152]{1,0:T(8,128)(2,1)S(1)}, u32[]{:S(2)}, u32[]{:S(2)}) collective-permute-start(bf16[16,1152]{1,0:T(8,128)(2,1)S(1)} %get-tuple-element.25), channel_id=1, source_target_pairs={{0,1},{1,2},{2,3},{4,5},{5,6},{6,7},{8,9},{9,10},{10,11},{12,13},{... | collective-permute-start | bytes 110600 | tf_op jit(solution)/shard_map/ppermute | solution.py:373
  17.7 1.3 %collective-permute-start.1 = (bf16[16,1152]{1,0:T(8,128)(2,1)S(1)}, bf16[16,1152]{1,0:T(8,128)(2,1)S(1)}, u32[]{:S(2)}, u32[]{:S(2)}) collective-permute-start(bf16[16,1152]{1,0:T(8,128)(2,1)S(1)} %get-tuple-element.26), channel_id=1, source_target_pairs={{1,0},{2,1},{3,2},{5,4},{6,5},{7,6},{9,8},{10,9},{11,10},{13,12},{... | collective-permute-start | bytes 110600 | tf_op jit(solution)/shard_map/ppermute | solution.py:374
  19.0 0.2 decay.1
  19.2 6.1 %all-to-all-done = bf16[16,28,2,128]{3,2,1,0:T(2,128)(2,1)S(1)} async-done(((bf16[16,28,2,128]{3,2,1,0:T(2,128)(2,1)}), bf16[16,28,2,128]{3,2,1,0:T(2,128)(2,1)S(1)}, u32[]{:S(2)}, u32[]{:S(2)}) %all-to-all-start) | async-done | bytes 229408 | tf_op jit(solution)/shard_map/all_to_all | solution.py:368
  25.4 0.7 block_forward.1
  26.1 11.4 %all-to-all-start.1 = ((bf16[32,14,2,128]{3,2,1,0:T(2,128)(2,1)}), bf16[32,14,2,128]{3,2,1,0:T(2,128)(2,1)S(1)}, u32[]{:S(2)}, u32[]{:S(2)}) async-start(bf16[32,14,2,128]{3,2,1,0:T(2,128)(2,1)} %bitcast.4), calls=%async_computation.1 | async-start | bytes 458752 | tf_op jit(solution)/shard_map/all_to_all | solution.py:368
  37.5 0.0 copy-start.4
  37.6 2.1 %collective-permute-start.2 = (bf16[48,1152]{1,0:T(8,128)(2,1)S(1)}, bf16[48,1152]{1,0:T(8,128)(2,1)S(1)}, u32[]{:S(2)}, u32[]{:S(2)}) collective-permute-start(bf16[48,1152]{1,0:T(8,128)(2,1)S(1)} %get-tuple-element.27), channel_id=1, source_target_pairs={{0,4},{4,8},{8,12},{1,5},{5,9},{9,13},{2,6},{6,10},{10,14},{3,7},{... | collective-permute-start | bytes 331784 | tf_op jit(solution)/shard_map/ppermute | solution.py:373
  39.6 2.4 %collective-permute-start.3 = (bf16[48,1152]{1,0:T(8,128)(2,1)S(1)}, bf16[48,1152]{1,0:T(8,128)(2,1)S(1)}, u32[]{:S(2)}, u32[]{:S(2)}) collective-permute-start(bf16[48,1152]{1,0:T(8,128)(2,1)S(1)} %get-tuple-element.28), channel_id=1, source_target_pairs={{4,0},{8,4},{12,8},{5,1},{9,5},{13,9},{6,2},{10,6},{14,10},{7,3},{... | collective-permute-start | bytes 331784 | tf_op jit(solution)/shard_map/ppermute | solution.py:374
  42.1 0.9 conv.1.ga_ref
  43.0 3.0 %collective-permute-done.3.below_ref = bf16[48,1152]{1,0:T(8,128)(2,1)S(1)} collective-permute-done((bf16[48,1152]{1,0:T(8,128)(2,1)S(1)}, bf16[48,1152]{1,0:T(8,128)(2,1)S(1)}, u32[]{:S(2)}, u32[]{:S(2)}) %collective-permute-start.3) | collective-permute-done | bytes 110624 | tf_op jit(solution)/shard_map/ppermute | solution.py:374
  46.0 2.5 %all-to-all-done.1 = bf16[32,14,2,128]{3,2,1,0:T(2,128)(2,1)S(1)} async-done(((bf16[32,14,2,128]{3,2,1,0:T(2,128)(2,1)}), bf16[32,14,2,128]{3,2,1,0:T(2,128)(2,1)S(1)}, u32[]{:S(2)}, u32[]{:S(2)}) %all-to-all-start.1) | async-done | bytes 229408 | tf_op jit(solution)/shard_map/all_to_all | solution.py:368
  48.5 1.2 %states.1 = (f32[56,128]{1,0:T(8,128)S(1)}, f32[256,1152]{1,0:T(8,128)S(1)}, bf16[256,1152]{1,0:T(8,128)(2,1)S(1)}, bf16[1152,128]{1,0:T(8,128)(2,1)S(1)}, f32[9,32,128]{2,1,0:T(8,128)S(1)}) custom-call(bf16[896,128]{1,0:T(8,128)(2,1)S(1)} %bitcast.29, f32[56,128]{1,0:T(8,128)S(1)} %get-tuple-element.24.sums_ref, f32[56,128]{1,0:T(8,128)S(1)} %get-tuple-element.21.lanes_ref, ...), custom_call_target="tpu_custom_call" | custom-call | flops 150994944 | bytes 4559360 | tf_op jit(solution)/shard_map/states/pallas_call | solution.py:38
  49.7 16.9 %all_to_all.25 = bf16[16,36,2,128]{3,2,1,0:T(2,128)(2,1)S(1)} all-to-all(bf16[16,36,2,128]{3,2,1,0:T(2,128)(2,1)S(1)} %bitcast.33), channel_id=1, replica_groups=mesh['tm'=32,'row'=4,'col'=4] {'row','col'}, dimensions={0} | all-to-all | bytes 589824 | tf_op jit(solution)/shard_map/all_to_all | solution.py:368
  66.6 0.8 locals.1
  67.3 17.2 %all_to_all.26 = bf16[32,14,2,128]{3,2,1,0:T(2,128)(2,1)S(1)} all-to-all(bf16[32,14,2,128]{3,2,1,0:T(2,128)(2,1)S(1)} %bitcast.34), channel_id=1, replica_groups=mesh['tm'=32,'row'=4,'col'=4] {'tm'}, dimensions={0} | all-to-all | bytes 458752 | tf_op jit(solution)/shard_map/all_to_all | solution.py:368
  84.5 0.8 carried.1
  85.3 4.1 %all-to-all-start.4 = ((bf16[16,28,2,128]{3,2,1,0:T(2,128)(2,1)}), bf16[16,28,2,128]{3,2,1,0:T(2,128)(2,1)S(1)}, u32[]{:S(2)}, u32[]{:S(2)}) async-start(bf16[16,28,2,128]{3,2,1,0:T(2,128)(2,1)} %bitcast.13), calls=%async_computation.4 | async-start | bytes 458752 | tf_op jit(solution)/shard_map/all_to_all | solution.py:368
  89.5 1.6 %query.1 = bf16[256,1152]{1,0:T(8,128)(2,1)} custom-call(bf16[1152,128]{1,0:T(8,128)(2,1)S(1)} %bitcast.21, bf16[256,1152]{1,0:T(8,128)(2,1)S(1)} %bitcast.19, bf16[256,1152]{1,0:T(8,128)(2,1)S(1)} %get-tuple-element.30.num_ref, bf16[256,128]{1,0:T(8,128)(2,1)S(1)} %get-tuple-element.32.den_ref, f32[56,128]{1,0:T(8,128)S(1)} %get-tuple-element.33.own_ref), custom_call_target="tpu_custom_call" | custom-call | flops 75497472 | bytes 2158592 | tf_op jit(solution)/shard_map/query/pallas_call | solution.py:38
  91.1 9.3 %all-to-all-done.4 = bf16[16,28,2,128]{3,2,1,0:T(2,128)(2,1)S(1)} async-done(((bf16[16,28,2,128]{3,2,1,0:T(2,128)(2,1)}), bf16[16,28,2,128]{3,2,1,0:T(2,128)(2,1)S(1)}, u32[]{:S(2)}, u32[]{:S(2)}) %all-to-all-start.4) | async-done | bytes 229408 | tf_op jit(solution)/shard_map/all_to_all | solution.py:368
  100.4 1.5 %key.1 = (bf16[256,1152]{1,0:T(8,128)(2,1)}, bf16[256,1152]{1,0:T(8,128)(2,1)}) custom-call(bf16[256,1152]{1,0:T(8,128)(2,1)S(1)} %bitcast.26, bf16[256,1152]{1,0:T(8,128)(2,1)S(1)} %bitcast.28, bf16[896,128]{1,0:T(8,128)(2,1)S(1)} %bitcast.32), custom_call_target="tpu_custom_call" | custom-call | flops 150994944 | bytes 2588672 | tf_op jit(solution)/shard_map/key/pallas_call | solution.py:38
  (15 shorter events, 0.1 us)
Async XLA Ops:
  0.6 12.8 %copy-start.1 = (bf16[2,8,16,1152]{3,2,1,0:T(8,128)(2,1)S(1)}, bf16[2,8,16,1152]{3,2,1,0:T(8,128)(2,1)}, u32[]{:S(2)}) copy-start(bf16[2,8,16,1152]{3,2,1,0:T(8,128)(2,1)} %param.9) | copy-start | bytes 1769476
  0.6 18.4 %copy-start.5 = (f32[2,36]{1,0:T(2,128)S(1)}, f32[2,36]{1,0:T(2,128)}, u32[]{:S(2)}) copy-start(f32[2,36]{1,0:T(2,128)} %decay_ref.1) | copy-start | bytes 868
  3.2 22.2 %all-to-all-start = ((bf16[16,28,2,128]{3,2,1,0:T(2,128)(2,1)}), bf16[16,28,2,128]{3,2,1,0:T(2,128)(2,1)S(1)}, u32[]{:S(2)}, u32[]{:S(2)}) async-start(bf16[16,28,2,128]{3,2,1,0:T(2,128)(2,1)} %bitcast.35), calls=%async_computation | async-start | bytes 458752 | tf_op jit(solution)/shard_map/all_to_all | solution.py:368
  13.5 24.0 %collective-permute-start = (bf16[16,1152]{1,0:T(8,128)(2,1)S(1)}, bf16[16,1152]{1,0:T(8,128)(2,1)S(1)}, u32[]{:S(2)}, u32[]{:S(2)}) collective-permute-start(bf16[16,1152]{1,0:T(8,128)(2,1)S(1)} %get-tuple-element.25), channel_id=1, source_target_pairs={{0,1},{1,2},{2,3},{4,5},{5,6},{6,7},{8,9},{9,10},{10,11},{12,13},{... | collective-permute-start | bytes 110600 | tf_op jit(solution)/shard_map/ppermute | solution.py:373
  17.7 19.8 %collective-permute-start.1 = (bf16[16,1152]{1,0:T(8,128)(2,1)S(1)}, bf16[16,1152]{1,0:T(8,128)(2,1)S(1)}, u32[]{:S(2)}, u32[]{:S(2)}) collective-permute-start(bf16[16,1152]{1,0:T(8,128)(2,1)S(1)} %get-tuple-element.26), channel_id=1, source_target_pairs={{1,0},{2,1},{3,2},{5,4},{6,5},{7,6},{9,8},{10,9},{11,10},{13,12},{... | collective-permute-start | bytes 110600 | tf_op jit(solution)/shard_map/ppermute | solution.py:374
  26.1 22.4 %all-to-all-start.1 = ((bf16[32,14,2,128]{3,2,1,0:T(2,128)(2,1)}), bf16[32,14,2,128]{3,2,1,0:T(2,128)(2,1)S(1)}, u32[]{:S(2)}, u32[]{:S(2)}) async-start(bf16[32,14,2,128]{3,2,1,0:T(2,128)(2,1)} %bitcast.4), calls=%async_computation.1 | async-start | bytes 458752 | tf_op jit(solution)/shard_map/all_to_all | solution.py:368
  37.5 4.6 %copy-start.4 = (f32[9,1152]{1,0:T(8,128)S(1)}, f32[9,1152]{1,0:T(8,128)}, u32[]{:S(2)}) copy-start(f32[9,1152]{1,0:T(8,128)} %weight_ref.3) | copy-start | bytes 124420
  37.6 10.9 %copy-start = (bf16[2,8,16,1152]{3,2,1,0:T(8,128)(2,1)S(1)}, bf16[2,8,16,1152]{3,2,1,0:T(8,128)(2,1)}, u32[]{:S(2)}) copy-start(bf16[2,8,16,1152]{3,2,1,0:T(8,128)(2,1)} %param.6) | copy-start | bytes 1769476
  37.6 5.4 %collective-permute-start.2 = (bf16[48,1152]{1,0:T(8,128)(2,1)S(1)}, bf16[48,1152]{1,0:T(8,128)(2,1)S(1)}, u32[]{:S(2)}, u32[]{:S(2)}) collective-permute-start(bf16[48,1152]{1,0:T(8,128)(2,1)S(1)} %get-tuple-element.27), channel_id=1, source_target_pairs={{0,4},{4,8},{8,12},{1,5},{5,9},{9,13},{2,6},{6,10},{10,14},{3,7},{... | collective-permute-start | bytes 331784 | tf_op jit(solution)/shard_map/ppermute | solution.py:373
  39.6 6.4 %collective-permute-start.3 = (bf16[48,1152]{1,0:T(8,128)(2,1)S(1)}, bf16[48,1152]{1,0:T(8,128)(2,1)S(1)}, u32[]{:S(2)}, u32[]{:S(2)}) collective-permute-start(bf16[48,1152]{1,0:T(8,128)(2,1)S(1)} %get-tuple-element.28), channel_id=1, source_target_pairs={{4,0},{8,4},{12,8},{5,1},{9,5},{13,9},{6,2},{10,6},{14,10},{7,3},{... | collective-permute-start | bytes 331784 | tf_op jit(solution)/shard_map/ppermute | solution.py:374
  85.3 15.1 %all-to-all-start.4 = ((bf16[16,28,2,128]{3,2,1,0:T(2,128)(2,1)}), bf16[16,28,2,128]{3,2,1,0:T(2,128)(2,1)S(1)}, u32[]{:S(2)}, u32[]{:S(2)}) async-start(bf16[16,28,2,128]{3,2,1,0:T(2,128)(2,1)} %bitcast.13), calls=%async_computation.4 | async-start | bytes 458752 | tf_op jit(solution)/shard_map/all_to_all | solution.py:368
  89.5 10.9 %copy-start.2 = (bf16[2,8,16,1152]{3,2,1,0:T(8,128)(2,1)S(1)}, bf16[2,8,16,1152]{3,2,1,0:T(8,128)(2,1)}, u32[]{:S(2)}) copy-start(bf16[2,8,16,1152]{3,2,1,0:T(8,128)(2,1)} %param.7) | copy-start | bytes 1769476
  89.5 10.9 %copy-start.3 = (bf16[2,8,16,1152]{3,2,1,0:T(8,128)(2,1)S(1)}, bf16[2,8,16,1152]{3,2,1,0:T(8,128)(2,1)}, u32[]{:S(2)}) copy-start(bf16[2,8,16,1152]{3,2,1,0:T(8,128)(2,1)} %param.8) | copy-start | bytes 1769476

commit v4 on v3

--- a/solution.py
+++ b/solution.py
@@ -22,7 +22,7 @@
 SLOTS = EXTRA + 1
 OWNED = FRAMES * SLOTS
 BOTH = 2 * FRAMES * STATES
-PIECE = 64
+PIECE = 128
 PIECES = FRAMES * TOKENS // PIECE
 SPACE = ("row", "col")
 VMEM_BYTES = 16 * 1024 * 1024
@@ -190,9 +190,9 @@
     return taps[tap] * cells[0] + taps[tap + 1] * cells[1] + taps[tap + 2] * cells[2]
 
 
-def from_row(ref, taps, row_off, f, lanes):
-    corners = ref[FRAMES * COLS :, lanes].astype(F32)
-    x = ref[f * COLS : (f + 1) * COLS, lanes].astype(F32)
+def from_row(edge, taps, row_off, f):
+    corners = edge[FRAMES * COLS :]
+    x = edge[f * COLS : (f + 1) * COLS]
     return weighted(taps, row_off, around(x, corners[2 * f : 2 * f + 1], corners[2 * f + 1 : 2 * f + 2]))
 
 
@@ -202,8 +202,8 @@
     lanes_ref,
     q_ref,
     ga_ref,
-    above_ref,
-    below_ref,
+    pair_ref,
+    next_ref,
     weight_ref,
     own_ref,
     inverse_ref,
@@ -236,8 +236,9 @@
             lanes = slice(g * LANES, (g + 1) * LANES)
             taps = [weight_ref[t : t + 1, lanes] for t in range(9)]
             inner = part(ga_ref, f, g)
-            top = inner[:COLS] + from_row(above_ref, taps, 1, f, lanes)
-            bottom = inner[-COLS:] + from_row(below_ref, taps, -1, f, lanes)
+            above, below = swapped("row", pair_ref[:, lanes].astype(F32), next_ref[:, lanes].astype(F32))
+            top = inner[:COLS] + from_row(above, taps, 1, f)
+            bottom = inner[-COLS:] + from_row(below, taps, -1, f)
             grad_attn = jnp.concatenate([top, inner[COLS:-COLS], bottom], axis=0)
             grad_num = (grad_attn * inverse).astype(BF16)
             here = (slice(f * TOKENS, (f + 1) * TOKENS), slice(g * LANES, (g + 1) * LANES))
@@ -293,31 +294,40 @@
     copies(jnp.concatenate([first, second], axis=0), out_ref)
 
 
-def edge_cols_kernel(g_ref, first_ref, last_ref, first, last):
+def swapped(axis, first, second):
+    odd = lax.axis_index(axis) % 2 == 1
+    return jnp.where(odd, first, second), jnp.where(odd, second, first)
+
+
+def edge_cols_kernel(g_ref, inner_ref, outer_ref, first, last):
     for at in range(FRAMES * ROWS):
         x = g_ref[at * COLS : (at + 1) * COLS, :].astype(F32)
         first[at : at + 1, :] = x[:1]
         last[at : at + 1, :] = x[COLS - 1 :]
-    first_ref[...] = first[...].astype(BF16)
-    last_ref[...] = last[...].astype(BF16)
-
-
-def edge_rows_kernel(g_ref, left_ref, right_ref, first_ref, last_ref, corners):
-    left = left_ref[...].astype(F32)
-    right = right_ref[...].astype(F32)
-    for out_ref, row in ((first_ref, 0), (last_ref, ROWS - 1)):
+    inner, outer = swapped("col", first[...], last[...])
+    inner_ref[...] = inner.astype(BF16)
+    outer_ref[...] = outer.astype(BF16)
+
+
+def edge_rows_kernel(g_ref, pair_ref, next_ref, inner_ref, outer_ref, corners):
+    left, right = swapped("col", pair_ref[...].astype(F32), next_ref[...].astype(F32))
+    edges = []
+    for row in (0, ROWS - 1):
         corners[...] = jnp.zeros(corners.shape, F32)
+        cells = []
         for f in range(FRAMES):
             at = f * ROWS + row
-            out_ref[f * COLS : (f + 1) * COLS, :] = g_ref[at * COLS : (at + 1) * COLS, :]
+            cells.append(g_ref[at * COLS : (at + 1) * COLS, :].astype(F32))
             corners[2 * f : 2 * f + 1, :] = left[at : at + 1]
             corners[2 * f + 1 : 2 * f + 2, :] = right[at : at + 1]
-        out_ref[FRAMES * COLS :, :] = corners[...].astype(BF16)
-
-
-def conv_kernel(g_ref, left_ref, right_ref, weight_ref, out_ref):
-    left = left_ref[...].astype(F32)
-    right = right_ref[...].astype(F32)
+        edges.append(jnp.concatenate(cells + [corners[...]], axis=0))
+    inner, outer = swapped("row", *edges)
+    inner_ref[...] = inner.astype(BF16)
+    outer_ref[...] = outer.astype(BF16)
+
+
+def conv_kernel(g_ref, pair_ref, next_ref, weight_ref, out_ref):
+    left, right = swapped("col", pair_ref[...].astype(F32), next_ref[...].astype(F32))
     for f in range(FRAMES):
         for g in range(GROUPS):
             lanes = slice(g * LANES, (g + 1) * LANES)
@@ -368,11 +378,13 @@
     return lax.all_to_all(block, axes, 0, 0, tiled=True).reshape(count * rows, LANES)
 
 
-def neighbours(first, last, axis):
+def neighbours(inner, outer, axis):
     count = lax.axis_size(axis)
-    before = lax.ppermute(last, axis, [(i, i + 1) for i in range(count - 1)])
-    after = lax.ppermute(first, axis, [(i + 1, i) for i in range(count - 1)])
-    return before, after
+    pairs = [[(i, i + 1) for i in range(start, count - 1, 2)] for start in range(2)]
+    return tuple(
+        lax.ppermute(edge, axis, [way for a, b in pair for way in ((a, b), (b, a))])
+        for edge, pair in zip((inner, outer), pairs)
+    )
 
 
 def per_device(query_tokens, key_tokens, value_tokens, grad_output, frame_decay, conv_weight):
@@ -406,14 +418,16 @@
     side = ((FRAMES * ROWS, CH), BF16)
     edge = ((FRAMES * COLS + 16, CH), BF16)
     held_side = pltpu.VMEM(side[0], F32)
-    first, last = call(edge_cols_kernel, [side, side], g, scratch=[held_side, held_side], name="edge_cols")
-    left, right = neighbours(first, last, "col")
-    first, last = call(edge_rows_kernel, [edge, edge], g, left, right, scratch=[held_side], flops=20_000_000_000, name="edge_rows")
-    above, below = neighbours(first, last, "row")
+    inner, outer = call(edge_cols_kernel, [side, side], g, scratch=[held_side, held_side], name="edge_cols")
+    beside = neighbours(inner, outer, "col")
+    inner, outer = call(
+        edge_rows_kernel, [edge, edge], g, *beside, scratch=[held_side], flops=20_000_000_000, name="edge_rows"
+    )
+    across = neighbours(inner, outer, "row")
     sums, sent = call(block_forward_kernel, [owned, time], x, lanes, decay_row, name="block_forward")
     y = exchange(sent, "tm", blocks)
     (grad_attn,) = call(
-        conv_kernel, [(flat, F32)], g, left, right, conv_weight, flops=20 * flat[0] * flat[1], name="conv"
+        conv_kernel, [(flat, F32)], g, *beside, conv_weight, flops=20 * flat[0] * flat[1], name="conv"
     )
     own, inverse, grad_num, sent, weights = call(
         states_kernel,
@@ -423,8 +437,7 @@
         lanes,
         q,
         grad_attn,
-        above,
-        below,
+        *across,
         conv_weight,
         scratch=[held_time, carry, held_both],
         flops=2 * work,

time: 103 us -> 101 us (0.981)
  blocking collectives: 34.1 us -> 32.8 us
  waiting for transfers between devices: 20.9 us -> 22 us
    all_to_all x2, blocking collectives: 34.1 us -> 32.8 us  [exchange(): lax.all_to_all(block, axes, 0, 0, tiled=True).reshape(count * rows, LANES)]
where the time goes in v4:
time: 101 us
  starting transfers between devices  34.7 us (34%)
  blocking collectives  32.8 us (32%)
  waiting for transfers between devices  22 us (22%)
  Pallas kernels  10.3 us (10%)
    all_to_all x2, blocking collectives, exchange(): lax.all_to_all(block, axes, 0, 0, tiled=True).reshape(count * rows, LANES)  32.8 us
    all_to_all x3, starting transfers between devices, exchange(): lax.all_to_all(block, axes, 0, 0, tiled=True).reshape(count * rows, LANES)  25.7 us
    all_to_all x3, waiting for transfers between devices, exchange(): lax.all_to_all(block, axes, 0, 0, tiled=True).reshape(count * rows, LANES)  18.7 us
    pallas_call x11, Pallas kernels, call(): pl.pallas_call(body, out_shape=out_shape, in_specs=[near] * (len(args) -...  10.3 us
    ppermute x4, starting transfers between devices, neighbours(): lax.ppermute(edge, axis, [way for a, b in pair for way in ((a, b), (b, a))])  9.02 us
    ppermute x4, waiting for transfers between devices, neighbours(): lax.ppermute(edge, axis, [way for a, b in pair for way in ((a, b), (b, a))])  3.3 us
  transfers between devices with their start and end apart: 7, of which 4 were waited for; matrix products, arithmetic and copies ran while one was open for 0% of the time, Pallas kernels for 4%

profile of v4, /device:TPU:1, one launch (start us, length us, event | category | flops | bytes accessed | tf_op | source)
XLA Modules:
  0.0 100.7 jit_solution(14567719441445004079)
XLA Ops:
  0.7 2.4 %update.1 = bf16[896,128]{1,0:T(8,128)(2,1)} custom-call(bf16[256,1152]{1,0:T(8,128)(2,1)} %bitcast.25, bf16[256,1152]{1,0:T(8,128)(2,1)} %bitcast.27), custom_call_target="tpu_custom_call" | custom-call | flops 75497472 | bytes 1409024 | tf_op jit(solution)/shard_map/update/pallas_call | solution.py:38
  3.1 10.2 %all-to-all-start = ((bf16[16,28,2,128]{3,2,1,0:T(2,128)(2,1)}), bf16[16,28,2,128]{3,2,1,0:T(2,128)(2,1)S(1)}, u32[]{:S(2)}, u32[]{:S(2)}) async-start(bf16[16,28,2,128]{3,2,1,0:T(2,128)(2,1)} %bitcast.35), calls=%async_computation | async-start | bytes 458752 | tf_op jit(solution)/shard_map/all_to_all | solution.py:378
  13.3 0.1 edge_cols.1
  13.4 4.2 %collective-permute-start = (bf16[16,1152]{1,0:T(8,128)(2,1)S(1)}, bf16[16,1152]{1,0:T(8,128)(2,1)S(1)}, u32[]{:S(2)}, u32[]{:S(2)}) collective-permute-start(bf16[16,1152]{1,0:T(8,128)(2,1)S(1)} %get-tuple-element.25), channel_id=1, source_target_pairs={{0,1},{1,0},{2,3},{3,2},{4,5},{5,4},{6,7},{7,6},{8,9},{9,8},{10,11... | collective-permute-start | bytes 110600 | tf_op jit(solution)/shard_map/ppermute | solution.py:385
  17.6 0.7 collective-permute-start.1
  18.3 0.2 decay.1
  18.5 6.5 %all-to-all-done = bf16[16,28,2,128]{3,2,1,0:T(2,128)(2,1)S(1)} async-done(((bf16[16,28,2,128]{3,2,1,0:T(2,128)(2,1)}), bf16[16,28,2,128]{3,2,1,0:T(2,128)(2,1)S(1)}, u32[]{:S(2)}, u32[]{:S(2)}) %all-to-all-start) | async-done | bytes 229408 | tf_op jit(solution)/shard_map/all_to_all | solution.py:378
  25.0 0.7 block_forward.1
  25.7 11.3 %all-to-all-start.1 = ((bf16[32,14,2,128]{3,2,1,0:T(2,128)(2,1)}), bf16[32,14,2,128]{3,2,1,0:T(2,128)(2,1)S(1)}, u32[]{:S(2)}, u32[]{:S(2)}) async-start(bf16[32,14,2,128]{3,2,1,0:T(2,128)(2,1)} %bitcast.4), calls=%async_computation.1 | async-start | bytes 458752 | tf_op jit(solution)/shard_map/all_to_all | solution.py:378
  37.1 0.1 edge_rows.1
  37.2 2.1 %collective-permute-start.2 = (bf16[48,1152]{1,0:T(8,128)(2,1)S(1)}, bf16[48,1152]{1,0:T(8,128)(2,1)S(1)}, u32[]{:S(2)}, u32[]{:S(2)}) collective-permute-start(bf16[48,1152]{1,0:T(8,128)(2,1)S(1)} %get-tuple-element.27), channel_id=1, source_target_pairs={{0,4},{4,0},{8,12},{12,8},{1,5},{5,1},{9,13},{13,9},{2,6},{6,2},{1... | collective-permute-start | bytes 331784 | tf_op jit(solution)/shard_map/ppermute | solution.py:385
  39.3 2.1 %collective-permute-start.3 = (bf16[48,1152]{1,0:T(8,128)(2,1)S(1)}, bf16[48,1152]{1,0:T(8,128)(2,1)S(1)}, u32[]{:S(2)}, u32[]{:S(2)}) collective-permute-start(bf16[48,1152]{1,0:T(8,128)(2,1)S(1)} %get-tuple-element.28), channel_id=1, source_target_pairs={{4,8},{8,4},{5,9},{9,5},{6,10},{10,6},{7,11},{11,7},{20,24},{24,20... | collective-permute-start | bytes 331784 | tf_op jit(solution)/shard_map/ppermute | solution.py:385
  41.4 0.9 conv.1.ga_ref
  42.3 3.3 %collective-permute-done.3.next_ref = bf16[48,1152]{1,0:T(8,128)(2,1)S(1)} collective-permute-done((bf16[48,1152]{1,0:T(8,128)(2,1)S(1)}, bf16[48,1152]{1,0:T(8,128)(2,1)S(1)}, u32[]{:S(2)}, u32[]{:S(2)}) %collective-permute-start.3) | collective-permute-done | bytes 110624 | tf_op jit(solution)/shard_map/ppermute | solution.py:385
  45.6 2.8 %all-to-all-done.1 = bf16[32,14,2,128]{3,2,1,0:T(2,128)(2,1)S(1)} async-done(((bf16[32,14,2,128]{3,2,1,0:T(2,128)(2,1)}), bf16[32,14,2,128]{3,2,1,0:T(2,128)(2,1)S(1)}, u32[]{:S(2)}, u32[]{:S(2)}) %all-to-all-start.1) | async-done | bytes 229408 | tf_op jit(solution)/shard_map/all_to_all | solution.py:378
  48.5 1.2 %states.1 = (f32[56,128]{1,0:T(8,128)S(1)}, f32[256,1152]{1,0:T(8,128)S(1)}, bf16[256,1152]{1,0:T(8,128)(2,1)S(1)}, bf16[1152,128]{1,0:T(8,128)(2,1)S(1)}, f32[9,32,128]{2,1,0:T(8,128)S(1)}) custom-call(bf16[896,128]{1,0:T(8,128)(2,1)S(1)} %bitcast.29, f32[56,128]{1,0:T(8,128)S(1)} %get-tuple-element.24.sums_ref, f32[56,128]{1,0:T(8,128)S(1)} %get-tuple-element.21.lanes_ref, ...), custom_call_target="tpu_custom_call" | custom-call | flops 150994944 | bytes 4559360 | tf_op jit(solution)/shard_map/states/pallas_call | solution.py:38
  49.7 15.6 %all_to_all.25 = bf16[16,36,2,128]{3,2,1,0:T(2,128)(2,1)S(1)} all-to-all(bf16[16,36,2,128]{3,2,1,0:T(2,128)(2,1)S(1)} %bitcast.33), channel_id=1, replica_groups=mesh['tm'=32,'row'=4,'col'=4] {'row','col'}, dimensions={0} | all-to-all | bytes 589824 | tf_op jit(solution)/shard_map/all_to_all | solution.py:378
  65.3 0.8 locals.1
  66.1 17.3 %all_to_all.26 = bf16[32,14,2,128]{3,2,1,0:T(2,128)(2,1)S(1)} all-to-all(bf16[32,14,2,128]{3,2,1,0:T(2,128)(2,1)S(1)} %bitcast.34), channel_id=1, replica_groups=mesh['tm'=32,'row'=4,'col'=4] {'tm'}, dimensions={0} | all-to-all | bytes 458752 | tf_op jit(solution)/shard_map/all_to_all | solution.py:378
  83.3 0.8 carried.1
  84.1 4.1 %all-to-all-start.4 = ((bf16[16,28,2,128]{3,2,1,0:T(2,128)(2,1)}), bf16[16,28,2,128]{3,2,1,0:T(2,128)(2,1)S(1)}, u32[]{:S(2)}, u32[]{:S(2)}) async-start(bf16[16,28,2,128]{3,2,1,0:T(2,128)(2,1)} %bitcast.13), calls=%async_computation.4 | async-start | bytes 458752 | tf_op jit(solution)/shard_map/all_to_all | solution.py:378
  88.2 1.6 %query.1 = bf16[256,1152]{1,0:T(8,128)(2,1)} custom-call(bf16[1152,128]{1,0:T(8,128)(2,1)S(1)} %bitcast.21, bf16[256,1152]{1,0:T(8,128)(2,1)S(1)} %bitcast.19, bf16[256,1152]{1,0:T(8,128)(2,1)S(1)} %get-tuple-element.30.num_ref, bf16[256,128]{1,0:T(8,128)(2,1)S(1)} %get-tuple-element.32.den_ref, f32[56,128]{1,0:T(8,128)S(1)} %get-tuple-element.33.own_ref), custom_call_target="tpu_custom_call" | custom-call | flops 75497472 | bytes 2158592 | tf_op jit(solution)/shard_map/query/pallas_call | solution.py:38
  89.9 9.3 %all-to-all-done.4 = bf16[16,28,2,128]{3,2,1,0:T(2,128)(2,1)S(1)} async-done(((bf16[16,28,2,128]{3,2,1,0:T(2,128)(2,1)}), bf16[16,28,2,128]{3,2,1,0:T(2,128)(2,1)S(1)}, u32[]{:S(2)}, u32[]{:S(2)}) %all-to-all-start.4) | async-done | bytes 229408 | tf_op jit(solution)/shard_map/all_to_all | solution.py:378
  99.2 1.5 %key.1 = (bf16[256,1152]{1,0:T(8,128)(2,1)}, bf16[256,1152]{1,0:T(8,128)(2,1)}) custom-call(bf16[256,1152]{1,0:T(8,128)(2,1)S(1)} %bitcast.26, bf16[256,1152]{1,0:T(8,128)(2,1)S(1)} %bitcast.28, bf16[896,128]{1,0:T(8,128)(2,1)S(1)} %bitcast.32), custom_call_target="tpu_custom_call" | custom-call | flops 150994944 | bytes 2588672 | tf_op jit(solution)/shard_map/key/pallas_call | solution.py:38
  (15 shorter events, 0.0 us)
Async XLA Ops:
  0.6 12.7 %copy-start.1 = (bf16[2,8,16,1152]{3,2,1,0:T(8,128)(2,1)S(1)}, bf16[2,8,16,1152]{3,2,1,0:T(8,128)(2,1)}, u32[]{:S(2)}) copy-start(bf16[2,8,16,1152]{3,2,1,0:T(8,128)(2,1)} %param.9) | copy-start | bytes 1769476
  0.6 17.7 %copy-start.5 = (f32[2,36]{1,0:T(2,128)S(1)}, f32[2,36]{1,0:T(2,128)}, u32[]{:S(2)}) copy-start(f32[2,36]{1,0:T(2,128)} %decay_ref.1) | copy-start | bytes 868
  3.1 21.9 %all-to-all-start = ((bf16[16,28,2,128]{3,2,1,0:T(2,128)(2,1)}), bf16[16,28,2,128]{3,2,1,0:T(2,128)(2,1)S(1)}, u32[]{:S(2)}, u32[]{:S(2)}) async-start(bf16[16,28,2,128]{3,2,1,0:T(2,128)(2,1)} %bitcast.35), calls=%async_computation | async-start | bytes 458752 | tf_op jit(solution)/shard_map/all_to_all | solution.py:378
  13.4 23.6 %collective-permute-start = (bf16[16,1152]{1,0:T(8,128)(2,1)S(1)}, bf16[16,1152]{1,0:T(8,128)(2,1)S(1)}, u32[]{:S(2)}, u32[]{:S(2)}) collective-permute-start(bf16[16,1152]{1,0:T(8,128)(2,1)S(1)} %get-tuple-element.25), channel_id=1, source_target_pairs={{0,1},{1,0},{2,3},{3,2},{4,5},{5,4},{6,7},{7,6},{8,9},{9,8},{10,11... | collective-permute-start | bytes 110600 | tf_op jit(solution)/shard_map/ppermute | solution.py:385
  17.6 19.5 %collective-permute-start.1 = (bf16[16,1152]{1,0:T(8,128)(2,1)S(1)}, bf16[16,1152]{1,0:T(8,128)(2,1)S(1)}, u32[]{:S(2)}, u32[]{:S(2)}) collective-permute-start(bf16[16,1152]{1,0:T(8,128)(2,1)S(1)} %get-tuple-element.26), channel_id=1, source_target_pairs={{1,2},{2,1},{5,6},{6,5},{9,10},{10,9},{13,14},{14,13},{17,18},{18,... | collective-permute-start | bytes 110600 | tf_op jit(solution)/shard_map/ppermute | solution.py:385
  25.7 22.8 %all-to-all-start.1 = ((bf16[32,14,2,128]{3,2,1,0:T(2,128)(2,1)}), bf16[32,14,2,128]{3,2,1,0:T(2,128)(2,1)S(1)}, u32[]{:S(2)}, u32[]{:S(2)}) async-start(bf16[32,14,2,128]{3,2,1,0:T(2,128)(2,1)} %bitcast.4), calls=%async_computation.1 | async-start | bytes 458752 | tf_op jit(solution)/shard_map/all_to_all | solution.py:378
  37.1 4.3 %copy-start.4 = (f32[9,1152]{1,0:T(8,128)S(1)}, f32[9,1152]{1,0:T(8,128)}, u32[]{:S(2)}) copy-start(f32[9,1152]{1,0:T(8,128)} %weight_ref.3) | copy-start | bytes 124420
  37.2 11.3 %copy-start = (bf16[2,8,16,1152]{3,2,1,0:T(8,128)(2,1)S(1)}, bf16[2,8,16,1152]{3,2,1,0:T(8,128)(2,1)}, u32[]{:S(2)}) copy-start(bf16[2,8,16,1152]{3,2,1,0:T(8,128)(2,1)} %param.6) | copy-start | bytes 1769476
  37.2 5.1 %collective-permute-start.2 = (bf16[48,1152]{1,0:T(8,128)(2,1)S(1)}, bf16[48,1152]{1,0:T(8,128)(2,1)S(1)}, u32[]{:S(2)}, u32[]{:S(2)}) collective-permute-start(bf16[48,1152]{1,0:T(8,128)(2,1)S(1)} %get-tuple-element.27), channel_id=1, source_target_pairs={{0,4},{4,0},{8,12},{12,8},{1,5},{5,1},{9,13},{13,9},{2,6},{6,2},{1... | collective-permute-start | bytes 331784 | tf_op jit(solution)/shard_map/ppermute | solution.py:385
  39.3 6.4 %collective-permute-start.3 = (bf16[48,1152]{1,0:T(8,128)(2,1)S(1)}, bf16[48,1152]{1,0:T(8,128)(2,1)S(1)}, u32[]{:S(2)}, u32[]{:S(2)}) collective-permute-start(bf16[48,1152]{1,0:T(8,128)(2,1)S(1)} %get-tuple-element.28), channel_id=1, source_target_pairs={{4,8},{8,4},{5,9},{9,5},{6,10},{10,6},{7,11},{11,7},{20,24},{24,20... | collective-permute-start | bytes 331784 | tf_op jit(solution)/shard_map/ppermute | solution.py:385
  84.1 15.1 %all-to-all-start.4 = ((bf16[16,28,2,128]{3,2,1,0:T(2,128)(2,1)}), bf16[16,28,2,128]{3,2,1,0:T(2,128)(2,1)S(1)}, u32[]{:S(2)}, u32[]{:S(2)}) async-start(bf16[16,28,2,128]{3,2,1,0:T(2,128)(2,1)} %bitcast.13), calls=%async_computation.4 | async-start | bytes 458752 | tf_op jit(solution)/shard_map/all_to_all | solution.py:378
  88.2 10.9 %copy-start.2 = (bf16[2,8,16,1152]{3,2,1,0:T(8,128)(2,1)S(1)}, bf16[2,8,16,1152]{3,2,1,0:T(8,128)(2,1)}, u32[]{:S(2)}) copy-start(bf16[2,8,16,1152]{3,2,1,0:T(8,128)(2,1)} %param.7) | copy-start | bytes 1769476
  88.2 10.9 %copy-start.3 = (bf16[2,8,16,1152]{3,2,1,0:T(8,128)(2,1)S(1)}, bf16[2,8,16,1152]{3,2,1,0:T(8,128)(2,1)}, u32[]{:S(2)}) copy-start(bf16[2,8,16,1152]{3,2,1,0:T(8,128)(2,1)} %param.8) | copy-start | bytes 1769476

commit v5 on v4

--- a/solution.py
+++ b/solution.py
@@ -155,12 +155,13 @@
 
 
 def block_weights(held, index, count, backward):
-    mine = lax.axis_index("tm")
+    mine = count - 1 - lax.axis_index("tm")
     decays = held[pl.ds(EXTRA, count, stride=SLOTS), :].astype(BF16)
     source = iota((LANES, LANES), 0)
     onto = (source < 3 * HEADS) & (source % HEADS == index * PER_GROUP + lane_head((LANES, LANES)))
     block = dot(decays, onto.astype(BF16))
     at = iota((count, LANES), 0)
+    backward = not backward
     between = at > mine if backward else at < mine
     product = shifted(jnp.where(between, block, 1.0), 1 if backward else -1, count)
     step = 1
@@ -375,7 +376,8 @@
 def exchange(block, axes, count):
     rows = block.shape[0] // count
     block = block.reshape(count, rows // 2, 2, LANES)
-    return lax.all_to_all(block, axes, 0, 0, tiled=True).reshape(count * rows, LANES)
+    groups = [list(reversed(range(count)))]
+    return lax.all_to_all(block, axes, 0, 0, tiled=True, axis_index_groups=groups).reshape(count * rows, LANES)
 
 
 def neighbours(inner, outer, axis):

time: 101 us -> 94.4 us (0.935)
  waiting for transfers between devices: 22 us -> 11.9 us
  starting transfers between devices: 34.7 us -> 42.6 us
  blocking collectives: 32.8 us -> 28.1 us
    all_to_all x3, waiting for transfers between devices: 18.7 us -> 9.13 us  [exchange(): lax.all_to_all(block, axes, 0, 0, tiled=True, axis_index_groups=groups)]
    all_to_all x3, starting transfers between devices: 25.7 us -> 31.7 us  [exchange(): lax.all_to_all(block, axes, 0, 0, tiled=True, axis_index_groups=groups)]
    all_to_all x2, blocking collectives: 32.8 us -> 28.1 us  [exchange(): lax.all_to_all(block, axes, 0, 0, tiled=True, axis_index_groups=groups)]
    ppermute x4, starting transfers between devices: 9.02 us -> 11 us  [neighbours(): lax.ppermute(edge, axis, [way for a, b in pair for way in ((a, b), (b, a))])]
  transfers between devices with their start and end apart: 7 -> 7, of which waited for: 4 -> 3; matrix products, arithmetic and copies ran while one was open for 0% -> 0% of each run, Pallas kernels for 4% -> 4%
where the time goes in v5:
time: 94.4 us; the launch traced here: 93.8 us
  starting transfers between devices  42.6 us (45%)
  blocking collectives  28.1 us (30%)
  waiting for transfers between devices  11.9 us (13%)
  Pallas kernels  10.3 us (11%)
    all_to_all x3, starting transfers between devices, exchange(): lax.all_to_all(block, axes, 0, 0, tiled=True, axis_index_groups=groups)  31.7 us
    all_to_all x2, blocking collectives, exchange(): lax.all_to_all(block, axes, 0, 0, tiled=True, axis_index_groups=groups)  28.1 us
    ppermute x4, starting transfers between devices, neighbours(): lax.ppermute(edge, axis, [way for a, b in pair for way in ((a, b), (b, a))])  11 us
    pallas_call x11, Pallas kernels, call(): pl.pallas_call(body, out_shape=out_shape, in_specs=[near] * (len(args) -...  10.3 us
    all_to_all x3, waiting for transfers between devices, exchange(): lax.all_to_all(block, axes, 0, 0, tiled=True, axis_index_groups=groups)  9.13 us
    ppermute x4, waiting for transfers between devices, neighbours(): lax.ppermute(edge, axis, [way for a, b in pair for way in ((a, b), (b, a))])  2.76 us
  transfers between devices with their start and end apart: 7, of which 3 were waited for; matrix products, arithmetic and copies ran while one was open for 0% of the time, Pallas kernels for 4%

profile of v5, /device:TPU:1, one launch (start us, length us, event | category | flops | bytes accessed | tf_op | source)
XLA Modules:
  0.0 93.8 jit_solution(3630865601899006924)
XLA Ops:
  0.7 2.4 %update.1 = bf16[896,128]{1,0:T(8,128)(2,1)} custom-call(bf16[256,1152]{1,0:T(8,128)(2,1)} %bitcast.25, bf16[256,1152]{1,0:T(8,128)(2,1)} %bitcast.27), custom_call_target="tpu_custom_call" | custom-call | flops 75497472 | bytes 1409024 | tf_op jit(solution)/shard_map/update/pallas_call | solution.py:38
  3.1 10.7 %all-to-all-start = ((bf16[16,28,2,128]{3,2,1,0:T(2,128)(2,1)}), bf16[16,28,2,128]{3,2,1,0:T(2,128)(2,1)S(1)}, u32[]{:S(2)}, u32[]{:S(2)}) async-start(bf16[16,28,2,128]{3,2,1,0:T(2,128)(2,1)} %bitcast.35), calls=%async_computation | async-start | bytes 458752 | tf_op jit(solution)/shard_map/all_to_all | solution.py:380
  13.8 0.1 edge_cols.1
  14.0 4.0 %collective-permute-start = (bf16[16,1152]{1,0:T(8,128)(2,1)S(1)}, bf16[16,1152]{1,0:T(8,128)(2,1)S(1)}, u32[]{:S(2)}, u32[]{:S(2)}) collective-permute-start(bf16[16,1152]{1,0:T(8,128)(2,1)S(1)} %get-tuple-element.25), channel_id=1, source_target_pairs={{0,1},{1,0},{2,3},{3,2},{4,5},{5,4},{6,7},{7,6},{8,9},{9,8},{10,11... | collective-permute-start | bytes 110600 | tf_op jit(solution)/shard_map/ppermute | solution.py:387
  17.9 0.7 collective-permute-start.1
  18.6 0.2 decay.1
  18.8 3.0 %all-to-all-done = bf16[16,28,2,128]{3,2,1,0:T(2,128)(2,1)S(1)} async-done(((bf16[16,28,2,128]{3,2,1,0:T(2,128)(2,1)}), bf16[16,28,2,128]{3,2,1,0:T(2,128)(2,1)S(1)}, u32[]{:S(2)}, u32[]{:S(2)}) %all-to-all-start) | async-done | bytes 229408 | tf_op jit(solution)/shard_map/all_to_all | solution.py:380
  21.8 0.7 block_forward.1
  22.5 12.5 %all-to-all-start.1 = ((bf16[32,14,2,128]{3,2,1,0:T(2,128)(2,1)}), bf16[32,14,2,128]{3,2,1,0:T(2,128)(2,1)S(1)}, u32[]{:S(2)}, u32[]{:S(2)}) async-start(bf16[32,14,2,128]{3,2,1,0:T(2,128)(2,1)} %bitcast.4), calls=%async_computation.1 | async-start | bytes 458752 | tf_op jit(solution)/shard_map/all_to_all | solution.py:380
  35.0 0.1 edge_rows.1
  35.1 0.0 copy-start
  35.1 3.9 %collective-permute-start.2 = (bf16[48,1152]{1,0:T(8,128)(2,1)S(1)}, bf16[48,1152]{1,0:T(8,128)(2,1)S(1)}, u32[]{:S(2)}, u32[]{:S(2)}) collective-permute-start(bf16[48,1152]{1,0:T(8,128)(2,1)S(1)} %get-tuple-element.27), channel_id=1, source_target_pairs={{0,4},{4,0},{8,12},{12,8},{1,5},{5,1},{9,13},{13,9},{2,6},{6,2},{1... | collective-permute-start | bytes 331784 | tf_op jit(solution)/shard_map/ppermute | solution.py:387
  39.1 2.4 %collective-permute-start.3 = (bf16[48,1152]{1,0:T(8,128)(2,1)S(1)}, bf16[48,1152]{1,0:T(8,128)(2,1)S(1)}, u32[]{:S(2)}, u32[]{:S(2)}) collective-permute-start(bf16[48,1152]{1,0:T(8,128)(2,1)S(1)} %get-tuple-element.28), channel_id=1, source_target_pairs={{4,8},{8,4},{5,9},{9,5},{6,10},{10,6},{7,11},{11,7},{20,24},{24,20... | collective-permute-start | bytes 331784 | tf_op jit(solution)/shard_map/ppermute | solution.py:387
  41.5 0.9 conv.1.ga_ref
  42.4 2.8 %collective-permute-done.3.next_ref = bf16[48,1152]{1,0:T(8,128)(2,1)S(1)} collective-permute-done((bf16[48,1152]{1,0:T(8,128)(2,1)S(1)}, bf16[48,1152]{1,0:T(8,128)(2,1)S(1)}, u32[]{:S(2)}, u32[]{:S(2)}) %collective-permute-start.3) | collective-permute-done | bytes 110624 | tf_op jit(solution)/shard_map/ppermute | solution.py:387
  45.2 1.2 %states.1 = (f32[56,128]{1,0:T(8,128)S(1)}, f32[256,1152]{1,0:T(8,128)S(1)}, bf16[256,1152]{1,0:T(8,128)(2,1)S(1)}, bf16[1152,128]{1,0:T(8,128)(2,1)S(1)}, f32[9,32,128]{2,1,0:T(8,128)S(1)}) custom-call(bf16[896,128]{1,0:T(8,128)(2,1)S(1)} %bitcast.29, f32[56,128]{1,0:T(8,128)S(1)} %get-tuple-element.24.sums_ref, f32[56,128]{1,0:T(8,128)S(1)} %get-tuple-element.21.lanes_ref, ...), custom_call_target="tpu_custom_call" | custom-call | flops 150994944 | bytes 4559360 | tf_op jit(solution)/shard_map/states/pallas_call | solution.py:38
  46.4 13.3 %all_to_all.25 = bf16[16,36,2,128]{3,2,1,0:T(2,128)(2,1)S(1)} all-to-all(bf16[16,36,2,128]{3,2,1,0:T(2,128)(2,1)S(1)} %bitcast.33), channel_id=1, replica_groups={{15,14,13,12,11,10,9,8,7,6,5,4,3,2,1,0},{31,30,29,28,27,26,25,24,23,22,..., dimensions={0} | all-to-all | bytes 589824 | tf_op jit(solution)/shard_map/all_to_all | solution.py:380
  59.7 0.8 locals.1
  60.4 14.8 %all_to_all.26 = bf16[32,14,2,128]{3,2,1,0:T(2,128)(2,1)S(1)} all-to-all(bf16[32,14,2,128]{3,2,1,0:T(2,128)(2,1)S(1)} %bitcast.34), channel_id=1, replica_groups={{496,480,464,448,432,416,400,384,368,352,336,320,304,288,272,256,240,22..., dimensions={0} | all-to-all | bytes 458752 | tf_op jit(solution)/shard_map/all_to_all | solution.py:380
  75.3 0.8 carried.1
  76.1 8.5 %all-to-all-start.4 = ((bf16[16,28,2,128]{3,2,1,0:T(2,128)(2,1)}), bf16[16,28,2,128]{3,2,1,0:T(2,128)(2,1)S(1)}, u32[]{:S(2)}, u32[]{:S(2)}) async-start(bf16[16,28,2,128]{3,2,1,0:T(2,128)(2,1)} %bitcast.13), calls=%async_computation.4 | async-start | bytes 458752 | tf_op jit(solution)/shard_map/all_to_all | solution.py:380
  84.5 1.6 %query.1 = bf16[256,1152]{1,0:T(8,128)(2,1)} custom-call(bf16[1152,128]{1,0:T(8,128)(2,1)S(1)} %bitcast.21, bf16[256,1152]{1,0:T(8,128)(2,1)S(1)} %bitcast.19, bf16[256,1152]{1,0:T(8,128)(2,1)S(1)} %get-tuple-element.30.num_ref, bf16[256,128]{1,0:T(8,128)(2,1)S(1)} %get-tuple-element.32.den_ref, f32[56,128]{1,0:T(8,128)S(1)} %get-tuple-element.33.own_ref), custom_call_target="tpu_custom_call" | custom-call | flops 75497472 | bytes 2158592 | tf_op jit(solution)/shard_map/query/pallas_call | solution.py:38
  86.1 6.2 %all-to-all-done.4 = bf16[16,28,2,128]{3,2,1,0:T(2,128)(2,1)S(1)} async-done(((bf16[16,28,2,128]{3,2,1,0:T(2,128)(2,1)}), bf16[16,28,2,128]{3,2,1,0:T(2,128)(2,1)S(1)}, u32[]{:S(2)}, u32[]{:S(2)}) %all-to-all-start.4) | async-done | bytes 229408 | tf_op jit(solution)/shard_map/all_to_all | solution.py:380
  92.3 1.5 %key.1 = (bf16[256,1152]{1,0:T(8,128)(2,1)}, bf16[256,1152]{1,0:T(8,128)(2,1)}) custom-call(bf16[256,1152]{1,0:T(8,128)(2,1)S(1)} %bitcast.26, bf16[256,1152]{1,0:T(8,128)(2,1)S(1)} %bitcast.28, bf16[896,128]{1,0:T(8,128)(2,1)S(1)} %bitcast.32), custom_call_target="tpu_custom_call" | custom-call | flops 150994944 | bytes 2588672 | tf_op jit(solution)/shard_map/key/pallas_call | solution.py:38
  (15 shorter events, 0.0 us)
Async XLA Ops:
  0.6 13.2 %copy-start.1 = (bf16[2,8,16,1152]{3,2,1,0:T(8,128)(2,1)S(1)}, bf16[2,8,16,1152]{3,2,1,0:T(8,128)(2,1)}, u32[]{:S(2)}) copy-start(bf16[2,8,16,1152]{3,2,1,0:T(8,128)(2,1)} %param.9) | copy-start | bytes 1769476
  0.6 18.0 %copy-start.5 = (f32[2,36]{1,0:T(2,128)S(1)}, f32[2,36]{1,0:T(2,128)}, u32[]{:S(2)}) copy-start(f32[2,36]{1,0:T(2,128)} %decay_ref.1) | copy-start | bytes 868
  3.1 18.7 %all-to-all-start = ((bf16[16,28,2,128]{3,2,1,0:T(2,128)(2,1)}), bf16[16,28,2,128]{3,2,1,0:T(2,128)(2,1)S(1)}, u32[]{:S(2)}, u32[]{:S(2)}) async-start(bf16[16,28,2,128]{3,2,1,0:T(2,128)(2,1)} %bitcast.35), calls=%async_computation | async-start | bytes 458752 | tf_op jit(solution)/shard_map/all_to_all | solution.py:380
  14.0 21.0 %collective-permute-start = (bf16[16,1152]{1,0:T(8,128)(2,1)S(1)}, bf16[16,1152]{1,0:T(8,128)(2,1)S(1)}, u32[]{:S(2)}, u32[]{:S(2)}) collective-permute-start(bf16[16,1152]{1,0:T(8,128)(2,1)S(1)} %get-tuple-element.25), channel_id=1, source_target_pairs={{0,1},{1,0},{2,3},{3,2},{4,5},{5,4},{6,7},{7,6},{8,9},{9,8},{10,11... | collective-permute-start | bytes 110600 | tf_op jit(solution)/shard_map/ppermute | solution.py:387
  17.9 17.1 %collective-permute-start.1 = (bf16[16,1152]{1,0:T(8,128)(2,1)S(1)}, bf16[16,1152]{1,0:T(8,128)(2,1)S(1)}, u32[]{:S(2)}, u32[]{:S(2)}) collective-permute-start(bf16[16,1152]{1,0:T(8,128)(2,1)S(1)} %get-tuple-element.26), channel_id=1, source_target_pairs={{1,2},{2,1},{5,6},{6,5},{9,10},{10,9},{13,14},{14,13},{17,18},{18,... | collective-permute-start | bytes 110600 | tf_op jit(solution)/shard_map/ppermute | solution.py:387
  22.5 22.6 %all-to-all-start.1 = ((bf16[32,14,2,128]{3,2,1,0:T(2,128)(2,1)}), bf16[32,14,2,128]{3,2,1,0:T(2,128)(2,1)S(1)}, u32[]{:S(2)}, u32[]{:S(2)}) async-start(bf16[32,14,2,128]{3,2,1,0:T(2,128)(2,1)} %bitcast.4), calls=%async_computation.1 | async-start | bytes 458752 | tf_op jit(solution)/shard_map/all_to_all | solution.py:380
  35.0 6.5 %copy-start.4 = (f32[9,1152]{1,0:T(8,128)S(1)}, f32[9,1152]{1,0:T(8,128)}, u32[]{:S(2)}) copy-start(f32[9,1152]{1,0:T(8,128)} %weight_ref.3) | copy-start | bytes 124420
  35.1 10.0 %copy-start = (bf16[2,8,16,1152]{3,2,1,0:T(8,128)(2,1)S(1)}, bf16[2,8,16,1152]{3,2,1,0:T(8,128)(2,1)}, u32[]{:S(2)}) copy-start(bf16[2,8,16,1152]{3,2,1,0:T(8,128)(2,1)} %param.6) | copy-start | bytes 1769476
  35.1 7.3 %collective-permute-start.2 = (bf16[48,1152]{1,0:T(8,128)(2,1)S(1)}, bf16[48,1152]{1,0:T(8,128)(2,1)S(1)}, u32[]{:S(2)}, u32[]{:S(2)}) collective-permute-start(bf16[48,1152]{1,0:T(8,128)(2,1)S(1)} %get-tuple-element.27), channel_id=1, source_target_pairs={{0,4},{4,0},{8,12},{12,8},{1,5},{5,1},{9,13},{13,9},{2,6},{6,2},{1... | collective-permute-start | bytes 331784 | tf_op jit(solution)/shard_map/ppermute | solution.py:387
  39.1 6.1 %collective-permute-start.3 = (bf16[48,1152]{1,0:T(8,128)(2,1)S(1)}, bf16[48,1152]{1,0:T(8,128)(2,1)S(1)}, u32[]{:S(2)}, u32[]{:S(2)}) collective-permute-start(bf16[48,1152]{1,0:T(8,128)(2,1)S(1)} %get-tuple-element.28), channel_id=1, source_target_pairs={{4,8},{8,4},{5,9},{9,5},{6,10},{10,6},{7,11},{11,7},{20,24},{24,20... | collective-permute-start | bytes 331784 | tf_op jit(solution)/shard_map/ppermute | solution.py:387
  76.1 16.2 %all-to-all-start.4 = ((bf16[16,28,2,128]{3,2,1,0:T(2,128)(2,1)}), bf16[16,28,2,128]{3,2,1,0:T(2,128)(2,1)S(1)}, u32[]{:S(2)}, u32[]{:S(2)}) async-start(bf16[16,28,2,128]{3,2,1,0:T(2,128)(2,1)} %bitcast.13), calls=%async_computation.4 | async-start | bytes 458752 | tf_op jit(solution)/shard_map/all_to_all | solution.py:380
  84.5 7.8 %copy-start.2 = (bf16[2,8,16,1152]{3,2,1,0:T(8,128)(2,1)S(1)}, bf16[2,8,16,1152]{3,2,1,0:T(8,128)(2,1)}, u32[]{:S(2)}) copy-start(bf16[2,8,16,1152]{3,2,1,0:T(8,128)(2,1)} %param.7) | copy-start | bytes 1769476
  84.5 7.8 %copy-start.3 = (bf16[2,8,16,1152]{3,2,1,0:T(8,128)(2,1)S(1)}, bf16[2,8,16,1152]{3,2,1,0:T(8,128)(2,1)}, u32[]{:S(2)}) copy-start(bf16[2,8,16,1152]{3,2,1,0:T(8,128)(2,1)} %param.8) | copy-start | bytes 1769476

commit v6 on v5

--- a/solution.py
+++ b/solution.py
@@ -203,8 +203,8 @@
     lanes_ref,
     q_ref,
     ga_ref,
+    next_ref,
     pair_ref,
-    next_ref,
     weight_ref,
     own_ref,
     inverse_ref,
@@ -310,7 +310,7 @@
     outer_ref[...] = outer.astype(BF16)
 
 
-def edge_rows_kernel(g_ref, pair_ref, next_ref, inner_ref, outer_ref, corners):
+def edge_rows_kernel(g_ref, pair_ref, next_ref, outer_ref, inner_ref, corners):
     left, right = swapped("col", pair_ref[...].astype(F32), next_ref[...].astype(F32))
     edges = []
     for row in (0, ROWS - 1):
@@ -383,10 +383,11 @@
 def neighbours(inner, outer, axis):
     count = lax.axis_size(axis)
     pairs = [[(i, i + 1) for i in range(start, count - 1, 2)] for start in range(2)]
-    return tuple(
+    far, near = (
         lax.ppermute(edge, axis, [way for a, b in pair for way in ((a, b), (b, a))])
-        for edge, pair in zip((inner, outer), pairs)
-    )
+        for edge, pair in zip((outer, inner), reversed(pairs))
+    )
+    return near, far
 
 
 def per_device(query_tokens, key_tokens, value_tokens, grad_output, frame_decay, conv_weight):
@@ -422,7 +423,7 @@
     held_side = pltpu.VMEM(side[0], F32)
     inner, outer = call(edge_cols_kernel, [side, side], g, scratch=[held_side, held_side], name="edge_cols")
     beside = neighbours(inner, outer, "col")
-    inner, outer = call(
+    outer, inner = call(
         edge_rows_kernel, [edge, edge], g, *beside, scratch=[held_side], flops=20_000_000_000, name="edge_rows"
     )
     across = neighbours(inner, outer, "row")
@@ -439,7 +440,7 @@
         lanes,
         q,
         grad_attn,
-        *across,
+        *reversed(across),
         conv_weight,
         scratch=[held_time, carry, held_both],
         flops=2 * work,

time: 94.4 us -> 93.2 us (0.987)
  waiting for transfers between devices: 11.9 us -> 9.49 us
  blocking collectives: 28.1 us -> 29.3 us
    ppermute x4, waiting for transfers between devices: 2.76 us -> 0.35 us  [neighbours(): lax.ppermute(edge, axis, [way for a, b in pair for way in ((a, b), (b, a))])]
    all_to_all x2, blocking collectives: 28.1 us -> 29.3 us  [exchange(): lax.all_to_all(block, axes, 0, 0, tiled=True, axis_index_groups=groups)]
where the time goes in v6:
time: 93.2 us; the launch traced here: 92.6 us
  starting transfers between devices  42.6 us (46%)
  blocking collectives  29.3 us (31%)
  Pallas kernels  10.3 us (11%)
  waiting for transfers between devices  9.49 us (10%)
    all_to_all x3, starting transfers between devices, exchange(): lax.all_to_all(block, axes, 0, 0, tiled=True, axis_index_groups=groups)  31.7 us
    all_to_all x2, blocking collectives, exchange(): lax.all_to_all(block, axes, 0, 0, tiled=True, axis_index_groups=groups)  29.3 us
    ppermute x4, starting transfers between devices, neighbours(): lax.ppermute(edge, axis, [way for a, b in pair for way in ((a, b), (b, a))])  11 us
    pallas_call x11, Pallas kernels, call(): pl.pallas_call(body, out_shape=out_shape, in_specs=[near] * (len(args) -...  10.3 us
    all_to_all x3, waiting for transfers between devices, exchange(): lax.all_to_all(block, axes, 0, 0, tiled=True, axis_index_groups=groups)  9.13 us
  transfers between devices with their start and end apart: 7, of which 3 were waited for; matrix products, arithmetic and copies ran while one was open for 0% of the time, Pallas kernels for 4%

profile of v6, /device:TPU:1, one launch (start us, length us, event | category | flops | bytes accessed | tf_op | source)
XLA Modules:
  0.0 92.6 jit_solution(13731759360999384802)
XLA Ops:
  0.7 2.4 %update.1 = bf16[896,128]{1,0:T(8,128)(2,1)} custom-call(bf16[256,1152]{1,0:T(8,128)(2,1)} %bitcast.25, bf16[256,1152]{1,0:T(8,128)(2,1)} %bitcast.27), custom_call_target="tpu_custom_call" | custom-call | flops 75497472 | bytes 1409024 | tf_op jit(solution)/shard_map/update/pallas_call | solution.py:38
  3.1 10.7 %all-to-all-start = ((bf16[16,28,2,128]{3,2,1,0:T(2,128)(2,1)}), bf16[16,28,2,128]{3,2,1,0:T(2,128)(2,1)S(1)}, u32[]{:S(2)}, u32[]{:S(2)}) async-start(bf16[16,28,2,128]{3,2,1,0:T(2,128)(2,1)} %bitcast.35), calls=%async_computation | async-start | bytes 458752 | tf_op jit(solution)/shard_map/all_to_all | solution.py:380
  13.8 0.1 edge_cols.1
  14.0 4.0 %collective-permute-start = (bf16[16,1152]{1,0:T(8,128)(2,1)S(1)}, bf16[16,1152]{1,0:T(8,128)(2,1)S(1)}, u32[]{:S(2)}, u32[]{:S(2)}) collective-permute-start(bf16[16,1152]{1,0:T(8,128)(2,1)S(1)} %get-tuple-element.25), channel_id=1, source_target_pairs={{0,1},{1,0},{2,3},{3,2},{4,5},{5,4},{6,7},{7,6},{8,9},{9,8},{10,11... | collective-permute-start | bytes 110600 | tf_op jit(solution)/shard_map/ppermute | solution.py:387
  17.9 0.7 collective-permute-start.1
  18.6 0.2 decay.1
  18.8 3.0 %all-to-all-done = bf16[16,28,2,128]{3,2,1,0:T(2,128)(2,1)S(1)} async-done(((bf16[16,28,2,128]{3,2,1,0:T(2,128)(2,1)}), bf16[16,28,2,128]{3,2,1,0:T(2,128)(2,1)S(1)}, u32[]{:S(2)}, u32[]{:S(2)}) %all-to-all-start) | async-done | bytes 229408 | tf_op jit(solution)/shard_map/all_to_all | solution.py:380
  21.8 0.7 block_forward.1
  22.5 12.5 %all-to-all-start.1 = ((bf16[32,14,2,128]{3,2,1,0:T(2,128)(2,1)}), bf16[32,14,2,128]{3,2,1,0:T(2,128)(2,1)S(1)}, u32[]{:S(2)}, u32[]{:S(2)}) async-start(bf16[32,14,2,128]{3,2,1,0:T(2,128)(2,1)} %bitcast.4), calls=%async_computation.1 | async-start | bytes 458752 | tf_op jit(solution)/shard_map/all_to_all | solution.py:380
  35.0 0.0 copy-start.4
  35.0 0.1 edge_rows.1
  35.1 4.4 %collective-permute-start.2 = (bf16[48,1152]{1,0:T(8,128)(2,1)S(1)}, bf16[48,1152]{1,0:T(8,128)(2,1)S(1)}, u32[]{:S(2)}, u32[]{:S(2)}) collective-permute-start(bf16[48,1152]{1,0:T(8,128)(2,1)S(1)} %get-tuple-element.27), channel_id=1, source_target_pairs={{4,8},{8,4},{5,9},{9,5},{6,10},{10,6},{7,11},{11,7},{20,24},{24,20... | collective-permute-start | bytes 331784 | tf_op jit(solution)/shard_map/ppermute | solution.py:387
  39.5 1.9 %collective-permute-start.3 = (bf16[48,1152]{1,0:T(8,128)(2,1)S(1)}, bf16[48,1152]{1,0:T(8,128)(2,1)S(1)}, u32[]{:S(2)}, u32[]{:S(2)}) collective-permute-start(bf16[48,1152]{1,0:T(8,128)(2,1)S(1)} %get-tuple-element.28), channel_id=1, source_target_pairs={{0,4},{4,0},{8,12},{12,8},{1,5},{5,1},{9,13},{13,9},{2,6},{6,2},{1... | collective-permute-start | bytes 331784 | tf_op jit(solution)/shard_map/ppermute | solution.py:387
  41.5 0.9 conv.1.ga_ref
  42.4 0.3 collective-permute-done.3.pair_ref
  42.7 1.2 %states.1 = (f32[56,128]{1,0:T(8,128)S(1)}, f32[256,1152]{1,0:T(8,128)S(1)}, bf16[256,1152]{1,0:T(8,128)(2,1)S(1)}, bf16[1152,128]{1,0:T(8,128)(2,1)S(1)}, f32[9,32,128]{2,1,0:T(8,128)S(1)}) custom-call(bf16[896,128]{1,0:T(8,128)(2,1)S(1)} %bitcast.29, f32[56,128]{1,0:T(8,128)S(1)} %get-tuple-element.24.sums_ref, f32[56,128]{1,0:T(8,128)S(1)} %get-tuple-element.21.lanes_ref, ...), custom_call_target="tpu_custom_call" | custom-call | flops 150994944 | bytes 4559360 | tf_op jit(solution)/shard_map/states/pallas_call | solution.py:38
  44.0 15.7 %all_to_all.25 = bf16[16,36,2,128]{3,2,1,0:T(2,128)(2,1)S(1)} all-to-all(bf16[16,36,2,128]{3,2,1,0:T(2,128)(2,1)S(1)} %bitcast.33), channel_id=1, replica_groups={{15,14,13,12,11,10,9,8,7,6,5,4,3,2,1,0},{31,30,29,28,27,26,25,24,23,22,..., dimensions={0} | all-to-all | bytes 589824 | tf_op jit(solution)/shard_map/all_to_all | solution.py:380
  59.7 0.8 locals.1
  60.4 13.6 %all_to_all.26 = bf16[32,14,2,128]{3,2,1,0:T(2,128)(2,1)S(1)} all-to-all(bf16[32,14,2,128]{3,2,1,0:T(2,128)(2,1)S(1)} %bitcast.34), channel_id=1, replica_groups={{496,480,464,448,432,416,400,384,368,352,336,320,304,288,272,256,240,22..., dimensions={0} | all-to-all | bytes 458752 | tf_op jit(solution)/shard_map/all_to_all | solution.py:380
  74.0 0.8 carried.1
  74.8 8.5 %all-to-all-start.4 = ((bf16[16,28,2,128]{3,2,1,0:T(2,128)(2,1)}), bf16[16,28,2,128]{3,2,1,0:T(2,128)(2,1)S(1)}, u32[]{:S(2)}, u32[]{:S(2)}) async-start(bf16[16,28,2,128]{3,2,1,0:T(2,128)(2,1)} %bitcast.13), calls=%async_computation.4 | async-start | bytes 458752 | tf_op jit(solution)/shard_map/all_to_all | solution.py:380
  83.3 1.6 %query.1 = bf16[256,1152]{1,0:T(8,128)(2,1)} custom-call(bf16[1152,128]{1,0:T(8,128)(2,1)S(1)} %bitcast.21, bf16[256,1152]{1,0:T(8,128)(2,1)S(1)} %bitcast.19, bf16[256,1152]{1,0:T(8,128)(2,1)S(1)} %get-tuple-element.30.num_ref, bf16[256,128]{1,0:T(8,128)(2,1)S(1)} %get-tuple-element.32.den_ref, f32[56,128]{1,0:T(8,128)S(1)} %get-tuple-element.33.own_ref), custom_call_target="tpu_custom_call" | custom-call | flops 75497472 | bytes 2158592 | tf_op jit(solution)/shard_map/query/pallas_call | solution.py:38
  84.9 6.2 %all-to-all-done.4 = bf16[16,28,2,128]{3,2,1,0:T(2,128)(2,1)S(1)} async-done(((bf16[16,28,2,128]{3,2,1,0:T(2,128)(2,1)}), bf16[16,28,2,128]{3,2,1,0:T(2,128)(2,1)S(1)}, u32[]{:S(2)}, u32[]{:S(2)}) %all-to-all-start.4) | async-done | bytes 229408 | tf_op jit(solution)/shard_map/all_to_all | solution.py:380
  91.1 1.5 %key.1 = (bf16[256,1152]{1,0:T(8,128)(2,1)}, bf16[256,1152]{1,0:T(8,128)(2,1)}) custom-call(bf16[256,1152]{1,0:T(8,128)(2,1)S(1)} %bitcast.26, bf16[256,1152]{1,0:T(8,128)(2,1)S(1)} %bitcast.28, bf16[896,128]{1,0:T(8,128)(2,1)S(1)} %bitcast.32), custom_call_target="tpu_custom_call" | custom-call | flops 150994944 | bytes 2588672 | tf_op jit(solution)/shard_map/key/pallas_call | solution.py:38
  (15 shorter events, 0.0 us)
Async XLA Ops:
  0.6 13.2 %copy-start.1 = (bf16[2,8,16,1152]{3,2,1,0:T(8,128)(2,1)S(1)}, bf16[2,8,16,1152]{3,2,1,0:T(8,128)(2,1)}, u32[]{:S(2)}) copy-start(bf16[2,8,16,1152]{3,2,1,0:T(8,128)(2,1)} %param.9) | copy-start | bytes 1769476
  0.6 18.0 %copy-start.5 = (f32[2,36]{1,0:T(2,128)S(1)}, f32[2,36]{1,0:T(2,128)}, u32[]{:S(2)}) copy-start(f32[2,36]{1,0:T(2,128)} %decay_ref.1) | copy-start | bytes 868
  3.1 18.7 %all-to-all-start = ((bf16[16,28,2,128]{3,2,1,0:T(2,128)(2,1)}), bf16[16,28,2,128]{3,2,1,0:T(2,128)(2,1)S(1)}, u32[]{:S(2)}, u32[]{:S(2)}) async-start(bf16[16,28,2,128]{3,2,1,0:T(2,128)(2,1)} %bitcast.35), calls=%async_computation | async-start | bytes 458752 | tf_op jit(solution)/shard_map/all_to_all | solution.py:380
  14.0 21.0 %collective-permute-start = (bf16[16,1152]{1,0:T(8,128)(2,1)S(1)}, bf16[16,1152]{1,0:T(8,128)(2,1)S(1)}, u32[]{:S(2)}, u32[]{:S(2)}) collective-permute-start(bf16[16,1152]{1,0:T(8,128)(2,1)S(1)} %get-tuple-element.25), channel_id=1, source_target_pairs={{0,1},{1,0},{2,3},{3,2},{4,5},{5,4},{6,7},{7,6},{8,9},{9,8},{10,11... | collective-permute-start | bytes 110600 | tf_op jit(solution)/shard_map/ppermute | solution.py:387
  17.9 17.1 %collective-permute-start.1 = (bf16[16,1152]{1,0:T(8,128)(2,1)S(1)}, bf16[16,1152]{1,0:T(8,128)(2,1)S(1)}, u32[]{:S(2)}, u32[]{:S(2)}) collective-permute-start(bf16[16,1152]{1,0:T(8,128)(2,1)S(1)} %get-tuple-element.26), channel_id=1, source_target_pairs={{1,2},{2,1},{5,6},{6,5},{9,10},{10,9},{13,14},{14,13},{17,18},{18,... | collective-permute-start | bytes 110600 | tf_op jit(solution)/shard_map/ppermute | solution.py:387
  22.5 20.2 %all-to-all-start.1 = ((bf16[32,14,2,128]{3,2,1,0:T(2,128)(2,1)}), bf16[32,14,2,128]{3,2,1,0:T(2,128)(2,1)S(1)}, u32[]{:S(2)}, u32[]{:S(2)}) async-start(bf16[32,14,2,128]{3,2,1,0:T(2,128)(2,1)} %bitcast.4), calls=%async_computation.1 | async-start | bytes 458752 | tf_op jit(solution)/shard_map/all_to_all | solution.py:380
  35.0 6.5 %copy-start.4 = (f32[9,1152]{1,0:T(8,128)S(1)}, f32[9,1152]{1,0:T(8,128)}, u32[]{:S(2)}) copy-start(f32[9,1152]{1,0:T(8,128)} %weight_ref.3) | copy-start | bytes 124420
  35.1 7.6 %copy-start = (bf16[2,8,16,1152]{3,2,1,0:T(8,128)(2,1)S(1)}, bf16[2,8,16,1152]{3,2,1,0:T(8,128)(2,1)}, u32[]{:S(2)}) copy-start(bf16[2,8,16,1152]{3,2,1,0:T(8,128)(2,1)} %param.6) | copy-start | bytes 1769476
  35.1 7.3 %collective-permute-start.2 = (bf16[48,1152]{1,0:T(8,128)(2,1)S(1)}, bf16[48,1152]{1,0:T(8,128)(2,1)S(1)}, u32[]{:S(2)}, u32[]{:S(2)}) collective-permute-start(bf16[48,1152]{1,0:T(8,128)(2,1)S(1)} %get-tuple-element.27), channel_id=1, source_target_pairs={{4,8},{8,4},{5,9},{9,5},{6,10},{10,6},{7,11},{11,7},{20,24},{24,20... | collective-permute-start | bytes 331784 | tf_op jit(solution)/shard_map/ppermute | solution.py:387
  39.5 3.2 %collective-permute-start.3 = (bf16[48,1152]{1,0:T(8,128)(2,1)S(1)}, bf16[48,1152]{1,0:T(8,128)(2,1)S(1)}, u32[]{:S(2)}, u32[]{:S(2)}) collective-permute-start(bf16[48,1152]{1,0:T(8,128)(2,1)S(1)} %get-tuple-element.28), channel_id=1, source_target_pairs={{0,4},{4,0},{8,12},{12,8},{1,5},{5,1},{9,13},{13,9},{2,6},{6,2},{1... | collective-permute-start | bytes 331784 | tf_op jit(solution)/shard_map/ppermute | solution.py:387
  74.8 16.2 %all-to-all-start.4 = ((bf16[16,28,2,128]{3,2,1,0:T(2,128)(2,1)}), bf16[16,28,2,128]{3,2,1,0:T(2,128)(2,1)S(1)}, u32[]{:S(2)}, u32[]{:S(2)}) async-start(bf16[16,28,2,128]{3,2,1,0:T(2,128)(2,1)} %bitcast.13), calls=%async_computation.4 | async-start | bytes 458752 | tf_op jit(solution)/shard_map/all_to_all | solution.py:380
  83.3 7.8 %copy-start.2 = (bf16[2,8,16,1152]{3,2,1,0:T(8,128)(2,1)S(1)}, bf16[2,8,16,1152]{3,2,1,0:T(8,128)(2,1)}, u32[]{:S(2)}) copy-start(bf16[2,8,16,1152]{3,2,1,0:T(8,128)(2,1)} %param.7) | copy-start | bytes 1769476
  83.3 7.8 %copy-start.3 = (bf16[2,8,16,1152]{3,2,1,0:T(8,128)(2,1)S(1)}, bf16[2,8,16,1152]{3,2,1,0:T(8,128)(2,1)}, u32[]{:S(2)}) copy-start(bf16[2,8,16,1152]{3,2,1,0:T(8,128)(2,1)} %param.8) | copy-start | bytes 1769476
